TPU v7x, 32 devices: a whole 2x2x4 slice. The times are simulated.
32 devices in a mesh: dp: 8 (over y, x, core), tensor: 4 (over z).
Axes of the slice: x: 2, y: 2, z: 4, core: 2. Of those that a mesh axis runs over, the one named last changes fastest.
Arguments:
- x_rows: bfloat16 [64, 128, 3072], P('dp', 'tensor'), may hold values from -6 to 6
- g_rows: bfloat16 [64, 128, 3072], P('dp', 'tensor'), may hold values from -1.5 to 1.5
- w_up: bfloat16 [3072, 12288], P(None, 'tensor'), may hold values from -0.109375 to 0.109375
- w_down_t: bfloat16 [3072, 12288], P(None, 'tensor'), may hold values from -0.0546875 to 0.0546875
- block_count: int32 [8], replicated, may hold values from 1 to 8, 32 in all
- patches: int32 [8, 8], replicated, may hold values from 64 to 128, as said below
Outputs:
- input_grad: bfloat16 [32, 128, 3072], P('dp', 'tensor')
- up_grad: bfloat16 [3072, 12288], P('dp', 'tensor')
- down_grad_t: bfloat16 [3072, 12288], P('dp', 'tensor')
Inputs may be any that keep to these rules, and one draw needn't show every extreme that they name: `block_count`: the counts sum to 32; the largest is exactly 8. `patches`: in each source at least one block is full.
All inputs are finite; a program needn't handle non-finite values.
Results may differ from a plain program's by a relative error of at most 0.023.
Values may be sent and summed in bfloat16 or wider, within the bound.
No kernel may reach another device: no remote copies, remote signals or barrier semaphores. Data moves between devices by JAX's collectives and lax.ppermute only.
A program may use at most 192 MiB of HBM per device.

v0:
```python
import functools

import jax
import jax.numpy as jnp
from jax import lax
from jax.experimental import pallas as pl
from jax.experimental.pallas import tpu as pltpu
from jax.sharding import PartitionSpec as P

OWNB = 4
BF16 = jnp.bfloat16
F32 = jnp.float32
VMEM_LIMIT = 64 * 1024 * 1024
SHORT = pl.CostEstimate(flops=1, bytes_accessed=1, transcendentals=0)


def chip_with(j, v, core):
    return jnp.where(core == 0, 2 * j + v, ((j >> 1) << 2) + 2 * v + (j & 1))


def pool_bit(chip, core):
    return jnp.where(core == 0, chip & 1, (chip >> 1) & 1)


def other_bits(chip, core):
    return jnp.where(core == 0, chip >> 1, ((chip >> 2) << 1) + (chip & 1))


def chip_perm(dp, flip, cross=False):
    return [(i, 2 * ((i >> 1) ^ flip(i & 1)) + ((i & 1) ^ int(cross))) for i in range(dp)]


def start_of(count, source, dp):
    total = jnp.int32(0)
    for j in range(dp):
        total = total + jnp.where(source > j, count[j], 0)
    return total


def source_of(count, number, dp):
    end, source = jnp.int32(0), jnp.int32(0)
    for j in range(dp):
        end = end + count[j]
        source = source + jnp.where(end <= number, 1, 0)
    return source


def run(copies):
    for copy in copies:
        copy.start()
    for copy in copies:
        copy.wait()


def pack_body(info, count, rows, out, sems):
    dp, blocks = out.shape[0], rows.shape[0]
    start = start_of(count, info[0], dp)
    copies = []
    for k in range(dp):
        block = jnp.minimum(lax.rem(k + OWNB * dp - start, dp), blocks - 1)
        copies.append(pltpu.make_async_copy(rows.at[block], out.at[k], sems.at[k]))
    run(copies)


def pack(rows, info, count, dp):
    _, here, d = rows.shape
    return pl.pallas_call(
        pack_body,
        out_shape=jax.ShapeDtypeStruct((dp, here, d), BF16),
        grid_spec=pltpu.PrefetchScalarGridSpec(
            num_scalar_prefetch=2,
            grid=(1,),
            in_specs=[pl.BlockSpec(memory_space=pl.ANY)],
            out_specs=pl.BlockSpec((dp, here, d), lambda n, i, c: (0, 0, 0)),
            scratch_shapes=[pltpu.SemaphoreType.DMA((dp,))],
        ),
        compiler_params=pltpu.CompilerParams(vmem_limit_bytes=VMEM_LIMIT),
        cost_estimate=SHORT,
    )(info, count, rows)


def select_body(info, count, patches, arrived, out, sems):
    dp, here = arrived.shape[0], out.shape[1]
    copies, filled = [], []
    for m in range(OWNB):
        number = info[0] + dp * m
        source = source_of(count, number, dp)
        filled.append(patches[source, number - start_of(count, source, dp)])
        copies.append(pltpu.make_async_copy(arrived.at[source], out.at[m], sems.at[m]))
    run(copies)
    row = lax.broadcasted_iota(jnp.int32, out.shape[1:], 0) + info[1] * here
    for m in range(OWNB):
        out[m] = jnp.where(row < filled[m], out[m].astype(F32), 0.0).astype(out.dtype)


def select(arrived, info, count, patches):
    _, here, d = arrived.shape
    return pl.pallas_call(
        select_body,
        out_shape=jax.ShapeDtypeStruct((OWNB, here, d), BF16),
        grid_spec=pltpu.PrefetchScalarGridSpec(
            num_scalar_prefetch=3,
            grid=(1,),
            in_specs=[pl.BlockSpec(memory_space=pl.ANY)],
            out_specs=pl.BlockSpec((OWNB, here, d), lambda n, i, c, p: (0, 0, 0)),
            scratch_shapes=[pltpu.SemaphoreType.DMA((OWNB,))],
        ),
        compiler_params=pltpu.CompilerParams(vmem_limit_bytes=VMEM_LIMIT),
        cost_estimate=SHORT,
    )(info, count, patches, arrived)


def block_of(size, most):
    for width in range(most, 0, -128):
        if size % width == 0:
            return width
    return size


def load_rows(own, sib, rows):
    half = own.shape[0]
    rows[:half] = own[...]
    rows[half:] = sib[...]


def put_partner_columns(info, rows, out, hidden, chips):
    core, chip = info[0] & 1, info[0] >> 1
    width = rows.shape[1] // chips
    away = 1 - pool_bit(chip, core)
    for j in range(chips // 2):
        at = pl.multiple_of(chip_with(j, away, core) * width, 128)
        out[:, hidden + j * width:hidden + (j + 1) * width] = rows[:, pl.ds(at, width)]


def up_body(info, own, sib, w, out, slope, rows, *, hidden, chips):
    n = pl.program_id(0)

    @pl.when(n == 0)
    def _():
        load_rows(own, sib, rows)
        put_partner_columns(info, rows, out, hidden, chips)

    pre_act = jnp.dot(rows[...], w[...], preferred_element_type=F32)
    cdf = 0.5 * (1.0 + lax.erf(pre_act * 0.7071067811865476))
    density = jnp.exp(-0.5 * pre_act * pre_act) * 0.3989422804014327
    width = w.shape[1]
    out[:, pl.ds(pl.multiple_of(n * width, 128), width)] = (pre_act * cdf).astype(out.dtype)
    slope[...] = (cdf + pre_act * density).astype(slope.dtype)


def down_body(info, own, sib, w, slope, out, rows, *, hidden, chips):
    n = pl.program_id(0)

    @pl.when(n == 0)
    def _():
        load_rows(own, sib, rows)
        if out.shape[1] > hidden:
            put_partner_columns(info, rows, out, hidden, chips)

    act_grad = jnp.dot(rows[...], w[...], preferred_element_type=F32)
    width = w.shape[1]
    out[:, pl.ds(pl.multiple_of(n * width, 128), width)] = (act_grad * slope[...]).astype(out.dtype)


def columns_body(info, own, sib, out, rows, *, chips):
    load_rows(own, sib, rows)
    put_partner_columns(info, rows, out, 0, chips)


def partner_columns(own, sib, info, chips):
    half, d = own.shape
    spec = pl.BlockSpec((half, d), lambda n, i: (0, 0))
    return pl.pallas_call(
        functools.partial(columns_body, chips=chips),
        out_shape=jax.ShapeDtypeStruct((2 * half, d // 2), BF16),
        grid_spec=pltpu.PrefetchScalarGridSpec(
            num_scalar_prefetch=1,
            grid=(1,),
            in_specs=[spec, spec],
            out_specs=pl.BlockSpec((2 * half, d // 2), lambda n, i: (0, 0)),
            scratch_shapes=[pltpu.VMEM((2 * half, d), BF16)],
        ),
        compiler_params=pltpu.CompilerParams(vmem_limit_bytes=VMEM_LIMIT),
        cost_estimate=SHORT,
    )(info, own, sib)


def forward(own, sib, w, info, chips, slope=None, with_columns=True):
    half, d = own.shape
    hidden = w.shape[1] // 2
    width = block_of(hidden, 768)
    steps = hidden // width
    total = hidden + (d // 2 if with_columns else 0)
    out_shape = jax.ShapeDtypeStruct((2 * half, total), BF16)
    out_specs = pl.BlockSpec((2 * half, total), lambda n, i: (0, 0))
    slope_spec = pl.BlockSpec((2 * half, width), lambda n, i: (0, n))
    rows_spec = pl.BlockSpec((half, d), lambda n, i: (0, 0))
    w_spec = pl.BlockSpec((d, width), lambda n, i: (0, (i[0] & 1) * steps + n))
    in_specs = [rows_spec, rows_spec, w_spec]
    operands = [own, sib, w]
    if slope is None:
        body = up_body
        out_shape = (out_shape, jax.ShapeDtypeStruct((2 * half, hidden), BF16))
        out_specs = (out_specs, slope_spec)
    else:
        body = down_body
        in_specs.append(slope_spec)
        operands.append(slope)
    return pl.pallas_call(
        functools.partial(body, hidden=hidden, chips=chips),
        out_shape=out_shape,
        grid_spec=pltpu.PrefetchScalarGridSpec(
            num_scalar_prefetch=1,
            grid=(steps,),
            in_specs=in_specs,
            out_specs=out_specs,
            scratch_shapes=[pltpu.VMEM((2 * half, d), BF16)],
        ),
        compiler_params=pltpu.CompilerParams(vmem_limit_bytes=VMEM_LIMIT),
        cost_estimate=SHORT,
    )(info, *operands)


def input_body(info, pre, w, own, sib):
    value = lax.dot_general(pre[...], w[...], (((1,), (1,)), ((), ())), preferred_element_type=F32)
    half = own.shape[0]
    own[...] = value[:half].astype(own.dtype)
    sib[...] = value[half:].astype(sib.dtype)


def input_part(pre, w, info):
    rows = pre.shape[0]
    d, hidden = w.shape[0], w.shape[1] // 2
    width = block_of(d, 1536)
    shape = jax.ShapeDtypeStruct((rows // 2, d), BF16)
    spec = pl.BlockSpec((rows // 2, width), lambda n, i: (0, n))
    return pl.pallas_call(
        input_body,
        out_shape=(shape, shape),
        grid_spec=pltpu.PrefetchScalarGridSpec(
            num_scalar_prefetch=1,
            grid=(d // width,),
            in_specs=[
                pl.BlockSpec((rows, hidden), lambda n, i: (0, 0)),
                pl.BlockSpec((width, hidden), lambda n, i: (n, i[0] & 1)),
            ],
            out_specs=(spec, spec),
        ),
        compiler_params=pltpu.CompilerParams(vmem_limit_bytes=VMEM_LIMIT),
        cost_estimate=SHORT,
    )(info, pre, w)


def weight_body(at, *refs, begins, width, block):
    slots = len(begins)
    ins, outs, (left, right, total, left_sems, right_sems) = refs[:5 * slots], refs[5 * slots:-5], refs[-5:]
    half, hidden = ins[0].shape[0], right.shape[1]
    copies = []
    for s in range(slots):
        own, sib, there, mine, theirs = ins[5 * s:5 * s + 5]
        first = 4 * s * half
        for k, (rows, column, to, size) in enumerate((
            (own, at[0] * width, first, half),
            (sib, at[0] * width, first + half, half),
            (there, begins[s] + at[1] * width, first + 2 * half, 2 * half),
        )):
            source = rows.at[:, pl.ds(pl.multiple_of(column, 128), width)]
            copies.append(pltpu.make_async_copy(source, left.at[pl.ds(to, size)], left_sems.at[3 * s + k]))
        for k, hidden_side in enumerate((mine, theirs)):
            source = hidden_side.at[:, pl.ds(0, hidden)]
            to = right.at[pl.ds(first + 2 * k * half, 2 * half)]
            copies.append(pltpu.make_async_copy(source, to, right_sems.at[2 * s + k]))
    for copy in copies:
        copy.start()
    middle = slots // 2
    dims = (((0,), (0,)), ((), ()))
    early = 4 * middle * half
    span = width // 2
    is_first = at[2] == 0

    def by_columns(body):
        def step(n, carry):
            body(pl.ds(pl.multiple_of(n * block, 128), block))
            return carry

        lax.fori_loop(0, hidden // block, step, 0)

    def first_rows(cut):
        total[:, cut] = lax.dot_general(left[:early], right[:early, cut], dims, preferred_element_type=F32)

    def last_rows(cut):
        value = total[:, cut] + lax.dot_general(left[early:], right[early:, cut], dims, preferred_element_type=F32)
        if len(outs) == 1:
            outs[0][:, cut] = value.astype(outs[0].dtype)
        else:
            low, high = value[:span], value[span:]
            outs[0][:, cut] = jnp.where(is_first, low, high).astype(outs[0].dtype)
            outs[1][:, cut] = jnp.where(is_first, high, low).astype(outs[1].dtype)

    for copy in copies[:5 * middle]:
        copy.wait()
    by_columns(first_rows)
    for copy in copies[5 * middle:]:
        copy.wait()
    by_columns(last_rows)


def weight_part(rows, there_rows, rights, own_at, there_at, core, width, hidden, split):
    slots, size = len(rows), 2 * rows[0][0].shape[0]
    at = jnp.stack([own_at, there_at, core]).astype(jnp.int32)
    block = block_of(hidden, 512)
    operands = []
    for (own, sib), (there, _), (mine, theirs) in zip(rows, there_rows, rights):
        operands += [own, sib, there, mine, theirs]
    pieces = 2 if split else 1
    shape = jax.ShapeDtypeStruct((width // pieces, hidden), BF16)
    spec = pl.BlockSpec((width // pieces, hidden), lambda n, a: (0, 0))
    return pl.pallas_call(
        functools.partial(weight_body, begins=[begin for _, begin in there_rows], width=width, block=block),
        out_shape=(shape,) * pieces,
        grid_spec=pltpu.PrefetchScalarGridSpec(
            num_scalar_prefetch=1,
            grid=(1,),
            in_specs=[pl.BlockSpec(memory_space=pl.ANY)] * len(operands),
            out_specs=(spec,) * pieces,
            scratch_shapes=[
                pltpu.VMEM((2 * slots * size, width), BF16),
                pltpu.VMEM((2 * slots * size, hidden), BF16),
                pltpu.VMEM((width, hidden), F32),
                pltpu.SemaphoreType.DMA((3 * slots,)),
                pltpu.SemaphoreType.DMA((2 * slots,)),
            ],
        ),
        compiler_params=pltpu.CompilerParams(vmem_limit_bytes=VMEM_LIMIT),
        cost_estimate=SHORT,
    )(at, *operands)


def add(*values):
    return sum(v.astype(F32) for v in values).astype(BF16)


def local(x_rows, g_rows, w_up, w_down_t, block_count, patches):
    dp, tensor = lax.axis_size("dp"), lax.axis_size("tensor")
    chips = dp // 2
    me, plane = lax.axis_index("dp"), lax.axis_index("tensor")
    chip, core = me >> 1, me & 1
    info = jnp.stack([me, plane]).astype(jnp.int32)
    here, d = x_rows.shape[1:]
    hidden = w_up.shape[1] // 2
    ring = [(i, (i + 1) % tensor) for i in range(tensor)]
    to_sibling = [(i, i ^ 1) for i in range(dp)]
    to_pool = chip_perm(dp, lambda c: 1 << c)
    last = []

    def after(*values):
        out = lax.optimization_barrier((*values, *last))[:len(values)]
        return out if len(out) > 1 else out[0]

    def done(value):
        last[:] = [value]
        return value

    def onward(piece):
        return lax.ppermute(piece, "tensor", ring)

    def sibling(piece):
        return lax.ppermute(piece, "dp", to_sibling)

    def pooled(piece):
        return lax.ppermute(piece, "dp", to_pool)

    def exchange(rows):
        return lax.all_to_all(rows, "dp", split_axis=0, concat_axis=0, tiled=True)

    def chosen(arrived):
        return done(select(after(arrived), info, block_count, patches)).reshape(OWNB * here, d)

    def arrive(own, sib, ahead, further=True):
        piece = after(ahead)
        own.append(piece)
        sib.append(sibling(piece))
        return onward(piece) if further else None

    x_own, x_sib, x_there = [], [], []
    g_own, g_sib, g_there = [], [], []
    act, slope, pre, shares, pools = [], [], [], [], {}

    def settle(*names):
        last.extend(pools[name] for name in names if name in pools)

    def up(s):
        mine, slope_s = forward(*after(x_own[s], x_sib[s]), w_up, info, chips)
        theirs = pools["x", s] = pooled(done(mine))
        x_there.append((theirs, hidden))
        slope.append(slope_s)
        act.append((mine, theirs))

    def down(s, with_columns=True):
        mine = forward(*after(g_own[s], g_sib[s]), w_down_t, info, chips, slope[s], with_columns)
        theirs = pools["g", s] = pooled(done(mine))
        if with_columns:
            g_there.append((theirs, hidden))
        pre.append((mine, theirs))

    def share(s):
        own, sib = input_part(after(pre[s][0]), w_up, info)
        pools["share", s] = sibling(done(sib))
        shares.append((own, pools["share", s]))

    send_x = done(pack(x_rows, info, block_count, dp))
    arrived_x = exchange(send_x)
    send_g = done(pack(after(g_rows), info, block_count, dp))
    arrived_g = exchange(lax.optimization_barrier((send_g, arrived_x))[0])
    x_own.append(chosen(arrived_x))
    x_sib.append(sibling(x_own[0]))
    x_ahead = onward(x_own[0])
    up(0)
    end = tensor - 1
    for s in range(1, tensor):
        x_ahead = arrive(x_own, x_sib, x_ahead, s < end)
        if s == end:
            g_ahead = onward(after(g_own[0]))
        settle(("x", s - 2))
        up(s)
        if s == 1:
            g_own.append(chosen(arrived_g))
            g_sib.append(sibling(g_own[0]))
        if s == 2:
            settle(("x", 1))
            down(0)
    settle(("x", end - 1))
    share(0)
    for s in range(1, end):
        g_ahead = arrive(g_own, g_sib, g_ahead)
        settle(("share", s - 1), ("x", end) if s > 1 else None, ("g", s - 2))
        down(s)
        settle(("g", 0))
        share(s)

    settle(("g", end - 2))
    first_share = done(add(*after(*shares[1])))
    arrive(g_own, g_sib, g_ahead, False)
    running = onward(lax.optimization_barrier((first_share, g_own[end]))[0])
    columns = done(partner_columns(*after(g_own[end], g_sib[end]), info, chips))
    pools["columns"] = pooled(columns)
    g_there.append((pools["columns"], 0))
    settle(("share", end - 1), ("g", end - 1))
    down(end, False)

    span = d // dp
    near, mine_j = pool_bit(chip, core), other_bits(chip, core)

    def part(r, rows, there, rights, split):
        j = mine_j ^ r
        rows = [after(*rows[0]), *rows[1:]]
        parts = weight_part(
            rows, there, rights, chip_with(j, near, core), j, core, 2 * span, hidden, split
        )
        done(parts[0])
        return list(parts)

    bits = (chips // 2).bit_length() - 1

    def pass_on(parts):
        for k in reversed(range(1, bits)):
            perm = chip_perm(dp, lambda c: 2 << k)
            for r in range(1 << k, 2 << k):
                sent = [lax.ppermute(p, "dp", perm) for p in parts[r]]
                kept = parts.get(r ^ (1 << k))
                parts[r ^ (1 << k)] = [add(*both) for both in zip(kept, sent)] if kept else sent
        flip = lambda c: 2 >> c
        return [lax.ppermute(p, "dp", chip_perm(dp, flip, h == 1)) for h, p in enumerate(parts[1])]

    def core_rows(value, which):
        return lax.dynamic_slice_in_dim(value, which * span, span, 0)

    def finished(kept, parts, sent):
        if 0 in parts:
            kept = [add(*both) for both in zip(kept, parts[0])]
        if len(kept) == 2:
            mine = add(after(kept[0]), sent[0])
            other = add(sibling(kept[1]), sent[1])
        else:
            other = sibling(add(core_rows(kept[0], 1 - core), core_rows(sent[0], 1 - core)))
            mine = add(core_rows(after(kept[0]), core), core_rows(sent[0], core))
        return done(jnp.where(
            core == 0, jnp.concatenate([mine, other], axis=1), jnp.concatenate([other, mine], axis=1)
        ))

    down_sum = (list(zip(g_own, g_sib)), g_there, act, True)
    up_sum = (list(zip(x_own, x_sib)), x_there, pre, True)
    away = list(reversed(range(1, chips // 2)))
    settle("columns")
    last.append(running)
    down_parts = {r: part(r, *down_sum) for r in away}
    down_sent = pass_on(down_parts)
    settle(("g", end))
    for s in range(2, end):
        running = onward(done(add(*after(*shares[s]), running)))
    share(end)
    last.append(down_sent[0])
    up_parts = {r: part(r, *up_sum) for r in away}
    up_sent = pass_on(up_parts)
    down_kept = part(0, *down_sum)
    last.append(down_sent[1])
    running = onward(done(add(*after(*shares[end]), running)))
    last.append(up_sent[0])
    up_kept = part(0, *up_sum)
    last.append(up_sent[1])
    down_grad = finished(down_kept, down_parts, down_sent)
    up_grad = finished(up_kept, up_parts, up_sent)
    input_grad = add(*after(*shares[0]), running).reshape(OWNB, here, d)
    return input_grad, up_grad, down_grad


def solution(mesh):
    placed = (
        P("dp", "tensor", None),
        P("dp", "tensor", None),
        P(None, "tensor"),
        P(None, "tensor"),
        P(),
        P(),
    )
    return jax.shard_map(
        local,
        mesh=mesh,
        in_specs=placed,
        out_specs=(P("dp", "tensor", None), P("dp", "tensor"), P("dp", "tensor")),
        check_vma=False,
    )
```

profile of v0, /device:TPU:0, one launch (start us, length us, event | category | flops | bytes accessed | tf_op | source)
XLA Modules:
  0.0 271.5 jit_solution(15716050768000672490)
XLA Ops:
  1.2 3.4 %shard_map.85 = bf16[8,32,3072]{2,1,0:T(8,128)(2,1)} custom-call(s32[2]{0:T(128)} %pad_add_fusion.info, s32[8]{0:T(128)} %count.7, bf16[8,32,3072]{2,1,0:T(8,128)(2,1)} %rows.1), custom_call_target="tpu_custom_call" | custom-call | flops 1 | bytes 1 | tf_op jit(solution)/shard_map/pallas_call | solution.py:67
  4.6 5.2 %all-to-all-start = ((bf16[8,32,3072]{2,1,0:T(8,128)(2,1)}), bf16[8,32,3072]{2,1,0:T(8,128)(2,1)}, u32[]{:S(2)}, u32[]{:S(2)}) async-start(bf16[8,32,3072]{2,1,0:T(8,128)(2,1)} %shard_map.85), calls=%async_computation | async-start | bytes 3145728 | tf_op jit(solution)/shard_map/all_to_all | solution.py:374
  9.8 3.4 %shard_map.86 = bf16[8,32,3072]{2,1,0:T(8,128)(2,1)} custom-call(s32[2]{0:T(128)} %pad_add_fusion.info, s32[8]{0:T(128)} %count.7, bf16[8,32,3072]{2,1,0:T(8,128)(2,1)} %rows.2), custom_call_target="tpu_custom_call" | custom-call | flops 1 | bytes 1 | tf_op jit(solution)/shard_map/pallas_call | solution.py:67
  13.2 17.8 %all-to-all-done.arrived = bf16[8,32,3072]{2,1,0:T(8,128)(2,1)} async-done(((bf16[8,32,3072]{2,1,0:T(8,128)(2,1)}), bf16[8,32,3072]{2,1,0:T(8,128)(2,1)}, u32[]{:S(2)}, u32[]{:S(2)}) %all-to-all-start) | async-done | bytes 1572896 | tf_op jit(solution)/shard_map/all_to_all | solution.py:374
  30.9 3.1 %shard_map.87 = bf16[4,32,3072]{2,1,0:T(8,128)(2,1)} custom-call(s32[2]{0:T(128)} %pad_add_fusion.info, s32[8]{0:T(128)} %count.7, s32[8,8]{1,0:T(8,128)} %patches.3, bf16[8,32,3072]{2,1,0:T(8,128)(2,1)} %all-to-all-done.arrived), custom_call_target="tpu_custom_call" | custom-call | flops 1 | bytes 1 | tf_op jit(solution)/shard_map/pallas_call | solution.py:98
  34.1 2.1 collective-permute-start
  36.2 4.3 %all-to-all-start.1 = ((bf16[8,32,3072]{2,1,0:T(8,128)(2,1)}), bf16[8,32,3072]{2,1,0:T(8,128)(2,1)}, u32[]{:S(2)}, u32[]{:S(2)}) async-start(bf16[8,32,3072]{2,1,0:T(8,128)(2,1)} %shard_map.86), calls=%async_computation.1 | async-start | bytes 3145728 | tf_op jit(solution)/shard_map/all_to_all | solution.py:374
  40.5 8.1 %shard_map.88 = (bf16[256,3072]{1,0:T(8,128)(2,1)}, bf16[256,1536]{1,0:T(8,128)(2,1)}) custom-call(s32[2]{0:T(128)} %pad_add_fusion.info, bf16[128,3072]{1,0:T(8,128)(2,1)} %bitcast.12, bf16[128,3072]{1,0:T(8,128)(2,1)} %collective-permute-done.1.sib.refs_1_, bf16[3072,3072]{1,0:T(8,128)(2,1)} %w.23), custom_call_target="tpu_custom_call" | custom-call | flops 1 | bytes 1 | tf_op jit(solution)/shard_map/pallas_call | solution.py:209
  48.6 8.1 %collective-permute-done.own.refs_5_ = bf16[128,3072]{1,0:T(8,128)(2,1)} collective-permute-done((bf16[128,3072]{1,0:T(8,128)(2,1)}, bf16[128,3072]{1,0:T(8,128)(2,1)}, u32[]{:S(2)}, u32[]{:S(2)}) %collective-permute-start) | collective-permute-done | bytes 786464 | tf_op jit(solution)/shard_map/ppermute | solution.py:365
  57.2 2.1 collective-permute-done.2.sib.refs_6_
  59.3 8.1 %shard_map.89 = (bf16[256,3072]{1,0:T(8,128)(2,1)}, bf16[256,1536]{1,0:T(8,128)(2,1)}) custom-call(s32[2]{0:T(128)} %pad_add_fusion.info, bf16[128,3072]{1,0:T(8,128)(2,1)} %collective-permute-done.own.refs_5_, bf16[128,3072]{1,0:T(8,128)(2,1)} %collective-permute-done.2.sib.refs_6_, bf16[3072,3072]{1,0:T(8,128)(2,1)} %w.23), custom_call_target="tpu_custom_call" | custom-call | flops 1 | bytes 1 | tf_op jit(solution)/shard_map/pallas_call | solution.py:209
  67.9 3.0 %shard_map.90 = bf16[4,32,3072]{2,1,0:T(8,128)(2,1)} custom-call(s32[2]{0:T(128)} %pad_add_fusion.info, s32[8]{0:T(128)} %count.7, s32[8,8]{1,0:T(8,128)} %patches.3, bf16[8,32,3072]{2,1,0:T(8,128)(2,1)} %all-to-all-done.1.arrived), custom_call_target="tpu_custom_call" | custom-call | flops 1 | bytes 1 | tf_op jit(solution)/shard_map/pallas_call | solution.py:98
  70.9 7.8 %collective-permute-done.4.own.refs_10_ = bf16[128,3072]{1,0:T(8,128)(2,1)} collective-permute-done((bf16[128,3072]{1,0:T(8,128)(2,1)}, bf16[128,3072]{1,0:T(8,128)(2,1)}, u32[]{:S(2)}, u32[]{:S(2)}) %collective-permute-start.4) | collective-permute-done | bytes 786464 | tf_op jit(solution)/shard_map/ppermute | solution.py:365
  79.3 2.1 collective-permute-done.5.sib.refs_11_
  81.4 8.1 %shard_map.91 = (bf16[256,3072]{1,0:T(8,128)(2,1)}, bf16[256,1536]{1,0:T(8,128)(2,1)}) custom-call(s32[2]{0:T(128)} %pad_add_fusion.info, bf16[128,3072]{1,0:T(8,128)(2,1)} %collective-permute-done.4.own.refs_10_, bf16[128,3072]{1,0:T(8,128)(2,1)} %collective-permute-done.5.sib.refs_11_, bf16[3072,3072]{1,0:T(8,128)(2,1)} %w.23), custom_call_target="tpu_custom_call" | custom-call | flops 1 | bytes 1 | tf_op jit(solution)/shard_map/pallas_call | solution.py:209
  90.0 4.3 %collective-permute-done.7.refs_9_.refs_7_ = bf16[256,3072]{1,0:T(8,128)(2,1)} collective-permute-done((bf16[256,3072]{1,0:T(8,128)(2,1)}, bf16[256,3072]{1,0:T(8,128)(2,1)}, u32[]{:S(2)}, u32[]{:S(2)}) %collective-permute-start.7) | collective-permute-done | bytes 1572896 | tf_op jit(solution)/shard_map/ppermute | solution.py:371
  94.3 7.7 %shard_map.92.pre.refs_3_ = bf16[256,3072]{1,0:T(8,128)(2,1)} custom-call(s32[2]{0:T(128)} %pad_add_fusion.info, bf16[128,3072]{1,0:T(8,128)(2,1)} %bitcast.16, bf16[128,3072]{1,0:T(8,128)(2,1)} %collective-permute-done.3.sib.refs_1_, bf16[3072,3072]{1,0:T(8,128)(2,1)} %w.22, bf16[256,1536]{1,0:T(8,128)(2,1)} %get-tuple-element.96.slope), custom_call_target="tpu_custom_call" | custom-call | flops 1 | bytes 1 | tf_op jit(solution)/shard_map/pallas_call | solution.py:209
  103.1 1.6 collective-permute-start.12
  105.3 8.0 %shard_map.93 = (bf16[256,3072]{1,0:T(8,128)(2,1)}, bf16[256,1536]{1,0:T(8,128)(2,1)}) custom-call(s32[2]{0:T(128)} %pad_add_fusion.info, bf16[128,3072]{1,0:T(8,128)(2,1)} %collective-permute-done.8.own.refs_15_, bf16[128,3072]{1,0:T(8,128)(2,1)} %collective-permute-done.9.sib.refs_16_, bf16[3072,3072]{1,0:T(8,128)(2,1)} %w.23), custom_call_target="tpu_custom_call" | custom-call | flops 1 | bytes 1 | tf_op jit(solution)/shard_map/pallas_call | solution.py:209
  113.3 7.0 %shard_map.94 = (bf16[128,3072]{1,0:T(8,128)(2,1)}, bf16[128,3072]{1,0:T(8,128)(2,1)}) custom-call(s32[2]{0:T(128)} %pad_add_fusion.info, bf16[256,3072]{1,0:T(8,128)(2,1)} %shard_map.92.pre.refs_3_, bf16[3072,3072]{1,0:T(8,128)(2,1)} %w.23), custom_call_target="tpu_custom_call" | custom-call | flops 1 | bytes 1 | tf_op jit(solution)/shard_map/pallas_call | solution.py:237
  120.3 4.4 %collective-permute-done.12.own.refs_5_ = bf16[128,3072]{1,0:T(8,128)(2,1)} collective-permute-done((bf16[128,3072]{1,0:T(8,128)(2,1)}, bf16[128,3072]{1,0:T(8,128)(2,1)}, u32[]{:S(2)}, u32[]{:S(2)}) %collective-permute-start.12) | collective-permute-done | bytes 786464 | tf_op jit(solution)/shard_map/ppermute | solution.py:365
  125.7 1.6 collective-permute-done.14.sib.refs_6_
  128.4 7.8 %shard_map.95.pre.refs_8_ = bf16[256,3072]{1,0:T(8,128)(2,1)} custom-call(s32[2]{0:T(128)} %pad_add_fusion.info, bf16[128,3072]{1,0:T(8,128)(2,1)} %collective-permute-done.12.own.refs_5_, bf16[128,3072]{1,0:T(8,128)(2,1)} %collective-permute-done.14.sib.refs_6_, bf16[3072,3072]{1,0:T(8,128)(2,1)} %w.22, bf16[256,1536]{1,0:T(8,128)(2,1)} %get-tuple-element.108.slope), custom_call_target="tpu_custom_call" | custom-call | flops 1 | bytes 1 | tf_op jit(solution)/shard_map/pallas_call | solution.py:209
  136.7 7.0 %shard_map.96 = (bf16[128,3072]{1,0:T(8,128)(2,1)}, bf16[128,3072]{1,0:T(8,128)(2,1)}) custom-call(s32[2]{0:T(128)} %pad_add_fusion.info, bf16[256,3072]{1,0:T(8,128)(2,1)} %shard_map.95.pre.refs_8_, bf16[3072,3072]{1,0:T(8,128)(2,1)} %w.23), custom_call_target="tpu_custom_call" | custom-call | flops 1 | bytes 1 | tf_op jit(solution)/shard_map/pallas_call | solution.py:237
  143.7 3.0 %collective-permute-done.13.own.refs_10_ = bf16[128,3072]{1,0:T(8,128)(2,1)} collective-permute-done((bf16[128,3072]{1,0:T(8,128)(2,1)}, bf16[128,3072]{1,0:T(8,128)(2,1)}, u32[]{:S(2)}, u32[]{:S(2)}) %collective-permute-start.13) | collective-permute-done | bytes 786464 | tf_op jit(solution)/shard_map/ppermute | solution.py:365
  147.3 2.1 collective-permute-done.18.sib.refs_11_
  150.5 7.8 %shard_map.97.pre.refs_13_ = bf16[256,3072]{1,0:T(8,128)(2,1)} custom-call(s32[2]{0:T(128)} %pad_add_fusion.info, bf16[128,3072]{1,0:T(8,128)(2,1)} %collective-permute-done.13.own.refs_10_, bf16[128,3072]{1,0:T(8,128)(2,1)} %collective-permute-done.18.sib.refs_11_, bf16[3072,3072]{1,0:T(8,128)(2,1)} %w.22, bf16[256,1536]{1,0:T(8,128)(2,1)} %get-tuple-element.115.slope), custom_call_target="tpu_custom_call" | custom-call | flops 1 | bytes 1 | tf_op jit(solution)/shard_map/pallas_call | solution.py:209
  158.8 7.0 %shard_map.98 = (bf16[128,3072]{1,0:T(8,128)(2,1)}, bf16[128,3072]{1,0:T(8,128)(2,1)}) custom-call(s32[2]{0:T(128)} %pad_add_fusion.info, bf16[256,3072]{1,0:T(8,128)(2,1)} %shard_map.97.pre.refs_13_, bf16[3072,3072]{1,0:T(8,128)(2,1)} %w.23), custom_call_target="tpu_custom_call" | custom-call | flops 1 | bytes 1 | tf_op jit(solution)/shard_map/pallas_call | solution.py:237
  165.8 2.4 add_convert_fusion.7
  169.3 2.1 collective-permute-done.21.sib.refs_16_
  171.5 3.1 %shard_map.99 = bf16[256,1536]{1,0:T(8,128)(2,1)} custom-call(s32[2]{0:T(128)} %pad_add_fusion.info, bf16[128,3072]{1,0:T(8,128)(2,1)} %collective-permute-done.16.own.refs_15_, bf16[128,3072]{1,0:T(8,128)(2,1)} %collective-permute-done.21.sib.refs_16_), custom_call_target="tpu_custom_call" | custom-call | flops 1 | bytes 1 | tf_op jit(solution)/shard_map/pallas_call | solution.py:173
  175.5 4.1 %collective-permute-done.23.refs_12_.refs_14_ = bf16[256,3072]{1,0:T(8,128)(2,1)} collective-permute-done((bf16[256,3072]{1,0:T(8,128)(2,1)}, bf16[256,3072]{1,0:T(8,128)(2,1)}, u32[]{:S(2)}, u32[]{:S(2)}) %collective-permute-start.23) | collective-permute-done | bytes 1572896 | tf_op jit(solution)/shard_map/ppermute | solution.py:371
  179.6 7.4 %shard_map.100.pre.refs_18_ = bf16[256,1536]{1,0:T(8,128)(2,1)} custom-call(s32[2]{0:T(128)} %pad_add_fusion.info, bf16[128,3072]{1,0:T(8,128)(2,1)} %collective-permute-done.16.own.refs_15_, bf16[128,3072]{1,0:T(8,128)(2,1)} %collective-permute-done.21.sib.refs_16_, bf16[3072,3072]{1,0:T(8,128)(2,1)} %w.22, bf16[256,1536]{1,0:T(8,128)(2,1)} %get-tuple-element.125.slope), custom_call_target="tpu_custom_call" | custom-call | flops 1 | bytes 1 | tf_op jit(solution)/shard_map/pallas_call | solution.py:209
  188.1 2.8 %collective-permute-done.25 = bf16[128,3072]{1,0:T(8,128)(2,1)} collective-permute-done((bf16[128,3072]{1,0:T(8,128)(2,1)}, bf16[128,3072]{1,0:T(8,128)(2,1)}, u32[]{:S(2)}, u32[]{:S(2)}) %collective-permute-start.25) | collective-permute-done | bytes 786464 | tf_op jit(solution)/shard_map/ppermute | solution.py:365
  190.9 11.0 %shard_map.101 = (bf16[384,1536]{1,0:T(8,128)(2,1)}, bf16[384,1536]{1,0:T(8,128)(2,1)}) custom-call(s32[3]{0:T(128)} %get-tuple-element.156.at, bf16[128,3072]{1,0:T(8,128)(2,1)} %bitcast.18, bf16[128,3072]{1,0:T(8,128)(2,1)} %collective-permute-done.3.sib.refs_1_, bf16[256,3072]{1,0:T(8,128)(2,1)} %collective-permute-done.15.refs_2_.refs_4_, ...), custom_call_target="tpu_custom_call" | custom-call | flops 1 | bytes 1 | tf_op jit(solution)/shard_map/pallas_call | solution.py:318
  202.9 2.9 %add_convert_fusion.6 = bf16[128,3072]{1,0:T(8,128)(2,1)} fusion(bf16[128,3072]{1,0:T(8,128)(2,1)} %collective-permute-done.25, bf16[128,3072]{1,0:T(8,128)(2,1)} %collective-permute-done.22, bf16[128,3072]{1,0:T(8,128)(2,1)} %get-tuple-element.131), kind=kLoop, calls=%fused_computation.8 | loop fusion | flops 2359296 | bytes 3145728 | tf_op jit(solution)/shard_map/convert_element_type | solution.py:340
  205.7 7.0 %shard_map.102 = (bf16[128,3072]{1,0:T(8,128)(2,1)}, bf16[128,3072]{1,0:T(8,128)(2,1)}) custom-call(s32[2]{0:T(128)} %pad_add_fusion.info, bf16[256,1536]{1,0:T(8,128)(2,1)} %shard_map.100.pre.refs_18_, bf16[3072,3072]{1,0:T(8,128)(2,1)} %w.23), custom_call_target="tpu_custom_call" | custom-call | flops 1 | bytes 1 | tf_op jit(solution)/shard_map/pallas_call | solution.py:237
  214.0 4.5 %collective-permute-done.28 = bf16[384,1536]{1,0:T(8,128)(2,1)} collective-permute-done((bf16[384,1536]{1,0:T(8,128)(2,1)}, bf16[384,1536]{1,0:T(8,128)(2,1)}, u32[]{:S(2)}, u32[]{:S(2)}) %collective-permute-start.28) | collective-permute-done | bytes 1179680 | tf_op jit(solution)/shard_map/ppermute | solution.py:473
  218.5 11.1 %shard_map.103 = (bf16[384,1536]{1,0:T(8,128)(2,1)}, bf16[384,1536]{1,0:T(8,128)(2,1)}) custom-call(s32[3]{0:T(128)} %get-tuple-element.156.at, bf16[128,3072]{1,0:T(8,128)(2,1)} %bitcast.13, bf16[128,3072]{1,0:T(8,128)(2,1)} %collective-permute-done.1.sib.refs_1_, bf16[256,3072]{1,0:T(8,128)(2,1)} %collective-permute-done.6.refs_4_.refs_2_, ...), custom_call_target="tpu_custom_call" | custom-call | flops 1 | bytes 1 | tf_op jit(solution)/shard_map/pallas_call | solution.py:318
  230.5 11.0 %shard_map.104 = (bf16[384,1536]{1,0:T(8,128)(2,1)}, bf16[384,1536]{1,0:T(8,128)(2,1)}) custom-call(s32[3]{0:T(128)} %get-tuple-element.155.at, bf16[128,3072]{1,0:T(8,128)(2,1)} %bitcast.19, bf16[128,3072]{1,0:T(8,128)(2,1)} %collective-permute-done.3.sib.refs_1_, bf16[256,3072]{1,0:T(8,128)(2,1)} %collective-permute-done.15.refs_2_.refs_4_, ...), custom_call_target="tpu_custom_call" | custom-call | flops 1 | bytes 1 | tf_op jit(solution)/shard_map/pallas_call | solution.py:318
  242.7 2.8 %add_convert_fusion.5 = bf16[128,3072]{1,0:T(8,128)(2,1)} fusion(bf16[128,3072]{1,0:T(8,128)(2,1)} %collective-permute-done.30, bf16[128,3072]{1,0:T(8,128)(2,1)} %collective-permute-done.27, bf16[128,3072]{1,0:T(8,128)(2,1)} %get-tuple-element.143), kind=kLoop, calls=%fused_computation.7 | loop fusion | flops 2359296 | bytes 3145728 | tf_op jit(solution)/shard_map/convert_element_type | solution.py:340
  246.1 10.9 %shard_map.105 = (bf16[384,1536]{1,0:T(8,128)(2,1)}, bf16[384,1536]{1,0:T(8,128)(2,1)}) custom-call(s32[3]{0:T(128)} %get-tuple-element.155.at, bf16[128,3072]{1,0:T(8,128)(2,1)} %bitcast.14, bf16[128,3072]{1,0:T(8,128)(2,1)} %collective-permute-done.1.sib.refs_1_, bf16[256,3072]{1,0:T(8,128)(2,1)} %collective-permute-done.6.refs_4_.refs_2_, ...), custom_call_target="tpu_custom_call" | custom-call | flops 1 | bytes 1 | tf_op jit(solution)/shard_map/pallas_call | solution.py:318
  257.2 1.7 collective-permute-start.34
  258.9 1.9 add_convert_fusion.2
  262.3 1.7 maximum_select_fusion
  265.6 1.6 add_convert_fusion
  267.2 1.7 maximum_select_fusion.1
  268.9 2.6 add_convert_fusion.4
  (67 shorter events, 20.6 us)
Async XLA Ops:
  4.6 26.3 %all-to-all-start = ((bf16[8,32,3072]{2,1,0:T(8,128)(2,1)}), bf16[8,32,3072]{2,1,0:T(8,128)(2,1)}, u32[]{:S(2)}, u32[]{:S(2)}) async-start(bf16[8,32,3072]{2,1,0:T(8,128)(2,1)} %shard_map.85), calls=%async_computation | async-start | bytes 3145728 | tf_op jit(solution)/shard_map/all_to_all | solution.py:374
  34.0 6.5 %collective-permute-start.1 = (bf16[128,3072]{1,0:T(8,128)(2,1)}, bf16[128,3072]{1,0:T(8,128)(2,1)}, u32[]{:S(2)}, u32[]{:S(2)}) collective-permute-start(bf16[128,3072]{1,0:T(8,128)(2,1)} %bitcast.10), channel_id=1, source_target_pairs={{0,4},{4,0},{8,12},{12,8},{16,20},{20,16},{24,28},{28,24},{1,5},{5... | collective-permute-start | bytes 2359304 | tf_op jit(solution)/shard_map/ppermute | solution.py:368
  34.1 22.6 %collective-permute-start = (bf16[128,3072]{1,0:T(8,128)(2,1)}, bf16[128,3072]{1,0:T(8,128)(2,1)}, u32[]{:S(2)}, u32[]{:S(2)}) collective-permute-start(bf16[128,3072]{1,0:T(8,128)(2,1)} %bitcast.11), channel_id=1, source_target_pairs={{0,1},{1,2},{2,3},{3,0},{4,5},{5,6},{6,7},{7,4},{8,9},{9,10},{10,1... | collective-permute-start | bytes 2359304 | tf_op jit(solution)/shard_map/ppermute | solution.py:365
  36.2 31.7 %all-to-all-start.1 = ((bf16[8,32,3072]{2,1,0:T(8,128)(2,1)}), bf16[8,32,3072]{2,1,0:T(8,128)(2,1)}, u32[]{:S(2)}, u32[]{:S(2)}) async-start(bf16[8,32,3072]{2,1,0:T(8,128)(2,1)} %shard_map.86), calls=%async_computation.1 | async-start | bytes 3145728 | tf_op jit(solution)/shard_map/all_to_all | solution.py:374
  56.7 2.6 collective-permute-start.2
  56.7 22.1 %collective-permute-start.4 = (bf16[128,3072]{1,0:T(8,128)(2,1)}, bf16[128,3072]{1,0:T(8,128)(2,1)}, u32[]{:S(2)}, u32[]{:S(2)}) collective-permute-start(bf16[128,3072]{1,0:T(8,128)(2,1)} %collective-permute-done.own.refs_5_), channel_id=1, source_target_pairs={{0,1},{1,2},{2,3},{3,0},{4,5},{5,6},{6,7},{7,4},{8,9},{9,10},{10,1... | collective-permute-start | bytes 2359304 | tf_op jit(solution)/shard_map/ppermute | solution.py:365
  56.7 22.6 %collective-permute-start.6 = (bf16[256,3072]{1,0:T(8,128)(2,1)}, bf16[256,3072]{1,0:T(8,128)(2,1)}, u32[]{:S(2)}, u32[]{:S(2)}) collective-permute-start(bf16[256,3072]{1,0:T(8,128)(2,1)} %get-tuple-element.84.refs_3_), channel_id=1, source_target_pairs={{0,8},{4,20},{8,0},{12,28},{16,24},{20,4},{24,16},{28,12},{1,9},{5... | collective-permute-start | bytes 4718600 | tf_op jit(solution)/shard_map/ppermute | solution.py:371
  67.4 26.9 %collective-permute-start.7 = (bf16[256,3072]{1,0:T(8,128)(2,1)}, bf16[256,3072]{1,0:T(8,128)(2,1)}, u32[]{:S(2)}, u32[]{:S(2)}) collective-permute-start(bf16[256,3072]{1,0:T(8,128)(2,1)} %get-tuple-element.88.refs_8_), channel_id=1, source_target_pairs={{0,8},{4,20},{8,0},{12,28},{16,24},{20,4},{24,16},{28,12},{1,9},{5... | collective-permute-start | bytes 4718600 | tf_op jit(solution)/shard_map/ppermute | solution.py:371
  78.7 2.6 collective-permute-start.5
  78.7 11.2 %collective-permute-start.3 = (bf16[128,3072]{1,0:T(8,128)(2,1)}, bf16[128,3072]{1,0:T(8,128)(2,1)}, u32[]{:S(2)}, u32[]{:S(2)}) collective-permute-start(bf16[128,3072]{1,0:T(8,128)(2,1)} %bitcast.15), channel_id=1, source_target_pairs={{0,4},{4,0},{8,12},{12,8},{16,20},{20,16},{24,28},{28,24},{1,5},{5... | collective-permute-start | bytes 2359304 | tf_op jit(solution)/shard_map/ppermute | solution.py:368
  79.3 22.8 %collective-permute-start.8 = (bf16[128,3072]{1,0:T(8,128)(2,1)}, bf16[128,3072]{1,0:T(8,128)(2,1)}, u32[]{:S(2)}, u32[]{:S(2)}) collective-permute-start(bf16[128,3072]{1,0:T(8,128)(2,1)} %collective-permute-done.4.own.refs_10_), channel_id=1, source_target_pairs={{0,1},{1,2},{2,3},{3,0},{4,5},{5,6},{6,7},{7,4},{8,9},{9,10},{10,1... | collective-permute-start | bytes 2359304 | tf_op jit(solution)/shard_map/ppermute | solution.py:365
  89.5 23.9 %collective-permute-start.10 = (bf16[256,3072]{1,0:T(8,128)(2,1)}, bf16[256,3072]{1,0:T(8,128)(2,1)}, u32[]{:S(2)}, u32[]{:S(2)}) collective-permute-start(bf16[256,3072]{1,0:T(8,128)(2,1)} %get-tuple-element.93.refs_13_), channel_id=1, source_target_pairs={{0,8},{4,20},{8,0},{12,28},{16,24},{20,4},{24,16},{28,12},{1,9},{5... | collective-permute-start | bytes 4718600 | tf_op jit(solution)/shard_map/ppermute | solution.py:371
  102.0 3.3 %collective-permute-start.9 = (bf16[128,3072]{1,0:T(8,128)(2,1)}, bf16[128,3072]{1,0:T(8,128)(2,1)}, u32[]{:S(2)}, u32[]{:S(2)}) collective-permute-start(bf16[128,3072]{1,0:T(8,128)(2,1)} %collective-permute-done.8.own.refs_15_), channel_id=1, source_target_pairs={{0,4},{4,0},{8,12},{12,8},{16,20},{20,16},{24,28},{28,24},{1,5},{5... | collective-permute-start | bytes 2359304 | tf_op jit(solution)/shard_map/ppermute | solution.py:368
  103.1 21.6 %collective-permute-start.12 = (bf16[128,3072]{1,0:T(8,128)(2,1)}, bf16[128,3072]{1,0:T(8,128)(2,1)}, u32[]{:S(2)}, u32[]{:S(2)}) collective-permute-start(bf16[128,3072]{1,0:T(8,128)(2,1)} %bitcast.17), channel_id=1, source_target_pairs={{0,1},{1,2},{2,3},{3,0},{4,5},{5,6},{6,7},{7,4},{8,9},{9,10},{10,1... | collective-permute-start | bytes 2359304 | tf_op jit(solution)/shard_map/ppermute | solution.py:365
  104.6 32.1 %collective-permute-start.15 = (bf16[256,3072]{1,0:T(8,128)(2,1)}, bf16[256,3072]{1,0:T(8,128)(2,1)}, u32[]{:S(2)}, u32[]{:S(2)}) collective-permute-start(bf16[256,3072]{1,0:T(8,128)(2,1)} %shard_map.92.pre.refs_3_), channel_id=1, source_target_pairs={{0,8},{4,20},{8,0},{12,28},{16,24},{20,4},{24,16},{28,12},{1,9},{5... | collective-permute-start | bytes 4718600 | tf_op jit(solution)/shard_map/ppermute | solution.py:371
  124.7 2.6 collective-permute-start.14
  124.7 3.7 %collective-permute-start.11 = (bf16[128,3072]{1,0:T(8,128)(2,1)}, bf16[128,3072]{1,0:T(8,128)(2,1)}, u32[]{:S(2)}, u32[]{:S(2)}) collective-permute-start(bf16[128,3072]{1,0:T(8,128)(2,1)} %get-tuple-element.103), channel_id=1, source_target_pairs={{0,4},{4,0},{8,12},{12,8},{16,20},{20,16},{24,28},{28,24},{1,5},{5... | collective-permute-start | bytes 2359304 | tf_op jit(solution)/shard_map/ppermute | solution.py:368
  125.2 21.6 %collective-permute-start.13 = (bf16[128,3072]{1,0:T(8,128)(2,1)}, bf16[128,3072]{1,0:T(8,128)(2,1)}, u32[]{:S(2)}, u32[]{:S(2)}) collective-permute-start(bf16[128,3072]{1,0:T(8,128)(2,1)} %collective-permute-done.12.own.refs_5_), channel_id=1, source_target_pairs={{0,1},{1,2},{2,3},{3,0},{4,5},{5,6},{6,7},{7,4},{8,9},{9,10},{10,1... | collective-permute-start | bytes 2359304 | tf_op jit(solution)/shard_map/ppermute | solution.py:365
  125.2 25.3 %collective-permute-start.19 = (bf16[256,3072]{1,0:T(8,128)(2,1)}, bf16[256,3072]{1,0:T(8,128)(2,1)}, u32[]{:S(2)}, u32[]{:S(2)}) collective-permute-start(bf16[256,3072]{1,0:T(8,128)(2,1)} %get-tuple-element.100.refs_18_), channel_id=1, source_target_pairs={{0,8},{4,20},{8,0},{12,28},{16,24},{20,4},{24,16},{28,12},{1,9},{5... | collective-permute-start | bytes 4718600 | tf_op jit(solution)/shard_map/ppermute | solution.py:371
  136.2 29.6 %collective-permute-start.20 = (bf16[256,3072]{1,0:T(8,128)(2,1)}, bf16[256,3072]{1,0:T(8,128)(2,1)}, u32[]{:S(2)}, u32[]{:S(2)}) collective-permute-start(bf16[256,3072]{1,0:T(8,128)(2,1)} %shard_map.95.pre.refs_8_), channel_id=1, source_target_pairs={{0,8},{4,20},{8,0},{12,28},{16,24},{20,4},{24,16},{28,12},{1,9},{5... | collective-permute-start | bytes 4718600 | tf_op jit(solution)/shard_map/ppermute | solution.py:371
  146.8 2.6 collective-permute-start.18
  146.8 3.7 %collective-permute-start.17 = (bf16[128,3072]{1,0:T(8,128)(2,1)}, bf16[128,3072]{1,0:T(8,128)(2,1)}, u32[]{:S(2)}, u32[]{:S(2)}) collective-permute-start(bf16[128,3072]{1,0:T(8,128)(2,1)} %get-tuple-element.110), channel_id=1, source_target_pairs={{0,4},{4,0},{8,12},{12,8},{16,20},{20,16},{24,28},{28,24},{1,5},{5... | collective-permute-start | bytes 2359304 | tf_op jit(solution)/shard_map/ppermute | solution.py:368
  147.3 21.6 %collective-permute-start.16 = (bf16[128,3072]{1,0:T(8,128)(2,1)}, bf16[128,3072]{1,0:T(8,128)(2,1)}, u32[]{:S(2)}, u32[]{:S(2)}) collective-permute-start(bf16[128,3072]{1,0:T(8,128)(2,1)} %collective-permute-done.13.own.refs_10_), channel_id=1, source_target_pairs={{0,1},{1,2},{2,3},{3,0},{4,5},{5,6},{6,7},{7,4},{8,9},{9,10},{10,1... | collective-permute-start | bytes 2359304 | tf_op jit(solution)/shard_map/ppermute | solution.py:365
  158.3 21.3 %collective-permute-start.23 = (bf16[256,3072]{1,0:T(8,128)(2,1)}, bf16[256,3072]{1,0:T(8,128)(2,1)}, u32[]{:S(2)}, u32[]{:S(2)}) collective-permute-start(bf16[256,3072]{1,0:T(8,128)(2,1)} %shard_map.97.pre.refs_13_), channel_id=1, source_target_pairs={{0,8},{4,20},{8,0},{12,28},{16,24},{20,4},{24,16},{28,12},{1,9},{5... | collective-permute-start | bytes 4718600 | tf_op jit(solution)/shard_map/ppermute | solution.py:371
  168.8 2.6 collective-permute-start.21
  168.8 6.7 %collective-permute-start.22 = (bf16[128,3072]{1,0:T(8,128)(2,1)}, bf16[128,3072]{1,0:T(8,128)(2,1)}, u32[]{:S(2)}, u32[]{:S(2)}) collective-permute-start(bf16[128,3072]{1,0:T(8,128)(2,1)} %get-tuple-element.117), channel_id=1, source_target_pairs={{0,4},{4,0},{8,12},{12,8},{16,20},{20,16},{24,28},{28,24},{1,5},{5... | collective-permute-start | bytes 2359304 | tf_op jit(solution)/shard_map/ppermute | solution.py:368
  169.3 21.6 %collective-permute-start.25 = (bf16[128,3072]{1,0:T(8,128)(2,1)}, bf16[128,3072]{1,0:T(8,128)(2,1)}, u32[]{:S(2)}, u32[]{:S(2)}) collective-permute-start(bf16[128,3072]{1,0:T(8,128)(2,1)} %add_convert_fusion.7), channel_id=1, source_target_pairs={{0,1},{1,2},{2,3},{3,0},{4,5},{5,6},{6,7},{7,4},{8,9},{9,10},{10,1... | collective-permute-start | bytes 2359304 | tf_op jit(solution)/shard_map/ppermute | solution.py:365
  174.6 16.4 %collective-permute-start.24 = (bf16[256,1536]{1,0:T(8,128)(2,1)}, bf16[256,1536]{1,0:T(8,128)(2,1)}, u32[]{:S(2)}, u32[]{:S(2)}) collective-permute-start(bf16[256,1536]{1,0:T(8,128)(2,1)} %shard_map.99), channel_id=1, source_target_pairs={{0,8},{4,20},{8,0},{12,28},{16,24},{20,4},{24,16},{28,12},{1,9},{5... | collective-permute-start | bytes 2359304 | tf_op jit(solution)/shard_map/ppermute | solution.py:371
  187.0 15.9 %collective-permute-start.26 = (bf16[256,1536]{1,0:T(8,128)(2,1)}, bf16[256,1536]{1,0:T(8,128)(2,1)}, u32[]{:S(2)}, u32[]{:S(2)}) collective-permute-start(bf16[256,1536]{1,0:T(8,128)(2,1)} %shard_map.100.pre.refs_18_), channel_id=1, source_target_pairs={{0,8},{4,20},{8,0},{12,28},{16,24},{20,4},{24,16},{28,12},{1,9},{5... | collective-permute-start | bytes 2359304 | tf_op jit(solution)/shard_map/ppermute | solution.py:371
  201.9 16.6 %collective-permute-start.28 = (bf16[384,1536]{1,0:T(8,128)(2,1)}, bf16[384,1536]{1,0:T(8,128)(2,1)}, u32[]{:S(2)}, u32[]{:S(2)}) collective-permute-start(bf16[384,1536]{1,0:T(8,128)(2,1)} %get-tuple-element.130), channel_id=1, source_target_pairs={{0,16},{4,12},{8,24},{12,4},{16,0},{20,28},{24,8},{28,20},{1,17},{... | collective-permute-start | bytes 3538952 | tf_op jit(solution)/shard_map/ppermute | solution.py:473
  212.7 28.8 %collective-permute-start.27 = (bf16[128,3072]{1,0:T(8,128)(2,1)}, bf16[128,3072]{1,0:T(8,128)(2,1)}, u32[]{:S(2)}, u32[]{:S(2)}) collective-permute-start(bf16[128,3072]{1,0:T(8,128)(2,1)} %get-tuple-element.135), channel_id=1, source_target_pairs={{0,4},{4,0},{8,12},{12,8},{16,20},{20,16},{24,28},{28,24},{1,5},{5... | collective-permute-start | bytes 2359304 | tf_op jit(solution)/shard_map/ppermute | solution.py:368
  212.7 29.9 %collective-permute-start.29 = (bf16[384,1536]{1,0:T(8,128)(2,1)}, bf16[384,1536]{1,0:T(8,128)(2,1)}, u32[]{:S(2)}, u32[]{:S(2)}) collective-permute-start(bf16[384,1536]{1,0:T(8,128)(2,1)} %get-tuple-element.142), channel_id=1, source_target_pairs={{0,20},{4,8},{8,28},{12,0},{16,4},{20,24},{24,12},{28,16},{1,21},{... | collective-permute-start | bytes 3538952 | tf_op jit(solution)/shard_map/ppermute | solution.py:473
  214.0 28.7 %collective-permute-start.30 = (bf16[128,3072]{1,0:T(8,128)(2,1)}, bf16[128,3072]{1,0:T(8,128)(2,1)}, u32[]{:S(2)}, u32[]{:S(2)}) collective-permute-start(bf16[128,3072]{1,0:T(8,128)(2,1)} %add_convert_fusion.6), channel_id=1, source_target_pairs={{0,1},{1,2},{2,3},{3,0},{4,5},{5,6},{6,7},{7,4},{8,9},{9,10},{10,1... | collective-permute-start | bytes 2359304 | tf_op jit(solution)/shard_map/ppermute | solution.py:365
  229.5 16.6 %collective-permute-start.31 = (bf16[384,1536]{1,0:T(8,128)(2,1)}, bf16[384,1536]{1,0:T(8,128)(2,1)}, u32[]{:S(2)}, u32[]{:S(2)}) collective-permute-start(bf16[384,1536]{1,0:T(8,128)(2,1)} %get-tuple-element.138), channel_id=1, source_target_pairs={{0,16},{4,12},{8,24},{12,4},{16,0},{20,28},{24,8},{28,20},{1,17},{... | collective-permute-start | bytes 3538952 | tf_op jit(solution)/shard_map/ppermute | solution.py:473
  230.5 26.7 %collective-permute-start.32 = (bf16[384,1536]{1,0:T(8,128)(2,1)}, bf16[384,1536]{1,0:T(8,128)(2,1)}, u32[]{:S(2)}, u32[]{:S(2)}) collective-permute-start(bf16[384,1536]{1,0:T(8,128)(2,1)} %get-tuple-element.148), channel_id=1, source_target_pairs={{0,20},{4,8},{8,28},{12,0},{16,4},{20,24},{24,12},{28,16},{1,21},{... | collective-permute-start | bytes 3538952 | tf_op jit(solution)/shard_map/ppermute | solution.py:473
  241.5 17.3 %collective-permute-start.33 = (bf16[384,1536]{1,0:T(8,128)(2,1)}, bf16[384,1536]{1,0:T(8,128)(2,1)}, u32[]{:S(2)}, u32[]{:S(2)}) collective-permute-start(bf16[384,1536]{1,0:T(8,128)(2,1)} %get-tuple-element.150), channel_id=1, source_target_pairs={{0,4},{4,0},{8,12},{12,8},{16,20},{20,16},{24,28},{28,24},{1,5},{5... | collective-permute-start | bytes 3538952 | tf_op jit(solution)/shard_map/ppermute | solution.py:368
  245.5 23.4 %collective-permute-start.35 = (bf16[128,3072]{1,0:T(8,128)(2,1)}, bf16[128,3072]{1,0:T(8,128)(2,1)}, u32[]{:S(2)}, u32[]{:S(2)}) collective-permute-start(bf16[128,3072]{1,0:T(8,128)(2,1)} %add_convert_fusion.5), channel_id=1, source_target_pairs={{0,1},{1,2},{2,3},{3,0},{4,5},{5,6},{6,7},{7,4},{8,9},{9,10},{10,1... | collective-permute-start | bytes 2359304 | tf_op jit(solution)/shard_map/ppermute | solution.py:365
  257.2 3.6 %copy-start = (bf16[384,1536]{1,0:T(8,128)(2,1)S(1)}, bf16[384,1536]{1,0:T(8,128)(2,1)}, u32[]{:S(2)}) copy-start(bf16[384,1536]{1,0:T(8,128)(2,1)} %get-tuple-element.149) | copy-start | bytes 3538948
  257.2 8.4 %collective-permute-start.34 = (bf16[384,1536]{1,0:T(8,128)(2,1)}, bf16[384,1536]{1,0:T(8,128)(2,1)S(1)}, u32[]{:S(2)}, u32[]{:S(2)}) collective-permute-start(bf16[384,1536]{1,0:T(8,128)(2,1)} %get-tuple-element.152), channel_id=1, source_target_pairs={{0,4},{4,0},{8,12},{12,8},{16,20},{20,16},{24,28},{28,24},{1,5},{5... | collective-permute-start | bytes 3538952 | tf_op jit(solution)/shard_map/ppermute | solution.py:368
  262.3 1.7 copy-start.1
  267.2 1.7 copy-start.2
where the time goes:
time: 272 us
  Pallas kernels  151 us (56%)
  waiting for transfers between devices  70.7 us (26%)
  starting transfers between devices  27.3 us (10%)
  other arithmetic  21.9 us (8%)
    pallas_call x8, Pallas kernels, forward(): pl.pallas_call(functools.partial(body, hidden=hidden, chips=chips), out_s...  63 us
    pallas_call x4, Pallas kernels, weight_part(): pl.pallas_call(functools.partial(weight_body, begins=[begin for _, begin...  44 us
    pallas_call x4, Pallas kernels, input_part(): pl.pallas_call(input_body, out_shape=(shape, shape), grid_spec=pltpu.Pref...  28 us
    ppermute x9, waiting for transfers between devices, onward(): return lax.ppermute(piece, 'tensor', ring)  26.7 us
    all_to_all x2, waiting for transfers between devices, exchange(): return lax.all_to_all(rows, 'dp', split_axis=0, concat_axis=0, tiled=True)  17.8 us
    convert_element_type x8, other arithmetic, add(): return sum((v.astype(F32) for v in values)).astype(BF16)  17.3 us
    ppermute x14, waiting for transfers between devices, sibling(): return lax.ppermute(piece, 'dp', to_sibling)  12.5 us
    all_to_all x2, starting transfers between devices, exchange(): return lax.all_to_all(rows, 'dp', split_axis=0, concat_axis=0, tiled=True)  9.47 us
  transfers between devices with their start and end apart: 38, of which 20 were waited for; matrix products, arithmetic and copies ran while one was open for 7% of the time, Pallas kernels for 53%

commit v1 on v0

--- a/solution.py
+++ b/solution.py
@@ -445,8 +445,10 @@
     columns = done(partner_columns(*after(g_own[end], g_sib[end]), info, chips))
     pools["columns"] = pooled(columns)
     g_there.append((pools["columns"], 0))
-    settle(("share", end - 1), ("g", end - 1))
+    settle(("share", end - 1))
     down(end, False)
+    settle(("g", end - 1))
+    share(end)
 
     span = d // dp
     near, mine_j = pool_bit(chip, core), other_bits(chip, core)
@@ -495,22 +497,18 @@
     last.append(running)
     down_parts = {r: part(r, *down_sum) for r in away}
     down_sent = pass_on(down_parts)
-    settle(("g", end))
     for s in range(2, end):
         running = onward(done(add(*after(*shares[s]), running)))
-    share(end)
-    last.append(down_sent[0])
+    settle(("g", end))
     up_parts = {r: part(r, *up_sum) for r in away}
     up_sent = pass_on(up_parts)
     down_kept = part(0, *down_sum)
-    last.append(down_sent[1])
     running = onward(done(add(*after(*shares[end]), running)))
-    last.append(up_sent[0])
+    last.extend(down_sent)
     up_kept = part(0, *up_sum)
-    last.append(up_sent[1])
     down_grad = finished(down_kept, down_parts, down_sent)
+    input_grad = done(add(*after(*shares[0]), running)).reshape(OWNB, here, d)
     up_grad = finished(up_kept, up_parts, up_sent)
-    input_grad = add(*after(*shares[0]), running).reshape(OWNB, here, d)
     return input_grad, up_grad, down_grad
 
 

time: 272 us -> 265 us (0.974)
  waiting for transfers between devices: 70.7 us -> 63.4 us
    ppermute x4, waiting for transfers between devices: 5.22 us -> 0.01 us  [pass_on(): lax.ppermute(p, 'dp', chip_perm(dp, flip, h == 1))]
    ppermute x9, waiting for transfers between devices: 8.47 us -> 4.34 us  [pooled(): return lax.ppermute(piece, 'dp', to_pool)]
  transfers between devices with their start and end apart: 38 -> 38, of which waited for: 20 -> 16; matrix products, arithmetic and copies ran while one was open for 7% -> 7% of each run, Pallas kernels for 53% -> 55%
where the time goes in v1:
time: 265 us; the launch traced here: 264 us
  Pallas kernels  151 us (57%)
  waiting for transfers between devices  63.4 us (24%)
  starting transfers between devices  26.3 us (10%)
  other arithmetic  22.4 us (8%)
    pallas_call x8, Pallas kernels, forward(): pl.pallas_call(functools.partial(body, hidden=hidden, chips=chips), out_s...  63 us
    pallas_call x4, Pallas kernels, weight_part(): pl.pallas_call(functools.partial(weight_body, begins=[begin for _, begin...  44.1 us
    ppermute x9, waiting for transfers between devices, onward(): return lax.ppermute(piece, 'tensor', ring)  28.8 us
    pallas_call x4, Pallas kernels, input_part(): pl.pallas_call(input_body, out_shape=(shape, shape), grid_spec=pltpu.Pref...  27.9 us
    all_to_all x2, waiting for transfers between devices, exchange(): return lax.all_to_all(rows, 'dp', split_axis=0, concat_axis=0, tiled=True)  17.8 us
    convert_element_type x8, other arithmetic, add(): return sum((v.astype(F32) for v in values)).astype(BF16)  17.7 us
    ppermute x14, waiting for transfers between devices, sibling(): return lax.ppermute(piece, 'dp', to_sibling)  12.5 us
    all_to_all x2, starting transfers between devices, exchange(): return lax.all_to_all(rows, 'dp', split_axis=0, concat_axis=0, tiled=True)  9.48 us
  transfers between devices with their start and end apart: 38, of which 16 were waited for; matrix products, arithmetic and copies ran while one was open for 7% of the time, Pallas kernels for 55%

profile of v1, /device:TPU:0, one launch (start us, length us, event | category | flops | bytes accessed | tf_op | source)
XLA Modules:
  0.0 263.9 jit_solution(10958941699694164965)
XLA Ops:
  1.2 3.4 %shard_map.85 = bf16[8,32,3072]{2,1,0:T(8,128)(2,1)} custom-call(s32[2]{0:T(128)} %pad_add_fusion.info, s32[8]{0:T(128)} %count.7, bf16[8,32,3072]{2,1,0:T(8,128)(2,1)} %rows.1), custom_call_target="tpu_custom_call" | custom-call | flops 1 | bytes 1 | tf_op jit(solution)/shard_map/pallas_call | solution.py:67
  4.6 5.2 %all-to-all-start = ((bf16[8,32,3072]{2,1,0:T(8,128)(2,1)}), bf16[8,32,3072]{2,1,0:T(8,128)(2,1)}, u32[]{:S(2)}, u32[]{:S(2)}) async-start(bf16[8,32,3072]{2,1,0:T(8,128)(2,1)} %shard_map.85), calls=%async_computation | async-start | bytes 3145728 | tf_op jit(solution)/shard_map/all_to_all | solution.py:374
  9.8 3.4 %shard_map.86 = bf16[8,32,3072]{2,1,0:T(8,128)(2,1)} custom-call(s32[2]{0:T(128)} %pad_add_fusion.info, s32[8]{0:T(128)} %count.7, bf16[8,32,3072]{2,1,0:T(8,128)(2,1)} %rows.2), custom_call_target="tpu_custom_call" | custom-call | flops 1 | bytes 1 | tf_op jit(solution)/shard_map/pallas_call | solution.py:67
  13.1 17.8 %all-to-all-done.arrived = bf16[8,32,3072]{2,1,0:T(8,128)(2,1)} async-done(((bf16[8,32,3072]{2,1,0:T(8,128)(2,1)}), bf16[8,32,3072]{2,1,0:T(8,128)(2,1)}, u32[]{:S(2)}, u32[]{:S(2)}) %all-to-all-start) | async-done | bytes 1572896 | tf_op jit(solution)/shard_map/all_to_all | solution.py:374
  30.9 3.1 %shard_map.87 = bf16[4,32,3072]{2,1,0:T(8,128)(2,1)} custom-call(s32[2]{0:T(128)} %pad_add_fusion.info, s32[8]{0:T(128)} %count.7, s32[8,8]{1,0:T(8,128)} %patches.3, bf16[8,32,3072]{2,1,0:T(8,128)(2,1)} %all-to-all-done.arrived), custom_call_target="tpu_custom_call" | custom-call | flops 1 | bytes 1 | tf_op jit(solution)/shard_map/pallas_call | solution.py:98
  34.0 2.1 collective-permute-start
  36.2 4.3 %all-to-all-start.1 = ((bf16[8,32,3072]{2,1,0:T(8,128)(2,1)}), bf16[8,32,3072]{2,1,0:T(8,128)(2,1)}, u32[]{:S(2)}, u32[]{:S(2)}) async-start(bf16[8,32,3072]{2,1,0:T(8,128)(2,1)} %shard_map.86), calls=%async_computation.1 | async-start | bytes 3145728 | tf_op jit(solution)/shard_map/all_to_all | solution.py:374
  40.5 8.1 %shard_map.88 = (bf16[256,3072]{1,0:T(8,128)(2,1)}, bf16[256,1536]{1,0:T(8,128)(2,1)}) custom-call(s32[2]{0:T(128)} %pad_add_fusion.info, bf16[128,3072]{1,0:T(8,128)(2,1)} %bitcast.12, bf16[128,3072]{1,0:T(8,128)(2,1)} %collective-permute-done.1.sib.refs_1_, bf16[3072,3072]{1,0:T(8,128)(2,1)} %w.23), custom_call_target="tpu_custom_call" | custom-call | flops 1 | bytes 1 | tf_op jit(solution)/shard_map/pallas_call | solution.py:209
  48.6 8.1 %collective-permute-done.own.refs_5_ = bf16[128,3072]{1,0:T(8,128)(2,1)} collective-permute-done((bf16[128,3072]{1,0:T(8,128)(2,1)}, bf16[128,3072]{1,0:T(8,128)(2,1)}, u32[]{:S(2)}, u32[]{:S(2)}) %collective-permute-start) | collective-permute-done | bytes 786464 | tf_op jit(solution)/shard_map/ppermute | solution.py:365
  57.2 2.1 collective-permute-done.2.sib.refs_6_
  59.3 8.1 %shard_map.89 = (bf16[256,3072]{1,0:T(8,128)(2,1)}, bf16[256,1536]{1,0:T(8,128)(2,1)}) custom-call(s32[2]{0:T(128)} %pad_add_fusion.info, bf16[128,3072]{1,0:T(8,128)(2,1)} %collective-permute-done.own.refs_5_, bf16[128,3072]{1,0:T(8,128)(2,1)} %collective-permute-done.2.sib.refs_6_, bf16[3072,3072]{1,0:T(8,128)(2,1)} %w.23), custom_call_target="tpu_custom_call" | custom-call | flops 1 | bytes 1 | tf_op jit(solution)/shard_map/pallas_call | solution.py:209
  67.9 3.0 %shard_map.90 = bf16[4,32,3072]{2,1,0:T(8,128)(2,1)} custom-call(s32[2]{0:T(128)} %pad_add_fusion.info, s32[8]{0:T(128)} %count.7, s32[8,8]{1,0:T(8,128)} %patches.3, bf16[8,32,3072]{2,1,0:T(8,128)(2,1)} %all-to-all-done.1.arrived), custom_call_target="tpu_custom_call" | custom-call | flops 1 | bytes 1 | tf_op jit(solution)/shard_map/pallas_call | solution.py:98
  70.9 7.8 %collective-permute-done.4.own.refs_10_ = bf16[128,3072]{1,0:T(8,128)(2,1)} collective-permute-done((bf16[128,3072]{1,0:T(8,128)(2,1)}, bf16[128,3072]{1,0:T(8,128)(2,1)}, u32[]{:S(2)}, u32[]{:S(2)}) %collective-permute-start.4) | collective-permute-done | bytes 786464 | tf_op jit(solution)/shard_map/ppermute | solution.py:365
  79.2 2.1 collective-permute-done.5.sib.refs_11_
  81.3 8.1 %shard_map.91 = (bf16[256,3072]{1,0:T(8,128)(2,1)}, bf16[256,1536]{1,0:T(8,128)(2,1)}) custom-call(s32[2]{0:T(128)} %pad_add_fusion.info, bf16[128,3072]{1,0:T(8,128)(2,1)} %collective-permute-done.4.own.refs_10_, bf16[128,3072]{1,0:T(8,128)(2,1)} %collective-permute-done.5.sib.refs_11_, bf16[3072,3072]{1,0:T(8,128)(2,1)} %w.23), custom_call_target="tpu_custom_call" | custom-call | flops 1 | bytes 1 | tf_op jit(solution)/shard_map/pallas_call | solution.py:209
  90.0 4.3 %collective-permute-done.7.refs_9_.refs_7_ = bf16[256,3072]{1,0:T(8,128)(2,1)} collective-permute-done((bf16[256,3072]{1,0:T(8,128)(2,1)}, bf16[256,3072]{1,0:T(8,128)(2,1)}, u32[]{:S(2)}, u32[]{:S(2)}) %collective-permute-start.7) | collective-permute-done | bytes 1572896 | tf_op jit(solution)/shard_map/ppermute | solution.py:371
  94.3 7.7 %shard_map.92.pre.refs_3_ = bf16[256,3072]{1,0:T(8,128)(2,1)} custom-call(s32[2]{0:T(128)} %pad_add_fusion.info, bf16[128,3072]{1,0:T(8,128)(2,1)} %bitcast.16, bf16[128,3072]{1,0:T(8,128)(2,1)} %collective-permute-done.3.sib.refs_1_, bf16[3072,3072]{1,0:T(8,128)(2,1)} %w.22, bf16[256,1536]{1,0:T(8,128)(2,1)} %get-tuple-element.96.slope), custom_call_target="tpu_custom_call" | custom-call | flops 1 | bytes 1 | tf_op jit(solution)/shard_map/pallas_call | solution.py:209
  103.0 1.6 collective-permute-start.12
  105.3 8.0 %shard_map.93 = (bf16[256,3072]{1,0:T(8,128)(2,1)}, bf16[256,1536]{1,0:T(8,128)(2,1)}) custom-call(s32[2]{0:T(128)} %pad_add_fusion.info, bf16[128,3072]{1,0:T(8,128)(2,1)} %collective-permute-done.8.own.refs_15_, bf16[128,3072]{1,0:T(8,128)(2,1)} %collective-permute-done.9.sib.refs_16_, bf16[3072,3072]{1,0:T(8,128)(2,1)} %w.23), custom_call_target="tpu_custom_call" | custom-call | flops 1 | bytes 1 | tf_op jit(solution)/shard_map/pallas_call | solution.py:209
  113.3 7.0 %shard_map.94 = (bf16[128,3072]{1,0:T(8,128)(2,1)}, bf16[128,3072]{1,0:T(8,128)(2,1)}) custom-call(s32[2]{0:T(128)} %pad_add_fusion.info, bf16[256,3072]{1,0:T(8,128)(2,1)} %shard_map.92.pre.refs_3_, bf16[3072,3072]{1,0:T(8,128)(2,1)} %w.23), custom_call_target="tpu_custom_call" | custom-call | flops 1 | bytes 1 | tf_op jit(solution)/shard_map/pallas_call | solution.py:237
  120.3 4.4 %collective-permute-done.12.own.refs_5_ = bf16[128,3072]{1,0:T(8,128)(2,1)} collective-permute-done((bf16[128,3072]{1,0:T(8,128)(2,1)}, bf16[128,3072]{1,0:T(8,128)(2,1)}, u32[]{:S(2)}, u32[]{:S(2)}) %collective-permute-start.12) | collective-permute-done | bytes 786464 | tf_op jit(solution)/shard_map/ppermute | solution.py:365
  125.7 1.6 collective-permute-done.14.sib.refs_6_
  128.4 7.7 %shard_map.95.pre.refs_8_ = bf16[256,3072]{1,0:T(8,128)(2,1)} custom-call(s32[2]{0:T(128)} %pad_add_fusion.info, bf16[128,3072]{1,0:T(8,128)(2,1)} %collective-permute-done.12.own.refs_5_, bf16[128,3072]{1,0:T(8,128)(2,1)} %collective-permute-done.14.sib.refs_6_, bf16[3072,3072]{1,0:T(8,128)(2,1)} %w.22, bf16[256,1536]{1,0:T(8,128)(2,1)} %get-tuple-element.108.slope), custom_call_target="tpu_custom_call" | custom-call | flops 1 | bytes 1 | tf_op jit(solution)/shard_map/pallas_call | solution.py:209
  136.6 7.0 %shard_map.96 = (bf16[128,3072]{1,0:T(8,128)(2,1)}, bf16[128,3072]{1,0:T(8,128)(2,1)}) custom-call(s32[2]{0:T(128)} %pad_add_fusion.info, bf16[256,3072]{1,0:T(8,128)(2,1)} %shard_map.95.pre.refs_8_, bf16[3072,3072]{1,0:T(8,128)(2,1)} %w.23), custom_call_target="tpu_custom_call" | custom-call | flops 1 | bytes 1 | tf_op jit(solution)/shard_map/pallas_call | solution.py:237
  143.6 3.1 %collective-permute-done.13.own.refs_10_ = bf16[128,3072]{1,0:T(8,128)(2,1)} collective-permute-done((bf16[128,3072]{1,0:T(8,128)(2,1)}, bf16[128,3072]{1,0:T(8,128)(2,1)}, u32[]{:S(2)}, u32[]{:S(2)}) %collective-permute-start.13) | collective-permute-done | bytes 786464 | tf_op jit(solution)/shard_map/ppermute | solution.py:365
  147.3 2.1 collective-permute-done.16.sib.refs_11_
  150.5 7.8 %shard_map.97.pre.refs_13_ = bf16[256,3072]{1,0:T(8,128)(2,1)} custom-call(s32[2]{0:T(128)} %pad_add_fusion.info, bf16[128,3072]{1,0:T(8,128)(2,1)} %collective-permute-done.13.own.refs_10_, bf16[128,3072]{1,0:T(8,128)(2,1)} %collective-permute-done.16.sib.refs_11_, bf16[3072,3072]{1,0:T(8,128)(2,1)} %w.22, bf16[256,1536]{1,0:T(8,128)(2,1)} %get-tuple-element.114.slope), custom_call_target="tpu_custom_call" | custom-call | flops 1 | bytes 1 | tf_op jit(solution)/shard_map/pallas_call | solution.py:209
  158.8 7.0 %shard_map.98 = (bf16[128,3072]{1,0:T(8,128)(2,1)}, bf16[128,3072]{1,0:T(8,128)(2,1)}) custom-call(s32[2]{0:T(128)} %pad_add_fusion.info, bf16[256,3072]{1,0:T(8,128)(2,1)} %shard_map.97.pre.refs_13_, bf16[3072,3072]{1,0:T(8,128)(2,1)} %w.23), custom_call_target="tpu_custom_call" | custom-call | flops 1 | bytes 1 | tf_op jit(solution)/shard_map/pallas_call | solution.py:237
  165.8 2.5 add_convert_fusion.7
  169.3 2.1 collective-permute-done.22.sib.refs_16_
  171.4 3.1 %shard_map.99 = bf16[256,1536]{1,0:T(8,128)(2,1)} custom-call(s32[2]{0:T(128)} %pad_add_fusion.info, bf16[128,3072]{1,0:T(8,128)(2,1)} %collective-permute-done.20.own.refs_15_, bf16[128,3072]{1,0:T(8,128)(2,1)} %collective-permute-done.22.sib.refs_16_), custom_call_target="tpu_custom_call" | custom-call | flops 1 | bytes 1 | tf_op jit(solution)/shard_map/pallas_call | solution.py:173
  176.2 7.4 %shard_map.100.pre.refs_18_ = bf16[256,1536]{1,0:T(8,128)(2,1)} custom-call(s32[2]{0:T(128)} %pad_add_fusion.info, bf16[128,3072]{1,0:T(8,128)(2,1)} %collective-permute-done.20.own.refs_15_, bf16[128,3072]{1,0:T(8,128)(2,1)} %collective-permute-done.22.sib.refs_16_, bf16[3072,3072]{1,0:T(8,128)(2,1)} %w.22, bf16[256,1536]{1,0:T(8,128)(2,1)} %get-tuple-element.126.slope), custom_call_target="tpu_custom_call" | custom-call | flops 1 | bytes 1 | tf_op jit(solution)/shard_map/pallas_call | solution.py:209
  184.7 7.0 %shard_map.101 = (bf16[128,3072]{1,0:T(8,128)(2,1)}, bf16[128,3072]{1,0:T(8,128)(2,1)}) custom-call(s32[2]{0:T(128)} %pad_add_fusion.info, bf16[256,1536]{1,0:T(8,128)(2,1)} %shard_map.100.pre.refs_18_, bf16[3072,3072]{1,0:T(8,128)(2,1)} %w.23), custom_call_target="tpu_custom_call" | custom-call | flops 1 | bytes 1 | tf_op jit(solution)/shard_map/pallas_call | solution.py:237
  191.7 11.1 %shard_map.102 = (bf16[384,1536]{1,0:T(8,128)(2,1)}, bf16[384,1536]{1,0:T(8,128)(2,1)}) custom-call(s32[3]{0:T(128)} %get-tuple-element.156.at, bf16[128,3072]{1,0:T(8,128)(2,1)} %bitcast.18, bf16[128,3072]{1,0:T(8,128)(2,1)} %collective-permute-done.3.sib.refs_1_, bf16[256,3072]{1,0:T(8,128)(2,1)} %collective-permute-done.15.refs_2_.refs_4_, ...), custom_call_target="tpu_custom_call" | custom-call | flops 1 | bytes 1 | tf_op jit(solution)/shard_map/pallas_call | solution.py:318
  202.8 2.9 %add_convert_fusion.6 = bf16[128,3072]{1,0:T(8,128)(2,1)} fusion(bf16[128,3072]{1,0:T(8,128)(2,1)} %collective-permute-done.25, bf16[128,3072]{1,0:T(8,128)(2,1)} %collective-permute-done.19, bf16[128,3072]{1,0:T(8,128)(2,1)} %get-tuple-element.133), kind=kLoop, calls=%fused_computation.8 | loop fusion | flops 2359296 | bytes 3145728 | tf_op jit(solution)/shard_map/convert_element_type | solution.py:340
  207.8 11.0 %shard_map.103 = (bf16[384,1536]{1,0:T(8,128)(2,1)}, bf16[384,1536]{1,0:T(8,128)(2,1)}) custom-call(s32[3]{0:T(128)} %get-tuple-element.156.at, bf16[128,3072]{1,0:T(8,128)(2,1)} %bitcast.13, bf16[128,3072]{1,0:T(8,128)(2,1)} %collective-permute-done.1.sib.refs_1_, bf16[256,3072]{1,0:T(8,128)(2,1)} %collective-permute-done.6.refs_4_.refs_2_, ...), custom_call_target="tpu_custom_call" | custom-call | flops 1 | bytes 1 | tf_op jit(solution)/shard_map/pallas_call | solution.py:318
  219.7 11.0 %shard_map.104 = (bf16[384,1536]{1,0:T(8,128)(2,1)}, bf16[384,1536]{1,0:T(8,128)(2,1)}) custom-call(s32[3]{0:T(128)} %get-tuple-element.155.at, bf16[128,3072]{1,0:T(8,128)(2,1)} %bitcast.19, bf16[128,3072]{1,0:T(8,128)(2,1)} %collective-permute-done.3.sib.refs_1_, bf16[256,3072]{1,0:T(8,128)(2,1)} %collective-permute-done.15.refs_2_.refs_4_, ...), custom_call_target="tpu_custom_call" | custom-call | flops 1 | bytes 1 | tf_op jit(solution)/shard_map/pallas_call | solution.py:318
  230.8 1.2 collective-permute-start.35
  232.1 2.8 %add_convert_fusion.5 = bf16[128,3072]{1,0:T(8,128)(2,1)} fusion(bf16[128,3072]{1,0:T(8,128)(2,1)} %collective-permute-done.28, bf16[128,3072]{1,0:T(8,128)(2,1)} %collective-permute-done.27, bf16[128,3072]{1,0:T(8,128)(2,1)} %get-tuple-element.142), kind=kLoop, calls=%fused_computation.7 | loop fusion | flops 2359296 | bytes 3145728 | tf_op jit(solution)/shard_map/convert_element_type | solution.py:340
  234.9 11.0 %shard_map.105 = (bf16[384,1536]{1,0:T(8,128)(2,1)}, bf16[384,1536]{1,0:T(8,128)(2,1)}) custom-call(s32[3]{0:T(128)} %get-tuple-element.155.at, bf16[128,3072]{1,0:T(8,128)(2,1)} %bitcast.14, bf16[128,3072]{1,0:T(8,128)(2,1)} %collective-permute-done.1.sib.refs_1_, bf16[256,3072]{1,0:T(8,128)(2,1)} %collective-permute-done.6.refs_4_.refs_2_, ...), custom_call_target="tpu_custom_call" | custom-call | flops 1 | bytes 1 | tf_op jit(solution)/shard_map/pallas_call | solution.py:318
  246.0 1.9 add_convert_fusion.3
  247.9 1.9 add_convert_fusion.2
  249.8 1.7 maximum_select_fusion
  251.5 4.9 %collective-permute-done.32 = bf16[128,3072]{1,0:T(8,128)(2,1)} collective-permute-done((bf16[128,3072]{1,0:T(8,128)(2,1)}, bf16[128,3072]{1,0:T(8,128)(2,1)}, u32[]{:S(2)}, u32[]{:S(2)}) %collective-permute-start.32) | collective-permute-done | bytes 786464 | tf_op jit(solution)/shard_map/ppermute | solution.py:365
  256.4 2.6 add_convert_fusion.4
  259.0 1.6 add_convert_fusion.1
  260.6 1.6 add_convert_fusion
  262.2 1.7 maximum_select_fusion.1
  (65 shorter events, 16.2 us)
Async XLA Ops:
  4.6 26.3 %all-to-all-start = ((bf16[8,32,3072]{2,1,0:T(8,128)(2,1)}), bf16[8,32,3072]{2,1,0:T(8,128)(2,1)}, u32[]{:S(2)}, u32[]{:S(2)}) async-start(bf16[8,32,3072]{2,1,0:T(8,128)(2,1)} %shard_map.85), calls=%async_computation | async-start | bytes 3145728 | tf_op jit(solution)/shard_map/all_to_all | solution.py:374
  34.0 6.5 %collective-permute-start.1 = (bf16[128,3072]{1,0:T(8,128)(2,1)}, bf16[128,3072]{1,0:T(8,128)(2,1)}, u32[]{:S(2)}, u32[]{:S(2)}) collective-permute-start(bf16[128,3072]{1,0:T(8,128)(2,1)} %bitcast.10), channel_id=1, source_target_pairs={{0,4},{4,0},{8,12},{12,8},{16,20},{20,16},{24,28},{28,24},{1,5},{5... | collective-permute-start | bytes 2359304 | tf_op jit(solution)/shard_map/ppermute | solution.py:368
  34.0 22.6 %collective-permute-start = (bf16[128,3072]{1,0:T(8,128)(2,1)}, bf16[128,3072]{1,0:T(8,128)(2,1)}, u32[]{:S(2)}, u32[]{:S(2)}) collective-permute-start(bf16[128,3072]{1,0:T(8,128)(2,1)} %bitcast.11), channel_id=1, source_target_pairs={{0,1},{1,2},{2,3},{3,0},{4,5},{5,6},{6,7},{7,4},{8,9},{9,10},{10,1... | collective-permute-start | bytes 2359304 | tf_op jit(solution)/shard_map/ppermute | solution.py:365
  36.2 31.7 %all-to-all-start.1 = ((bf16[8,32,3072]{2,1,0:T(8,128)(2,1)}), bf16[8,32,3072]{2,1,0:T(8,128)(2,1)}, u32[]{:S(2)}, u32[]{:S(2)}) async-start(bf16[8,32,3072]{2,1,0:T(8,128)(2,1)} %shard_map.86), calls=%async_computation.1 | async-start | bytes 3145728 | tf_op jit(solution)/shard_map/all_to_all | solution.py:374
  56.6 2.6 collective-permute-start.2
  56.7 22.1 %collective-permute-start.4 = (bf16[128,3072]{1,0:T(8,128)(2,1)}, bf16[128,3072]{1,0:T(8,128)(2,1)}, u32[]{:S(2)}, u32[]{:S(2)}) collective-permute-start(bf16[128,3072]{1,0:T(8,128)(2,1)} %collective-permute-done.own.refs_5_), channel_id=1, source_target_pairs={{0,1},{1,2},{2,3},{3,0},{4,5},{5,6},{6,7},{7,4},{8,9},{9,10},{10,1... | collective-permute-start | bytes 2359304 | tf_op jit(solution)/shard_map/ppermute | solution.py:365
  56.7 22.6 %collective-permute-start.6 = (bf16[256,3072]{1,0:T(8,128)(2,1)}, bf16[256,3072]{1,0:T(8,128)(2,1)}, u32[]{:S(2)}, u32[]{:S(2)}) collective-permute-start(bf16[256,3072]{1,0:T(8,128)(2,1)} %get-tuple-element.84.refs_3_), channel_id=1, source_target_pairs={{0,8},{4,20},{8,0},{12,28},{16,24},{20,4},{24,16},{28,12},{1,9},{5... | collective-permute-start | bytes 4718600 | tf_op jit(solution)/shard_map/ppermute | solution.py:371
  67.4 26.9 %collective-permute-start.7 = (bf16[256,3072]{1,0:T(8,128)(2,1)}, bf16[256,3072]{1,0:T(8,128)(2,1)}, u32[]{:S(2)}, u32[]{:S(2)}) collective-permute-start(bf16[256,3072]{1,0:T(8,128)(2,1)} %get-tuple-element.88.refs_8_), channel_id=1, source_target_pairs={{0,8},{4,20},{8,0},{12,28},{16,24},{20,4},{24,16},{28,12},{1,9},{5... | collective-permute-start | bytes 4718600 | tf_op jit(solution)/shard_map/ppermute | solution.py:371
  78.7 2.6 collective-permute-start.5
  78.7 11.2 %collective-permute-start.3 = (bf16[128,3072]{1,0:T(8,128)(2,1)}, bf16[128,3072]{1,0:T(8,128)(2,1)}, u32[]{:S(2)}, u32[]{:S(2)}) collective-permute-start(bf16[128,3072]{1,0:T(8,128)(2,1)} %bitcast.15), channel_id=1, source_target_pairs={{0,4},{4,0},{8,12},{12,8},{16,20},{20,16},{24,28},{28,24},{1,5},{5... | collective-permute-start | bytes 2359304 | tf_op jit(solution)/shard_map/ppermute | solution.py:368
  79.2 22.8 %collective-permute-start.8 = (bf16[128,3072]{1,0:T(8,128)(2,1)}, bf16[128,3072]{1,0:T(8,128)(2,1)}, u32[]{:S(2)}, u32[]{:S(2)}) collective-permute-start(bf16[128,3072]{1,0:T(8,128)(2,1)} %collective-permute-done.4.own.refs_10_), channel_id=1, source_target_pairs={{0,1},{1,2},{2,3},{3,0},{4,5},{5,6},{6,7},{7,4},{8,9},{9,10},{10,1... | collective-permute-start | bytes 2359304 | tf_op jit(solution)/shard_map/ppermute | solution.py:365
  89.5 23.9 %collective-permute-start.10 = (bf16[256,3072]{1,0:T(8,128)(2,1)}, bf16[256,3072]{1,0:T(8,128)(2,1)}, u32[]{:S(2)}, u32[]{:S(2)}) collective-permute-start(bf16[256,3072]{1,0:T(8,128)(2,1)} %get-tuple-element.93.refs_13_), channel_id=1, source_target_pairs={{0,8},{4,20},{8,0},{12,28},{16,24},{20,4},{24,16},{28,12},{1,9},{5... | collective-permute-start | bytes 4718600 | tf_op jit(solution)/shard_map/ppermute | solution.py:371
  102.0 3.3 %collective-permute-start.9 = (bf16[128,3072]{1,0:T(8,128)(2,1)}, bf16[128,3072]{1,0:T(8,128)(2,1)}, u32[]{:S(2)}, u32[]{:S(2)}) collective-permute-start(bf16[128,3072]{1,0:T(8,128)(2,1)} %collective-permute-done.8.own.refs_15_), channel_id=1, source_target_pairs={{0,4},{4,0},{8,12},{12,8},{16,20},{20,16},{24,28},{28,24},{1,5},{5... | collective-permute-start | bytes 2359304 | tf_op jit(solution)/shard_map/ppermute | solution.py:368
  103.0 21.6 %collective-permute-start.12 = (bf16[128,3072]{1,0:T(8,128)(2,1)}, bf16[128,3072]{1,0:T(8,128)(2,1)}, u32[]{:S(2)}, u32[]{:S(2)}) collective-permute-start(bf16[128,3072]{1,0:T(8,128)(2,1)} %bitcast.17), channel_id=1, source_target_pairs={{0,1},{1,2},{2,3},{3,0},{4,5},{5,6},{6,7},{7,4},{8,9},{9,10},{10,1... | collective-permute-start | bytes 2359304 | tf_op jit(solution)/shard_map/ppermute | solution.py:365
  104.6 32.0 %collective-permute-start.15 = (bf16[256,3072]{1,0:T(8,128)(2,1)}, bf16[256,3072]{1,0:T(8,128)(2,1)}, u32[]{:S(2)}, u32[]{:S(2)}) collective-permute-start(bf16[256,3072]{1,0:T(8,128)(2,1)} %shard_map.92.pre.refs_3_), channel_id=1, source_target_pairs={{0,8},{4,20},{8,0},{12,28},{16,24},{20,4},{24,16},{28,12},{1,9},{5... | collective-permute-start | bytes 4718600 | tf_op jit(solution)/shard_map/ppermute | solution.py:371
  124.7 2.6 collective-permute-start.14
  124.7 3.7 %collective-permute-start.11 = (bf16[128,3072]{1,0:T(8,128)(2,1)}, bf16[128,3072]{1,0:T(8,128)(2,1)}, u32[]{:S(2)}, u32[]{:S(2)}) collective-permute-start(bf16[128,3072]{1,0:T(8,128)(2,1)} %get-tuple-element.103), channel_id=1, source_target_pairs={{0,4},{4,0},{8,12},{12,8},{16,20},{20,16},{24,28},{28,24},{1,5},{5... | collective-permute-start | bytes 2359304 | tf_op jit(solution)/shard_map/ppermute | solution.py:368
  125.2 21.6 %collective-permute-start.13 = (bf16[128,3072]{1,0:T(8,128)(2,1)}, bf16[128,3072]{1,0:T(8,128)(2,1)}, u32[]{:S(2)}, u32[]{:S(2)}) collective-permute-start(bf16[128,3072]{1,0:T(8,128)(2,1)} %collective-permute-done.12.own.refs_5_), channel_id=1, source_target_pairs={{0,1},{1,2},{2,3},{3,0},{4,5},{5,6},{6,7},{7,4},{8,9},{9,10},{10,1... | collective-permute-start | bytes 2359304 | tf_op jit(solution)/shard_map/ppermute | solution.py:365
  125.2 25.3 %collective-permute-start.18 = (bf16[256,3072]{1,0:T(8,128)(2,1)}, bf16[256,3072]{1,0:T(8,128)(2,1)}, u32[]{:S(2)}, u32[]{:S(2)}) collective-permute-start(bf16[256,3072]{1,0:T(8,128)(2,1)} %get-tuple-element.100.refs_18_), channel_id=1, source_target_pairs={{0,8},{4,20},{8,0},{12,28},{16,24},{20,4},{24,16},{28,12},{1,9},{5... | collective-permute-start | bytes 4718600 | tf_op jit(solution)/shard_map/ppermute | solution.py:371
  136.1 29.7 %collective-permute-start.21 = (bf16[256,3072]{1,0:T(8,128)(2,1)}, bf16[256,3072]{1,0:T(8,128)(2,1)}, u32[]{:S(2)}, u32[]{:S(2)}) collective-permute-start(bf16[256,3072]{1,0:T(8,128)(2,1)} %shard_map.95.pre.refs_8_), channel_id=1, source_target_pairs={{0,8},{4,20},{8,0},{12,28},{16,24},{20,4},{24,16},{28,12},{1,9},{5... | collective-permute-start | bytes 4718600 | tf_op jit(solution)/shard_map/ppermute | solution.py:371
  146.7 2.6 collective-permute-start.16
  146.7 3.7 %collective-permute-start.17 = (bf16[128,3072]{1,0:T(8,128)(2,1)}, bf16[128,3072]{1,0:T(8,128)(2,1)}, u32[]{:S(2)}, u32[]{:S(2)}) collective-permute-start(bf16[128,3072]{1,0:T(8,128)(2,1)} %get-tuple-element.110), channel_id=1, source_target_pairs={{0,4},{4,0},{8,12},{12,8},{16,20},{20,16},{24,28},{28,24},{1,5},{5... | collective-permute-start | bytes 2359304 | tf_op jit(solution)/shard_map/ppermute | solution.py:368
  147.2 21.6 %collective-permute-start.20 = (bf16[128,3072]{1,0:T(8,128)(2,1)}, bf16[128,3072]{1,0:T(8,128)(2,1)}, u32[]{:S(2)}, u32[]{:S(2)}) collective-permute-start(bf16[128,3072]{1,0:T(8,128)(2,1)} %collective-permute-done.13.own.refs_10_), channel_id=1, source_target_pairs={{0,1},{1,2},{2,3},{3,0},{4,5},{5,6},{6,7},{7,4},{8,9},{9,10},{10,1... | collective-permute-start | bytes 2359304 | tf_op jit(solution)/shard_map/ppermute | solution.py:365
  158.3 26.4 %collective-permute-start.23 = (bf16[256,3072]{1,0:T(8,128)(2,1)}, bf16[256,3072]{1,0:T(8,128)(2,1)}, u32[]{:S(2)}, u32[]{:S(2)}) collective-permute-start(bf16[256,3072]{1,0:T(8,128)(2,1)} %shard_map.97.pre.refs_13_), channel_id=1, source_target_pairs={{0,8},{4,20},{8,0},{12,28},{16,24},{20,4},{24,16},{28,12},{1,9},{5... | collective-permute-start | bytes 4718600 | tf_op jit(solution)/shard_map/ppermute | solution.py:371
  168.8 2.6 collective-permute-start.22
  168.8 7.4 %collective-permute-start.19 = (bf16[128,3072]{1,0:T(8,128)(2,1)}, bf16[128,3072]{1,0:T(8,128)(2,1)}, u32[]{:S(2)}, u32[]{:S(2)}) collective-permute-start(bf16[128,3072]{1,0:T(8,128)(2,1)} %get-tuple-element.117), channel_id=1, source_target_pairs={{0,4},{4,0},{8,12},{12,8},{16,20},{20,16},{24,28},{28,24},{1,5},{5... | collective-permute-start | bytes 2359304 | tf_op jit(solution)/shard_map/ppermute | solution.py:368
  169.3 22.3 %collective-permute-start.25 = (bf16[128,3072]{1,0:T(8,128)(2,1)}, bf16[128,3072]{1,0:T(8,128)(2,1)}, u32[]{:S(2)}, u32[]{:S(2)}) collective-permute-start(bf16[128,3072]{1,0:T(8,128)(2,1)} %add_convert_fusion.7), channel_id=1, source_target_pairs={{0,1},{1,2},{2,3},{3,0},{4,5},{5,6},{6,7},{7,4},{8,9},{9,10},{10,1... | collective-permute-start | bytes 2359304 | tf_op jit(solution)/shard_map/ppermute | solution.py:365
  174.5 17.1 %collective-permute-start.24 = (bf16[256,1536]{1,0:T(8,128)(2,1)}, bf16[256,1536]{1,0:T(8,128)(2,1)}, u32[]{:S(2)}, u32[]{:S(2)}) collective-permute-start(bf16[256,1536]{1,0:T(8,128)(2,1)} %shard_map.99), channel_id=1, source_target_pairs={{0,8},{4,20},{8,0},{12,28},{16,24},{20,4},{24,16},{28,12},{1,9},{5... | collective-permute-start | bytes 2359304 | tf_op jit(solution)/shard_map/ppermute | solution.py:371
  183.6 24.1 %collective-permute-start.26 = (bf16[256,1536]{1,0:T(8,128)(2,1)}, bf16[256,1536]{1,0:T(8,128)(2,1)}, u32[]{:S(2)}, u32[]{:S(2)}) collective-permute-start(bf16[256,1536]{1,0:T(8,128)(2,1)} %shard_map.100.pre.refs_18_), channel_id=1, source_target_pairs={{0,8},{4,20},{8,0},{12,28},{16,24},{20,4},{24,16},{28,12},{1,9},{5... | collective-permute-start | bytes 2359304 | tf_op jit(solution)/shard_map/ppermute | solution.py:371
  191.7 39.1 %collective-permute-start.27 = (bf16[128,3072]{1,0:T(8,128)(2,1)}, bf16[128,3072]{1,0:T(8,128)(2,1)}, u32[]{:S(2)}, u32[]{:S(2)}) collective-permute-start(bf16[128,3072]{1,0:T(8,128)(2,1)} %get-tuple-element.128), channel_id=1, source_target_pairs={{0,4},{4,0},{8,12},{12,8},{16,20},{20,16},{24,28},{28,24},{1,5},{5... | collective-permute-start | bytes 2359304 | tf_op jit(solution)/shard_map/ppermute | solution.py:368
  205.6 25.2 %collective-permute-start.28 = (bf16[128,3072]{1,0:T(8,128)(2,1)}, bf16[128,3072]{1,0:T(8,128)(2,1)}, u32[]{:S(2)}, u32[]{:S(2)}) collective-permute-start(bf16[128,3072]{1,0:T(8,128)(2,1)} %add_convert_fusion.6), channel_id=1, source_target_pairs={{0,1},{1,2},{2,3},{3,0},{4,5},{5,6},{6,7},{7,4},{8,9},{9,10},{10,1... | collective-permute-start | bytes 2359304 | tf_op jit(solution)/shard_map/ppermute | solution.py:365
  205.7 29.2 %collective-permute-start.30 = (bf16[384,1536]{1,0:T(8,128)(2,1)}, bf16[384,1536]{1,0:T(8,128)(2,1)}, u32[]{:S(2)}, u32[]{:S(2)}) collective-permute-start(bf16[384,1536]{1,0:T(8,128)(2,1)} %get-tuple-element.144), channel_id=1, source_target_pairs={{0,20},{4,8},{8,28},{12,0},{16,4},{20,24},{24,12},{28,16},{1,21},{... | collective-permute-start | bytes 3538952 | tf_op jit(solution)/shard_map/ppermute | solution.py:475
  206.7 28.2 %collective-permute-start.29 = (bf16[384,1536]{1,0:T(8,128)(2,1)}, bf16[384,1536]{1,0:T(8,128)(2,1)}, u32[]{:S(2)}, u32[]{:S(2)}) collective-permute-start(bf16[384,1536]{1,0:T(8,128)(2,1)} %get-tuple-element.132), channel_id=1, source_target_pairs={{0,16},{4,12},{8,24},{12,4},{16,0},{20,28},{24,8},{28,20},{1,17},{... | collective-permute-start | bytes 3538952 | tf_op jit(solution)/shard_map/ppermute | solution.py:475
  218.8 40.3 %collective-permute-start.33 = (bf16[384,1536]{1,0:T(8,128)(2,1)}, bf16[384,1536]{1,0:T(8,128)(2,1)}, u32[]{:S(2)}, u32[]{:S(2)}) collective-permute-start(bf16[384,1536]{1,0:T(8,128)(2,1)} %get-tuple-element.137), channel_id=1, source_target_pairs={{0,16},{4,12},{8,24},{12,4},{16,0},{20,28},{24,8},{28,20},{1,17},{... | collective-permute-start | bytes 3538952 | tf_op jit(solution)/shard_map/ppermute | solution.py:475
  230.8 17.2 %collective-permute-start.31 = (bf16[384,1536]{1,0:T(8,128)(2,1)}, bf16[384,1536]{1,0:T(8,128)(2,1)}, u32[]{:S(2)}, u32[]{:S(2)}) collective-permute-start(bf16[384,1536]{1,0:T(8,128)(2,1)} %get-tuple-element.149), channel_id=1, source_target_pairs={{0,4},{4,0},{8,12},{12,8},{16,20},{20,16},{24,28},{28,24},{1,5},{5... | collective-permute-start | bytes 3538952 | tf_op jit(solution)/shard_map/ppermute | solution.py:368
  230.8 29.7 %collective-permute-start.35 = (bf16[384,1536]{1,0:T(8,128)(2,1)}, bf16[384,1536]{1,0:T(8,128)(2,1)}, u32[]{:S(2)}, u32[]{:S(2)}) collective-permute-start(bf16[384,1536]{1,0:T(8,128)(2,1)} %get-tuple-element.154), channel_id=1, source_target_pairs={{0,20},{4,8},{8,28},{12,0},{16,4},{20,24},{24,12},{28,16},{1,21},{... | collective-permute-start | bytes 3538952 | tf_op jit(solution)/shard_map/ppermute | solution.py:475
  234.9 21.5 %collective-permute-start.32 = (bf16[128,3072]{1,0:T(8,128)(2,1)}, bf16[128,3072]{1,0:T(8,128)(2,1)}, u32[]{:S(2)}, u32[]{:S(2)}) collective-permute-start(bf16[128,3072]{1,0:T(8,128)(2,1)} %add_convert_fusion.5), channel_id=1, source_target_pairs={{0,1},{1,2},{2,3},{3,0},{4,5},{5,6},{6,7},{7,4},{8,9},{9,10},{10,1... | collective-permute-start | bytes 2359304 | tf_op jit(solution)/shard_map/ppermute | solution.py:365
  245.9 14.7 %collective-permute-start.34 = (bf16[384,1536]{1,0:T(8,128)(2,1)}, bf16[384,1536]{1,0:T(8,128)(2,1)S(1)}, u32[]{:S(2)}, u32[]{:S(2)}) collective-permute-start(bf16[384,1536]{1,0:T(8,128)(2,1)} %get-tuple-element.153), channel_id=1, source_target_pairs={{0,4},{4,0},{8,12},{12,8},{16,20},{20,16},{24,28},{28,24},{1,5},{5... | collective-permute-start | bytes 3538952 | tf_op jit(solution)/shard_map/ppermute | solution.py:368
  249.8 6.6 %copy-start.1 = (bf16[128,3072]{1,0:T(8,128)(2,1)S(1)}, bf16[128,3072]{1,0:T(8,128)(2,1)}, u32[]{:S(2)}) copy-start(bf16[128,3072]{1,0:T(8,128)(2,1)} %get-tuple-element.150) | copy-start | bytes 2359300
  251.5 7.5 %copy-start = (bf16[384,1536]{1,0:T(8,128)(2,1)S(1)}, bf16[384,1536]{1,0:T(8,128)(2,1)}, u32[]{:S(2)}) copy-start(bf16[384,1536]{1,0:T(8,128)(2,1)} %get-tuple-element.152) | copy-start | bytes 3538948

commit v2 on v1

--- a/solution.py
+++ b/solution.py
@@ -462,6 +462,18 @@
         done(parts[0])
         return list(parts)
 
+    def halves(r, rows, there, rights, split):
+        if span % 128:
+            return part(r, rows, there, rights, split)
+        j = mine_j ^ r
+        at = chip_with(j, near, core)
+        parts = []
+        for which in (core, 1 - core):
+            rows = [after(*rows[0]), *rows[1:]]
+            parts += weight_part(rows, there, rights, 2 * at + which, 2 * j + which, core, span, hidden, False)
+            done(parts[-1])
+        return parts
+
     bits = (chips // 2).bit_length() - 1
 
     def pass_on(parts):
@@ -495,7 +507,7 @@
     away = list(reversed(range(1, chips // 2)))
     settle("columns")
     last.append(running)
-    down_parts = {r: part(r, *down_sum) for r in away}
+    down_parts = {r: halves(r, *down_sum) for r in away}
     down_sent = pass_on(down_parts)
     for s in range(2, end):
         running = onward(done(add(*after(*shares[s]), running)))
@@ -503,12 +515,13 @@
     up_parts = {r: part(r, *up_sum) for r in away}
     up_sent = pass_on(up_parts)
     down_kept = part(0, *down_sum)
+    last.append(down_sent[0])
     running = onward(done(add(*after(*shares[end]), running)))
-    last.extend(down_sent)
+    last.append(down_sent[1])
     up_kept = part(0, *up_sum)
     down_grad = finished(down_kept, down_parts, down_sent)
+    up_grad = finished(up_kept, up_parts, up_sent)
     input_grad = done(add(*after(*shares[0]), running)).reshape(OWNB, here, d)
-    up_grad = finished(up_kept, up_parts, up_sent)
     return input_grad, up_grad, down_grad
 
 

time: 265 us -> 267 us (level)
  waiting for transfers between devices: 63.4 us -> 58.7 us
  Pallas kernels: 151 us -> 155 us
    ppermute x9, waiting for transfers between devices: 28.8 us -> 24 us  [onward(): return lax.ppermute(piece, 'tensor', ring)]
    pallas_call x4 -> x5, Pallas kernels: 44.1 us -> 48.4 us  [weight_part(): pl.pallas_call(functools.partial(weight_body, begins=[begin for _, begin...]
  transfers between devices with their start and end apart: 38 -> 38, of which waited for: 16 -> 16; matrix products, arithmetic and copies ran while one was open for 7% -> 8% of each run, Pallas kernels for 55% -> 56%
where the time goes in v2:
time: 267 us; the launch traced here: 265 us
  Pallas kernels  155 us (58%)
  waiting for transfers between devices  58.7 us (22%)
  starting transfers between devices  26.2 us (10%)
  other arithmetic  24.2 us (9%)
    pallas_call x8, Pallas kernels, forward(): pl.pallas_call(functools.partial(body, hidden=hidden, chips=chips), out_s...  63 us
    pallas_call x5, Pallas kernels, weight_part(): pl.pallas_call(functools.partial(weight_body, begins=[begin for _, begin...  48.4 us
    pallas_call x4, Pallas kernels, input_part(): pl.pallas_call(input_body, out_shape=(shape, shape), grid_spec=pltpu.Pref...  28 us
    ppermute x9, waiting for transfers between devices, onward(): return lax.ppermute(piece, 'tensor', ring)  24 us
    all_to_all x2, waiting for transfers between devices, exchange(): return lax.all_to_all(rows, 'dp', split_axis=0, concat_axis=0, tiled=True)  17.8 us
    convert_element_type x8, other arithmetic, add(): return sum((v.astype(F32) for v in values)).astype(BF16)  17.7 us
    ppermute x14, waiting for transfers between devices, sibling(): return lax.ppermute(piece, 'dp', to_sibling)  12.5 us
    all_to_all x2, starting transfers between devices, exchange(): return lax.all_to_all(rows, 'dp', split_axis=0, concat_axis=0, tiled=True)  9.49 us
  transfers between devices with their start and end apart: 38, of which 16 were waited for; matrix products, arithmetic and copies ran while one was open for 8% of the time, Pallas kernels for 56%

profile of v2, /device:TPU:0, one launch (start us, length us, event | category | flops | bytes accessed | tf_op | source)
XLA Modules:
  0.0 265.4 jit_solution(3213750812071860169)
XLA Ops:
  1.3 3.4 %shard_map.85 = bf16[8,32,3072]{2,1,0:T(8,128)(2,1)} custom-call(s32[2]{0:T(128)} %pad_add_fusion.info, s32[8]{0:T(128)} %count.7, bf16[8,32,3072]{2,1,0:T(8,128)(2,1)} %rows.1), custom_call_target="tpu_custom_call" | custom-call | flops 1 | bytes 1 | tf_op jit(solution)/shard_map/pallas_call | solution.py:67
  4.6 5.2 %all-to-all-start = ((bf16[8,32,3072]{2,1,0:T(8,128)(2,1)}), bf16[8,32,3072]{2,1,0:T(8,128)(2,1)}, u32[]{:S(2)}, u32[]{:S(2)}) async-start(bf16[8,32,3072]{2,1,0:T(8,128)(2,1)} %shard_map.85), calls=%async_computation | async-start | bytes 3145728 | tf_op jit(solution)/shard_map/all_to_all | solution.py:374
  9.8 3.4 %shard_map.86 = bf16[8,32,3072]{2,1,0:T(8,128)(2,1)} custom-call(s32[2]{0:T(128)} %pad_add_fusion.info, s32[8]{0:T(128)} %count.7, bf16[8,32,3072]{2,1,0:T(8,128)(2,1)} %rows.2), custom_call_target="tpu_custom_call" | custom-call | flops 1 | bytes 1 | tf_op jit(solution)/shard_map/pallas_call | solution.py:67
  13.2 17.8 %all-to-all-done.arrived = bf16[8,32,3072]{2,1,0:T(8,128)(2,1)} async-done(((bf16[8,32,3072]{2,1,0:T(8,128)(2,1)}), bf16[8,32,3072]{2,1,0:T(8,128)(2,1)}, u32[]{:S(2)}, u32[]{:S(2)}) %all-to-all-start) | async-done | bytes 1572896 | tf_op jit(solution)/shard_map/all_to_all | solution.py:374
  31.0 3.1 %shard_map.87 = bf16[4,32,3072]{2,1,0:T(8,128)(2,1)} custom-call(s32[2]{0:T(128)} %pad_add_fusion.info, s32[8]{0:T(128)} %count.7, s32[8,8]{1,0:T(8,128)} %patches.3, bf16[8,32,3072]{2,1,0:T(8,128)(2,1)} %all-to-all-done.arrived), custom_call_target="tpu_custom_call" | custom-call | flops 1 | bytes 1 | tf_op jit(solution)/shard_map/pallas_call | solution.py:98
  34.1 2.1 collective-permute-start
  36.2 4.3 %all-to-all-start.1 = ((bf16[8,32,3072]{2,1,0:T(8,128)(2,1)}), bf16[8,32,3072]{2,1,0:T(8,128)(2,1)}, u32[]{:S(2)}, u32[]{:S(2)}) async-start(bf16[8,32,3072]{2,1,0:T(8,128)(2,1)} %shard_map.86), calls=%async_computation.1 | async-start | bytes 3145728 | tf_op jit(solution)/shard_map/all_to_all | solution.py:374
  40.5 8.1 %shard_map.88 = (bf16[256,3072]{1,0:T(8,128)(2,1)}, bf16[256,1536]{1,0:T(8,128)(2,1)}) custom-call(s32[2]{0:T(128)} %pad_add_fusion.info, bf16[128,3072]{1,0:T(8,128)(2,1)} %bitcast.22, bf16[128,3072]{1,0:T(8,128)(2,1)} %collective-permute-done.1.sib.refs_1_, bf16[3072,3072]{1,0:T(8,128)(2,1)} %w.23), custom_call_target="tpu_custom_call" | custom-call | flops 1 | bytes 1 | tf_op jit(solution)/shard_map/pallas_call | solution.py:209
  48.6 8.1 %collective-permute-done.own.refs_5_ = bf16[128,3072]{1,0:T(8,128)(2,1)} collective-permute-done((bf16[128,3072]{1,0:T(8,128)(2,1)}, bf16[128,3072]{1,0:T(8,128)(2,1)}, u32[]{:S(2)}, u32[]{:S(2)}) %collective-permute-start) | collective-permute-done | bytes 786464 | tf_op jit(solution)/shard_map/ppermute | solution.py:365
  57.2 2.1 collective-permute-done.2.sib.refs_6_
  59.3 8.1 %shard_map.89 = (bf16[256,3072]{1,0:T(8,128)(2,1)}, bf16[256,1536]{1,0:T(8,128)(2,1)}) custom-call(s32[2]{0:T(128)} %pad_add_fusion.info, bf16[128,3072]{1,0:T(8,128)(2,1)} %collective-permute-done.own.refs_5_, bf16[128,3072]{1,0:T(8,128)(2,1)} %collective-permute-done.2.sib.refs_6_, bf16[3072,3072]{1,0:T(8,128)(2,1)} %w.23), custom_call_target="tpu_custom_call" | custom-call | flops 1 | bytes 1 | tf_op jit(solution)/shard_map/pallas_call | solution.py:209
  67.9 3.0 %shard_map.90 = bf16[4,32,3072]{2,1,0:T(8,128)(2,1)} custom-call(s32[2]{0:T(128)} %pad_add_fusion.info, s32[8]{0:T(128)} %count.7, s32[8,8]{1,0:T(8,128)} %patches.3, bf16[8,32,3072]{2,1,0:T(8,128)(2,1)} %all-to-all-done.1.arrived), custom_call_target="tpu_custom_call" | custom-call | flops 1 | bytes 1 | tf_op jit(solution)/shard_map/pallas_call | solution.py:98
  71.0 7.8 %collective-permute-done.4.own.refs_10_ = bf16[128,3072]{1,0:T(8,128)(2,1)} collective-permute-done((bf16[128,3072]{1,0:T(8,128)(2,1)}, bf16[128,3072]{1,0:T(8,128)(2,1)}, u32[]{:S(2)}, u32[]{:S(2)}) %collective-permute-start.4) | collective-permute-done | bytes 786464 | tf_op jit(solution)/shard_map/ppermute | solution.py:365
  79.3 2.1 collective-permute-done.5.sib.refs_11_
  81.4 8.1 %shard_map.91 = (bf16[256,3072]{1,0:T(8,128)(2,1)}, bf16[256,1536]{1,0:T(8,128)(2,1)}) custom-call(s32[2]{0:T(128)} %pad_add_fusion.info, bf16[128,3072]{1,0:T(8,128)(2,1)} %collective-permute-done.4.own.refs_10_, bf16[128,3072]{1,0:T(8,128)(2,1)} %collective-permute-done.5.sib.refs_11_, bf16[3072,3072]{1,0:T(8,128)(2,1)} %w.23), custom_call_target="tpu_custom_call" | custom-call | flops 1 | bytes 1 | tf_op jit(solution)/shard_map/pallas_call | solution.py:209
  90.0 4.4 %collective-permute-done.7.refs_9_.refs_7_ = bf16[256,3072]{1,0:T(8,128)(2,1)} collective-permute-done((bf16[256,3072]{1,0:T(8,128)(2,1)}, bf16[256,3072]{1,0:T(8,128)(2,1)}, u32[]{:S(2)}, u32[]{:S(2)}) %collective-permute-start.7) | collective-permute-done | bytes 1572896 | tf_op jit(solution)/shard_map/ppermute | solution.py:371
  94.4 7.7 %shard_map.92.pre.refs_3_ = bf16[256,3072]{1,0:T(8,128)(2,1)} custom-call(s32[2]{0:T(128)} %pad_add_fusion.info, bf16[128,3072]{1,0:T(8,128)(2,1)} %bitcast.15, bf16[128,3072]{1,0:T(8,128)(2,1)} %collective-permute-done.3.sib.refs_1_, bf16[3072,3072]{1,0:T(8,128)(2,1)} %w.22, bf16[256,1536]{1,0:T(8,128)(2,1)} %get-tuple-element.96.slope), custom_call_target="tpu_custom_call" | custom-call | flops 1 | bytes 1 | tf_op jit(solution)/shard_map/pallas_call | solution.py:209
  103.1 1.6 collective-permute-start.12
  105.4 8.1 %shard_map.93 = (bf16[256,3072]{1,0:T(8,128)(2,1)}, bf16[256,1536]{1,0:T(8,128)(2,1)}) custom-call(s32[2]{0:T(128)} %pad_add_fusion.info, bf16[128,3072]{1,0:T(8,128)(2,1)} %collective-permute-done.8.own.refs_15_, bf16[128,3072]{1,0:T(8,128)(2,1)} %collective-permute-done.9.sib.refs_16_, bf16[3072,3072]{1,0:T(8,128)(2,1)} %w.23), custom_call_target="tpu_custom_call" | custom-call | flops 1 | bytes 1 | tf_op jit(solution)/shard_map/pallas_call | solution.py:209
  113.5 7.0 %shard_map.94 = (bf16[128,3072]{1,0:T(8,128)(2,1)}, bf16[128,3072]{1,0:T(8,128)(2,1)}) custom-call(s32[2]{0:T(128)} %pad_add_fusion.info, bf16[256,3072]{1,0:T(8,128)(2,1)} %shard_map.92.pre.refs_3_, bf16[3072,3072]{1,0:T(8,128)(2,1)} %w.23), custom_call_target="tpu_custom_call" | custom-call | flops 1 | bytes 1 | tf_op jit(solution)/shard_map/pallas_call | solution.py:237
  120.4 4.3 %collective-permute-done.12.own.refs_5_ = bf16[128,3072]{1,0:T(8,128)(2,1)} collective-permute-done((bf16[128,3072]{1,0:T(8,128)(2,1)}, bf16[128,3072]{1,0:T(8,128)(2,1)}, u32[]{:S(2)}, u32[]{:S(2)}) %collective-permute-start.12) | collective-permute-done | bytes 786464 | tf_op jit(solution)/shard_map/ppermute | solution.py:365
  125.8 1.6 collective-permute-done.14.sib.refs_6_
  128.5 7.7 %shard_map.95.pre.refs_8_ = bf16[256,3072]{1,0:T(8,128)(2,1)} custom-call(s32[2]{0:T(128)} %pad_add_fusion.info, bf16[128,3072]{1,0:T(8,128)(2,1)} %collective-permute-done.12.own.refs_5_, bf16[128,3072]{1,0:T(8,128)(2,1)} %collective-permute-done.14.sib.refs_6_, bf16[3072,3072]{1,0:T(8,128)(2,1)} %w.22, bf16[256,1536]{1,0:T(8,128)(2,1)} %get-tuple-element.108.slope), custom_call_target="tpu_custom_call" | custom-call | flops 1 | bytes 1 | tf_op jit(solution)/shard_map/pallas_call | solution.py:209
  136.7 7.0 %shard_map.96 = (bf16[128,3072]{1,0:T(8,128)(2,1)}, bf16[128,3072]{1,0:T(8,128)(2,1)}) custom-call(s32[2]{0:T(128)} %pad_add_fusion.info, bf16[256,3072]{1,0:T(8,128)(2,1)} %shard_map.95.pre.refs_8_, bf16[3072,3072]{1,0:T(8,128)(2,1)} %w.23), custom_call_target="tpu_custom_call" | custom-call | flops 1 | bytes 1 | tf_op jit(solution)/shard_map/pallas_call | solution.py:237
  143.7 3.1 %collective-permute-done.13.own.refs_10_ = bf16[128,3072]{1,0:T(8,128)(2,1)} collective-permute-done((bf16[128,3072]{1,0:T(8,128)(2,1)}, bf16[128,3072]{1,0:T(8,128)(2,1)}, u32[]{:S(2)}, u32[]{:S(2)}) %collective-permute-start.13) | collective-permute-done | bytes 786464 | tf_op jit(solution)/shard_map/ppermute | solution.py:365
  147.3 2.1 collective-permute-done.18.sib.refs_11_
  150.6 7.8 %shard_map.97.pre.refs_13_ = bf16[256,3072]{1,0:T(8,128)(2,1)} custom-call(s32[2]{0:T(128)} %pad_add_fusion.info, bf16[128,3072]{1,0:T(8,128)(2,1)} %collective-permute-done.13.own.refs_10_, bf16[128,3072]{1,0:T(8,128)(2,1)} %collective-permute-done.18.sib.refs_11_, bf16[3072,3072]{1,0:T(8,128)(2,1)} %w.22, bf16[256,1536]{1,0:T(8,128)(2,1)} %get-tuple-element.115.slope), custom_call_target="tpu_custom_call" | custom-call | flops 1 | bytes 1 | tf_op jit(solution)/shard_map/pallas_call | solution.py:209
  158.9 7.0 %shard_map.98 = (bf16[128,3072]{1,0:T(8,128)(2,1)}, bf16[128,3072]{1,0:T(8,128)(2,1)}) custom-call(s32[2]{0:T(128)} %pad_add_fusion.info, bf16[256,3072]{1,0:T(8,128)(2,1)} %shard_map.97.pre.refs_13_, bf16[3072,3072]{1,0:T(8,128)(2,1)} %w.23), custom_call_target="tpu_custom_call" | custom-call | flops 1 | bytes 1 | tf_op jit(solution)/shard_map/pallas_call | solution.py:237
  165.9 2.4 add_convert_fusion.7
  169.4 2.1 collective-permute-done.21.sib.refs_16_
  171.5 3.1 %shard_map.99 = bf16[256,1536]{1,0:T(8,128)(2,1)} custom-call(s32[2]{0:T(128)} %pad_add_fusion.info, bf16[128,3072]{1,0:T(8,128)(2,1)} %collective-permute-done.16.own.refs_15_, bf16[128,3072]{1,0:T(8,128)(2,1)} %collective-permute-done.21.sib.refs_16_), custom_call_target="tpu_custom_call" | custom-call | flops 1 | bytes 1 | tf_op jit(solution)/shard_map/pallas_call | solution.py:173
  176.9 7.4 %shard_map.100.pre.refs_18_ = bf16[256,1536]{1,0:T(8,128)(2,1)} custom-call(s32[2]{0:T(128)} %pad_add_fusion.info, bf16[128,3072]{1,0:T(8,128)(2,1)} %collective-permute-done.16.own.refs_15_, bf16[128,3072]{1,0:T(8,128)(2,1)} %collective-permute-done.21.sib.refs_16_, bf16[3072,3072]{1,0:T(8,128)(2,1)} %w.22, bf16[256,1536]{1,0:T(8,128)(2,1)} %get-tuple-element.125.slope), custom_call_target="tpu_custom_call" | custom-call | flops 1 | bytes 1 | tf_op jit(solution)/shard_map/pallas_call | solution.py:209
  185.3 7.0 %shard_map.101 = (bf16[128,3072]{1,0:T(8,128)(2,1)}, bf16[128,3072]{1,0:T(8,128)(2,1)}) custom-call(s32[2]{0:T(128)} %pad_add_fusion.info, bf16[256,1536]{1,0:T(8,128)(2,1)} %shard_map.100.pre.refs_18_, bf16[3072,3072]{1,0:T(8,128)(2,1)} %w.23), custom_call_target="tpu_custom_call" | custom-call | flops 1 | bytes 1 | tf_op jit(solution)/shard_map/pallas_call | solution.py:237
  192.4 7.8 %shard_map.102 = bf16[384,1536]{1,0:T(8,128)(2,1)} custom-call(s32[3]{0:T(128)} %add_add_fusion.3.at, bf16[128,3072]{1,0:T(8,128)(2,1)} %bitcast.17, bf16[128,3072]{1,0:T(8,128)(2,1)} %collective-permute-done.3.sib.refs_1_, bf16[256,3072]{1,0:T(8,128)(2,1)} %collective-permute-done.15.refs_2_.refs_4_, bf16[256,3072]{1,0:T(8,128)(2,1)} %get-tuple-element.84.refs_3_, ...), custom_call_target="tpu_custom_call" | custom-call | flops 1 | bytes 1 | tf_op jit(solution)/shard_map/pallas_call | solution.py:318
  201.1 7.7 %shard_map.103 = bf16[384,1536]{1,0:T(8,128)(2,1)} custom-call(s32[3]{0:T(128)} %add_add_fusion.2.at, bf16[128,3072]{1,0:T(8,128)(2,1)} %bitcast.18, bf16[128,3072]{1,0:T(8,128)(2,1)} %collective-permute-done.3.sib.refs_1_, bf16[256,3072]{1,0:T(8,128)(2,1)} %collective-permute-done.15.refs_2_.refs_4_, bf16[256,3072]{1,0:T(8,128)(2,1)} %get-tuple-element.84.refs_3_, ...), custom_call_target="tpu_custom_call" | custom-call | flops 1 | bytes 1 | tf_op jit(solution)/shard_map/pallas_call | solution.py:318
  208.8 2.9 %add_convert_fusion.6 = bf16[128,3072]{1,0:T(8,128)(2,1)} fusion(bf16[128,3072]{1,0:T(8,128)(2,1)} %collective-permute-done.26, bf16[128,3072]{1,0:T(8,128)(2,1)} %collective-permute-done.22, bf16[128,3072]{1,0:T(8,128)(2,1)} %get-tuple-element.135), kind=kLoop, calls=%fused_computation.8 | loop fusion | flops 2359296 | bytes 3145728 | tf_op jit(solution)/shard_map/convert_element_type | solution.py:340
  213.8 11.0 %shard_map.104 = (bf16[384,1536]{1,0:T(8,128)(2,1)}, bf16[384,1536]{1,0:T(8,128)(2,1)}) custom-call(s32[3]{0:T(128)} %add_add_fusion.1.at, bf16[128,3072]{1,0:T(8,128)(2,1)} %bitcast.23, bf16[128,3072]{1,0:T(8,128)(2,1)} %collective-permute-done.1.sib.refs_1_, bf16[256,3072]{1,0:T(8,128)(2,1)} %collective-permute-done.6.refs_4_.refs_2_, ...), custom_call_target="tpu_custom_call" | custom-call | flops 1 | bytes 1 | tf_op jit(solution)/shard_map/pallas_call | solution.py:318
  224.7 1.2 collective-permute-start.32
  225.9 11.0 %shard_map.105 = (bf16[384,1536]{1,0:T(8,128)(2,1)}, bf16[384,1536]{1,0:T(8,128)(2,1)}) custom-call(s32[3]{0:T(128)} %add_add_fusion.at, bf16[128,3072]{1,0:T(8,128)(2,1)} %bitcast.19, bf16[128,3072]{1,0:T(8,128)(2,1)} %collective-permute-done.3.sib.refs_1_, bf16[256,3072]{1,0:T(8,128)(2,1)} %collective-permute-done.15.refs_2_.refs_4_, ...), custom_call_target="tpu_custom_call" | custom-call | flops 1 | bytes 1 | tf_op jit(solution)/shard_map/pallas_call | solution.py:318
  238.1 2.8 %add_convert_fusion.5 = bf16[128,3072]{1,0:T(8,128)(2,1)} fusion(bf16[128,3072]{1,0:T(8,128)(2,1)} %collective-permute-done.29, bf16[128,3072]{1,0:T(8,128)(2,1)} %collective-permute-done.24, bf16[128,3072]{1,0:T(8,128)(2,1)} %get-tuple-element.143), kind=kLoop, calls=%fused_computation.7 | loop fusion | flops 2359296 | bytes 3145728 | tf_op jit(solution)/shard_map/convert_element_type | solution.py:340
  240.9 11.0 %shard_map.106 = (bf16[384,1536]{1,0:T(8,128)(2,1)}, bf16[384,1536]{1,0:T(8,128)(2,1)}) custom-call(s32[3]{0:T(128)} %add_add_fusion.at, bf16[128,3072]{1,0:T(8,128)(2,1)} %bitcast.24, bf16[128,3072]{1,0:T(8,128)(2,1)} %collective-permute-done.1.sib.refs_1_, bf16[256,3072]{1,0:T(8,128)(2,1)} %collective-permute-done.6.refs_4_.refs_2_, ...), custom_call_target="tpu_custom_call" | custom-call | flops 1 | bytes 1 | tf_op jit(solution)/shard_map/pallas_call | solution.py:318
  252.2 1.9 add_convert_fusion.3
  254.1 1.9 add_convert_fusion.2
  256.0 1.7 maximum_select_fusion
  257.7 1.6 add_convert_fusion.1
  259.3 1.6 add_convert_fusion
  260.8 1.7 maximum_select_fusion.1
  262.8 2.6 add_convert_fusion.4
  (69 shorter events, 18.2 us)
Async XLA Ops:
  4.6 26.3 %all-to-all-start = ((bf16[8,32,3072]{2,1,0:T(8,128)(2,1)}), bf16[8,32,3072]{2,1,0:T(8,128)(2,1)}, u32[]{:S(2)}, u32[]{:S(2)}) async-start(bf16[8,32,3072]{2,1,0:T(8,128)(2,1)} %shard_map.85), calls=%async_computation | async-start | bytes 3145728 | tf_op jit(solution)/shard_map/all_to_all | solution.py:374
  34.0 6.5 %collective-permute-start.1 = (bf16[128,3072]{1,0:T(8,128)(2,1)}, bf16[128,3072]{1,0:T(8,128)(2,1)}, u32[]{:S(2)}, u32[]{:S(2)}) collective-permute-start(bf16[128,3072]{1,0:T(8,128)(2,1)} %bitcast.20), channel_id=1, source_target_pairs={{0,4},{4,0},{8,12},{12,8},{16,20},{20,16},{24,28},{28,24},{1,5},{5... | collective-permute-start | bytes 2359304 | tf_op jit(solution)/shard_map/ppermute | solution.py:368
  34.1 22.6 %collective-permute-start = (bf16[128,3072]{1,0:T(8,128)(2,1)}, bf16[128,3072]{1,0:T(8,128)(2,1)}, u32[]{:S(2)}, u32[]{:S(2)}) collective-permute-start(bf16[128,3072]{1,0:T(8,128)(2,1)} %bitcast.21), channel_id=1, source_target_pairs={{0,1},{1,2},{2,3},{3,0},{4,5},{5,6},{6,7},{7,4},{8,9},{9,10},{10,1... | collective-permute-start | bytes 2359304 | tf_op jit(solution)/shard_map/ppermute | solution.py:365
  36.2 31.7 %all-to-all-start.1 = ((bf16[8,32,3072]{2,1,0:T(8,128)(2,1)}), bf16[8,32,3072]{2,1,0:T(8,128)(2,1)}, u32[]{:S(2)}, u32[]{:S(2)}) async-start(bf16[8,32,3072]{2,1,0:T(8,128)(2,1)} %shard_map.86), calls=%async_computation.1 | async-start | bytes 3145728 | tf_op jit(solution)/shard_map/all_to_all | solution.py:374
  56.7 2.6 collective-permute-start.2
  56.7 22.1 %collective-permute-start.4 = (bf16[128,3072]{1,0:T(8,128)(2,1)}, bf16[128,3072]{1,0:T(8,128)(2,1)}, u32[]{:S(2)}, u32[]{:S(2)}) collective-permute-start(bf16[128,3072]{1,0:T(8,128)(2,1)} %collective-permute-done.own.refs_5_), channel_id=1, source_target_pairs={{0,1},{1,2},{2,3},{3,0},{4,5},{5,6},{6,7},{7,4},{8,9},{9,10},{10,1... | collective-permute-start | bytes 2359304 | tf_op jit(solution)/shard_map/ppermute | solution.py:365
  56.7 22.6 %collective-permute-start.6 = (bf16[256,3072]{1,0:T(8,128)(2,1)}, bf16[256,3072]{1,0:T(8,128)(2,1)}, u32[]{:S(2)}, u32[]{:S(2)}) collective-permute-start(bf16[256,3072]{1,0:T(8,128)(2,1)} %get-tuple-element.84.refs_3_), channel_id=1, source_target_pairs={{0,8},{4,20},{8,0},{12,28},{16,24},{20,4},{24,16},{28,12},{1,9},{5... | collective-permute-start | bytes 4718600 | tf_op jit(solution)/shard_map/ppermute | solution.py:371
  67.4 27.0 %collective-permute-start.7 = (bf16[256,3072]{1,0:T(8,128)(2,1)}, bf16[256,3072]{1,0:T(8,128)(2,1)}, u32[]{:S(2)}, u32[]{:S(2)}) collective-permute-start(bf16[256,3072]{1,0:T(8,128)(2,1)} %get-tuple-element.88.refs_8_), channel_id=1, source_target_pairs={{0,8},{4,20},{8,0},{12,28},{16,24},{20,4},{24,16},{28,12},{1,9},{5... | collective-permute-start | bytes 4718600 | tf_op jit(solution)/shard_map/ppermute | solution.py:371
  78.8 2.6 collective-permute-start.5
  78.8 11.2 %collective-permute-start.3 = (bf16[128,3072]{1,0:T(8,128)(2,1)}, bf16[128,3072]{1,0:T(8,128)(2,1)}, u32[]{:S(2)}, u32[]{:S(2)}) collective-permute-start(bf16[128,3072]{1,0:T(8,128)(2,1)} %bitcast.14), channel_id=1, source_target_pairs={{0,4},{4,0},{8,12},{12,8},{16,20},{20,16},{24,28},{28,24},{1,5},{5... | collective-permute-start | bytes 2359304 | tf_op jit(solution)/shard_map/ppermute | solution.py:368
  79.3 22.8 %collective-permute-start.8 = (bf16[128,3072]{1,0:T(8,128)(2,1)}, bf16[128,3072]{1,0:T(8,128)(2,1)}, u32[]{:S(2)}, u32[]{:S(2)}) collective-permute-start(bf16[128,3072]{1,0:T(8,128)(2,1)} %collective-permute-done.4.own.refs_10_), channel_id=1, source_target_pairs={{0,1},{1,2},{2,3},{3,0},{4,5},{5,6},{6,7},{7,4},{8,9},{9,10},{10,1... | collective-permute-start | bytes 2359304 | tf_op jit(solution)/shard_map/ppermute | solution.py:365
  89.5 24.0 %collective-permute-start.10 = (bf16[256,3072]{1,0:T(8,128)(2,1)}, bf16[256,3072]{1,0:T(8,128)(2,1)}, u32[]{:S(2)}, u32[]{:S(2)}) collective-permute-start(bf16[256,3072]{1,0:T(8,128)(2,1)} %get-tuple-element.93.refs_13_), channel_id=1, source_target_pairs={{0,8},{4,20},{8,0},{12,28},{16,24},{20,4},{24,16},{28,12},{1,9},{5... | collective-permute-start | bytes 4718600 | tf_op jit(solution)/shard_map/ppermute | solution.py:371
  102.1 3.3 %collective-permute-start.9 = (bf16[128,3072]{1,0:T(8,128)(2,1)}, bf16[128,3072]{1,0:T(8,128)(2,1)}, u32[]{:S(2)}, u32[]{:S(2)}) collective-permute-start(bf16[128,3072]{1,0:T(8,128)(2,1)} %collective-permute-done.8.own.refs_15_), channel_id=1, source_target_pairs={{0,4},{4,0},{8,12},{12,8},{16,20},{20,16},{24,28},{28,24},{1,5},{5... | collective-permute-start | bytes 2359304 | tf_op jit(solution)/shard_map/ppermute | solution.py:368
  103.1 21.6 %collective-permute-start.12 = (bf16[128,3072]{1,0:T(8,128)(2,1)}, bf16[128,3072]{1,0:T(8,128)(2,1)}, u32[]{:S(2)}, u32[]{:S(2)}) collective-permute-start(bf16[128,3072]{1,0:T(8,128)(2,1)} %bitcast.16), channel_id=1, source_target_pairs={{0,1},{1,2},{2,3},{3,0},{4,5},{5,6},{6,7},{7,4},{8,9},{9,10},{10,1... | collective-permute-start | bytes 2359304 | tf_op jit(solution)/shard_map/ppermute | solution.py:365
  104.7 32.0 %collective-permute-start.15 = (bf16[256,3072]{1,0:T(8,128)(2,1)}, bf16[256,3072]{1,0:T(8,128)(2,1)}, u32[]{:S(2)}, u32[]{:S(2)}) collective-permute-start(bf16[256,3072]{1,0:T(8,128)(2,1)} %shard_map.92.pre.refs_3_), channel_id=1, source_target_pairs={{0,8},{4,20},{8,0},{12,28},{16,24},{20,4},{24,16},{28,12},{1,9},{5... | collective-permute-start | bytes 4718600 | tf_op jit(solution)/shard_map/ppermute | solution.py:371
  124.7 2.6 collective-permute-start.14
  124.7 3.7 %collective-permute-start.11 = (bf16[128,3072]{1,0:T(8,128)(2,1)}, bf16[128,3072]{1,0:T(8,128)(2,1)}, u32[]{:S(2)}, u32[]{:S(2)}) collective-permute-start(bf16[128,3072]{1,0:T(8,128)(2,1)} %get-tuple-element.103), channel_id=1, source_target_pairs={{0,4},{4,0},{8,12},{12,8},{16,20},{20,16},{24,28},{28,24},{1,5},{5... | collective-permute-start | bytes 2359304 | tf_op jit(solution)/shard_map/ppermute | solution.py:368
  125.2 21.6 %collective-permute-start.13 = (bf16[128,3072]{1,0:T(8,128)(2,1)}, bf16[128,3072]{1,0:T(8,128)(2,1)}, u32[]{:S(2)}, u32[]{:S(2)}) collective-permute-start(bf16[128,3072]{1,0:T(8,128)(2,1)} %collective-permute-done.12.own.refs_5_), channel_id=1, source_target_pairs={{0,1},{1,2},{2,3},{3,0},{4,5},{5,6},{6,7},{7,4},{8,9},{9,10},{10,1... | collective-permute-start | bytes 2359304 | tf_op jit(solution)/shard_map/ppermute | solution.py:365
  125.2 25.3 %collective-permute-start.19 = (bf16[256,3072]{1,0:T(8,128)(2,1)}, bf16[256,3072]{1,0:T(8,128)(2,1)}, u32[]{:S(2)}, u32[]{:S(2)}) collective-permute-start(bf16[256,3072]{1,0:T(8,128)(2,1)} %get-tuple-element.100.refs_18_), channel_id=1, source_target_pairs={{0,8},{4,20},{8,0},{12,28},{16,24},{20,4},{24,16},{28,12},{1,9},{5... | collective-permute-start | bytes 4718600 | tf_op jit(solution)/shard_map/ppermute | solution.py:371
  136.2 29.7 %collective-permute-start.20 = (bf16[256,3072]{1,0:T(8,128)(2,1)}, bf16[256,3072]{1,0:T(8,128)(2,1)}, u32[]{:S(2)}, u32[]{:S(2)}) collective-permute-start(bf16[256,3072]{1,0:T(8,128)(2,1)} %shard_map.95.pre.refs_8_), channel_id=1, source_target_pairs={{0,8},{4,20},{8,0},{12,28},{16,24},{20,4},{24,16},{28,12},{1,9},{5... | collective-permute-start | bytes 4718600 | tf_op jit(solution)/shard_map/ppermute | solution.py:371
  146.8 2.6 collective-permute-start.18
  146.8 3.7 %collective-permute-start.17 = (bf16[128,3072]{1,0:T(8,128)(2,1)}, bf16[128,3072]{1,0:T(8,128)(2,1)}, u32[]{:S(2)}, u32[]{:S(2)}) collective-permute-start(bf16[128,3072]{1,0:T(8,128)(2,1)} %get-tuple-element.110), channel_id=1, source_target_pairs={{0,4},{4,0},{8,12},{12,8},{16,20},{20,16},{24,28},{28,24},{1,5},{5... | collective-permute-start | bytes 2359304 | tf_op jit(solution)/shard_map/ppermute | solution.py:368
  147.3 21.6 %collective-permute-start.16 = (bf16[128,3072]{1,0:T(8,128)(2,1)}, bf16[128,3072]{1,0:T(8,128)(2,1)}, u32[]{:S(2)}, u32[]{:S(2)}) collective-permute-start(bf16[128,3072]{1,0:T(8,128)(2,1)} %collective-permute-done.13.own.refs_10_), channel_id=1, source_target_pairs={{0,1},{1,2},{2,3},{3,0},{4,5},{5,6},{6,7},{7,4},{8,9},{9,10},{10,1... | collective-permute-start | bytes 2359304 | tf_op jit(solution)/shard_map/ppermute | solution.py:365
  158.4 27.0 %collective-permute-start.23 = (bf16[256,3072]{1,0:T(8,128)(2,1)}, bf16[256,3072]{1,0:T(8,128)(2,1)}, u32[]{:S(2)}, u32[]{:S(2)}) collective-permute-start(bf16[256,3072]{1,0:T(8,128)(2,1)} %shard_map.97.pre.refs_13_), channel_id=1, source_target_pairs={{0,8},{4,20},{8,0},{12,28},{16,24},{20,4},{24,16},{28,12},{1,9},{5... | collective-permute-start | bytes 4718600 | tf_op jit(solution)/shard_map/ppermute | solution.py:371
  168.9 2.6 collective-permute-start.21
  168.9 8.0 %collective-permute-start.22 = (bf16[128,3072]{1,0:T(8,128)(2,1)}, bf16[128,3072]{1,0:T(8,128)(2,1)}, u32[]{:S(2)}, u32[]{:S(2)}) collective-permute-start(bf16[128,3072]{1,0:T(8,128)(2,1)} %get-tuple-element.117), channel_id=1, source_target_pairs={{0,4},{4,0},{8,12},{12,8},{16,20},{20,16},{24,28},{28,24},{1,5},{5... | collective-permute-start | bytes 2359304 | tf_op jit(solution)/shard_map/ppermute | solution.py:368
  169.4 22.9 %collective-permute-start.26 = (bf16[128,3072]{1,0:T(8,128)(2,1)}, bf16[128,3072]{1,0:T(8,128)(2,1)}, u32[]{:S(2)}, u32[]{:S(2)}) collective-permute-start(bf16[128,3072]{1,0:T(8,128)(2,1)} %add_convert_fusion.7), channel_id=1, source_target_pairs={{0,1},{1,2},{2,3},{3,0},{4,5},{5,6},{6,7},{7,4},{8,9},{9,10},{10,1... | collective-permute-start | bytes 2359304 | tf_op jit(solution)/shard_map/ppermute | solution.py:365
  174.6 17.8 %collective-permute-start.25 = (bf16[256,1536]{1,0:T(8,128)(2,1)}, bf16[256,1536]{1,0:T(8,128)(2,1)}, u32[]{:S(2)}, u32[]{:S(2)}) collective-permute-start(bf16[256,1536]{1,0:T(8,128)(2,1)} %shard_map.99), channel_id=1, source_target_pairs={{0,8},{4,20},{8,0},{12,28},{16,24},{20,4},{24,16},{28,12},{1,9},{5... | collective-permute-start | bytes 2359304 | tf_op jit(solution)/shard_map/ppermute | solution.py:371
  184.3 29.5 %collective-permute-start.27 = (bf16[256,1536]{1,0:T(8,128)(2,1)}, bf16[256,1536]{1,0:T(8,128)(2,1)}, u32[]{:S(2)}, u32[]{:S(2)}) collective-permute-start(bf16[256,1536]{1,0:T(8,128)(2,1)} %shard_map.100.pre.refs_18_), channel_id=1, source_target_pairs={{0,8},{4,20},{8,0},{12,28},{16,24},{20,4},{24,16},{28,12},{1,9},{5... | collective-permute-start | bytes 2359304 | tf_op jit(solution)/shard_map/ppermute | solution.py:371
  192.3 44.6 %collective-permute-start.24 = (bf16[128,3072]{1,0:T(8,128)(2,1)}, bf16[128,3072]{1,0:T(8,128)(2,1)}, u32[]{:S(2)}, u32[]{:S(2)}) collective-permute-start(bf16[128,3072]{1,0:T(8,128)(2,1)} %get-tuple-element.128), channel_id=1, source_target_pairs={{0,4},{4,0},{8,12},{12,8},{16,20},{20,16},{24,28},{28,24},{1,5},{5... | collective-permute-start | bytes 2359304 | tf_op jit(solution)/shard_map/ppermute | solution.py:368
  200.2 36.9 %collective-permute-start.28 = (bf16[384,1536]{1,0:T(8,128)(2,1)}, bf16[384,1536]{1,0:T(8,128)(2,1)}, u32[]{:S(2)}, u32[]{:S(2)}) collective-permute-start(bf16[384,1536]{1,0:T(8,128)(2,1)} %shard_map.102), channel_id=1, source_target_pairs={{0,16},{4,12},{8,24},{12,4},{16,0},{20,28},{24,8},{28,20},{1,17},{... | collective-permute-start | bytes 3538952 | tf_op jit(solution)/shard_map/ppermute | solution.py:487
  211.7 26.3 %collective-permute-start.29 = (bf16[128,3072]{1,0:T(8,128)(2,1)}, bf16[128,3072]{1,0:T(8,128)(2,1)}, u32[]{:S(2)}, u32[]{:S(2)}) collective-permute-start(bf16[128,3072]{1,0:T(8,128)(2,1)} %add_convert_fusion.6), channel_id=1, source_target_pairs={{0,1},{1,2},{2,3},{3,0},{4,5},{5,6},{6,7},{7,4},{8,9},{9,10},{10,1... | collective-permute-start | bytes 2359304 | tf_op jit(solution)/shard_map/ppermute | solution.py:365
  211.7 29.2 %collective-permute-start.30 = (bf16[384,1536]{1,0:T(8,128)(2,1)}, bf16[384,1536]{1,0:T(8,128)(2,1)}, u32[]{:S(2)}, u32[]{:S(2)}) collective-permute-start(bf16[384,1536]{1,0:T(8,128)(2,1)} %shard_map.103), channel_id=1, source_target_pairs={{0,20},{4,8},{8,28},{12,0},{16,4},{20,24},{24,12},{28,16},{1,21},{... | collective-permute-start | bytes 3538952 | tf_op jit(solution)/shard_map/ppermute | solution.py:487
  224.7 33.0 %collective-permute-start.32 = (bf16[384,1536]{1,0:T(8,128)(2,1)}, bf16[384,1536]{1,0:T(8,128)(2,1)}, u32[]{:S(2)}, u32[]{:S(2)}) collective-permute-start(bf16[384,1536]{1,0:T(8,128)(2,1)} %get-tuple-element.139), channel_id=1, source_target_pairs={{0,16},{4,12},{8,24},{12,4},{16,0},{20,28},{24,8},{28,20},{1,17},{... | collective-permute-start | bytes 3538952 | tf_op jit(solution)/shard_map/ppermute | solution.py:487
  237.0 17.1 %collective-permute-start.31 = (bf16[384,1536]{1,0:T(8,128)(2,1)}, bf16[384,1536]{1,0:T(8,128)(2,1)}, u32[]{:S(2)}, u32[]{:S(2)}) collective-permute-start(bf16[384,1536]{1,0:T(8,128)(2,1)} %get-tuple-element.149), channel_id=1, source_target_pairs={{0,4},{4,0},{8,12},{12,8},{16,20},{20,16},{24,28},{28,24},{1,5},{5... | collective-permute-start | bytes 3538952 | tf_op jit(solution)/shard_map/ppermute | solution.py:368
  237.1 22.2 %collective-permute-start.34 = (bf16[384,1536]{1,0:T(8,128)(2,1)}, bf16[384,1536]{1,0:T(8,128)(2,1)}, u32[]{:S(2)}, u32[]{:S(2)}) collective-permute-start(bf16[384,1536]{1,0:T(8,128)(2,1)} %get-tuple-element.152), channel_id=1, source_target_pairs={{0,20},{4,8},{8,28},{12,0},{16,4},{20,24},{24,12},{28,16},{1,21},{... | collective-permute-start | bytes 3538952 | tf_op jit(solution)/shard_map/ppermute | solution.py:487
  240.9 21.9 %collective-permute-start.35 = (bf16[128,3072]{1,0:T(8,128)(2,1)}, bf16[128,3072]{1,0:T(8,128)(2,1)}, u32[]{:S(2)}, u32[]{:S(2)}) collective-permute-start(bf16[128,3072]{1,0:T(8,128)(2,1)} %add_convert_fusion.5), channel_id=1, source_target_pairs={{0,1},{1,2},{2,3},{3,0},{4,5},{5,6},{6,7},{7,4},{8,9},{9,10},{10,1... | collective-permute-start | bytes 2359304 | tf_op jit(solution)/shard_map/ppermute | solution.py:365
  251.9 7.4 %collective-permute-start.33 = (bf16[384,1536]{1,0:T(8,128)(2,1)}, bf16[384,1536]{1,0:T(8,128)(2,1)S(1)}, u32[]{:S(2)}, u32[]{:S(2)}) collective-permute-start(bf16[384,1536]{1,0:T(8,128)(2,1)} %get-tuple-element.151), channel_id=1, source_target_pairs={{0,4},{4,0},{8,12},{12,8},{16,20},{20,16},{24,28},{28,24},{1,5},{5... | collective-permute-start | bytes 3538952 | tf_op jit(solution)/shard_map/ppermute | solution.py:368
  256.0 1.7 copy-start
  260.8 1.9 copy-start.1

commit v3 on v1

--- a/solution.py
+++ b/solution.py
@@ -278,12 +278,12 @@
     span = width // 2
     is_first = at[2] == 0
 
-    def by_columns(body):
+    def by_columns(body, unroll):
         def step(n, carry):
             body(pl.ds(pl.multiple_of(n * block, 128), block))
             return carry
 
-        lax.fori_loop(0, hidden // block, step, 0)
+        lax.fori_loop(0, hidden // block, step, 0, unroll=unroll)
 
     def first_rows(cut):
         total[:, cut] = lax.dot_general(left[:early], right[:early, cut], dims, preferred_element_type=F32)
@@ -299,10 +299,10 @@
 
     for copy in copies[:5 * middle]:
         copy.wait()
-    by_columns(first_rows)
+    by_columns(first_rows, True)
     for copy in copies[5 * middle:]:
         copy.wait()
-    by_columns(last_rows)
+    by_columns(last_rows, False)
 
 
 def weight_part(rows, there_rows, rights, own_at, there_at, core, width, hidden, split):
@@ -474,18 +474,13 @@
         flip = lambda c: 2 >> c
         return [lax.ppermute(p, "dp", chip_perm(dp, flip, h == 1)) for h, p in enumerate(parts[1])]
 
-    def core_rows(value, which):
-        return lax.dynamic_slice_in_dim(value, which * span, span, 0)
-
-    def finished(kept, parts, sent):
+    def begun(kept, parts, sent):
         if 0 in parts:
             kept = [add(*both) for both in zip(kept, parts[0])]
-        if len(kept) == 2:
-            mine = add(after(kept[0]), sent[0])
-            other = add(sibling(kept[1]), sent[1])
-        else:
-            other = sibling(add(core_rows(kept[0], 1 - core), core_rows(sent[0], 1 - core)))
-            mine = add(core_rows(after(kept[0]), core), core_rows(sent[0], core))
+        return done(add(after(kept[0]), sent[0])), sibling(kept[1])
+
+    def finished(mine, sib, sent):
+        other = add(after(sib), sent[1])
         return done(jnp.where(
             core == 0, jnp.concatenate([mine, other], axis=1), jnp.concatenate([other, mine], axis=1)
         ))
@@ -506,9 +501,10 @@
     running = onward(done(add(*after(*shares[end]), running)))
     last.extend(down_sent)
     up_kept = part(0, *up_sum)
-    down_grad = finished(down_kept, down_parts, down_sent)
+    down_grad = finished(*begun(down_kept, down_parts, down_sent), down_sent)
+    up_begun = begun(up_kept, up_parts, up_sent)
     input_grad = done(add(*after(*shares[0]), running)).reshape(OWNB, here, d)
-    up_grad = finished(up_kept, up_parts, up_sent)
+    up_grad = finished(*up_begun, up_sent)
     return input_grad, up_grad, down_grad
 
 

time: 265 us -> 263 us (level)
  transfers between devices with their start and end apart: 38 -> 38, of which waited for: 16 -> 18; matrix products, arithmetic and copies ran while one was open for 7% -> 7% of each run, Pallas kernels for 55% -> 54%
where the time goes in v3:
time: 263 us; the launch traced here: 262 us
  Pallas kernels  149 us (57%)
  waiting for transfers between devices  63.5 us (24%)
  starting transfers between devices  26.3 us (10%)
  other arithmetic  22.5 us (9%)
    pallas_call x8, Pallas kernels, forward(): pl.pallas_call(functools.partial(body, hidden=hidden, chips=chips), out_s...  63 us
    pallas_call x4, Pallas kernels, weight_part(): pl.pallas_call(functools.partial(weight_body, begins=[begin for _, begin...  42.5 us
    pallas_call x4, Pallas kernels, input_part(): pl.pallas_call(input_body, out_shape=(shape, shape), grid_spec=pltpu.Pref...  27.9 us
    ppermute x9, waiting for transfers between devices, onward(): return lax.ppermute(piece, 'tensor', ring)  26.8 us
    convert_element_type x8, other arithmetic, add(): return sum((v.astype(F32) for v in values)).astype(BF16)  17.8 us
    all_to_all x2, waiting for transfers between devices, exchange(): return lax.all_to_all(rows, 'dp', split_axis=0, concat_axis=0, tiled=True)  17.8 us
    ppermute x14, waiting for transfers between devices, sibling(): return lax.ppermute(piece, 'dp', to_sibling)  12.5 us
    all_to_all x2, starting transfers between devices, exchange(): return lax.all_to_all(rows, 'dp', split_axis=0, concat_axis=0, tiled=True)  9.48 us
  transfers between devices with their start and end apart: 38, of which 18 were waited for; matrix products, arithmetic and copies ran while one was open for 7% of the time, Pallas kernels for 54%

profile of v3, /device:TPU:0, one launch (start us, length us, event | category | flops | bytes accessed | tf_op | source)
XLA Modules:
  0.0 262.4 jit_solution(11579697233251378140)
XLA Ops:
  1.2 3.4 %shard_map.85 = bf16[8,32,3072]{2,1,0:T(8,128)(2,1)} custom-call(s32[2]{0:T(128)} %pad_add_fusion.info, s32[8]{0:T(128)} %count.7, bf16[8,32,3072]{2,1,0:T(8,128)(2,1)} %rows.1), custom_call_target="tpu_custom_call" | custom-call | flops 1 | bytes 1 | tf_op jit(solution)/shard_map/pallas_call | solution.py:67
  4.6 5.2 %all-to-all-start = ((bf16[8,32,3072]{2,1,0:T(8,128)(2,1)}), bf16[8,32,3072]{2,1,0:T(8,128)(2,1)}, u32[]{:S(2)}, u32[]{:S(2)}) async-start(bf16[8,32,3072]{2,1,0:T(8,128)(2,1)} %shard_map.85), calls=%async_computation | async-start | bytes 3145728 | tf_op jit(solution)/shard_map/all_to_all | solution.py:374
  9.8 3.4 %shard_map.86 = bf16[8,32,3072]{2,1,0:T(8,128)(2,1)} custom-call(s32[2]{0:T(128)} %pad_add_fusion.info, s32[8]{0:T(128)} %count.7, bf16[8,32,3072]{2,1,0:T(8,128)(2,1)} %rows.2), custom_call_target="tpu_custom_call" | custom-call | flops 1 | bytes 1 | tf_op jit(solution)/shard_map/pallas_call | solution.py:67
  13.1 17.8 %all-to-all-done.arrived = bf16[8,32,3072]{2,1,0:T(8,128)(2,1)} async-done(((bf16[8,32,3072]{2,1,0:T(8,128)(2,1)}), bf16[8,32,3072]{2,1,0:T(8,128)(2,1)}, u32[]{:S(2)}, u32[]{:S(2)}) %all-to-all-start) | async-done | bytes 1572896 | tf_op jit(solution)/shard_map/all_to_all | solution.py:374
  30.9 3.1 %shard_map.87 = bf16[4,32,3072]{2,1,0:T(8,128)(2,1)} custom-call(s32[2]{0:T(128)} %pad_add_fusion.info, s32[8]{0:T(128)} %count.7, s32[8,8]{1,0:T(8,128)} %patches.3, bf16[8,32,3072]{2,1,0:T(8,128)(2,1)} %all-to-all-done.arrived), custom_call_target="tpu_custom_call" | custom-call | flops 1 | bytes 1 | tf_op jit(solution)/shard_map/pallas_call | solution.py:98
  34.1 2.1 collective-permute-start
  36.2 4.3 %all-to-all-start.1 = ((bf16[8,32,3072]{2,1,0:T(8,128)(2,1)}), bf16[8,32,3072]{2,1,0:T(8,128)(2,1)}, u32[]{:S(2)}, u32[]{:S(2)}) async-start(bf16[8,32,3072]{2,1,0:T(8,128)(2,1)} %shard_map.86), calls=%async_computation.1 | async-start | bytes 3145728 | tf_op jit(solution)/shard_map/all_to_all | solution.py:374
  40.5 8.1 %shard_map.88 = (bf16[256,3072]{1,0:T(8,128)(2,1)}, bf16[256,1536]{1,0:T(8,128)(2,1)}) custom-call(s32[2]{0:T(128)} %pad_add_fusion.info, bf16[128,3072]{1,0:T(8,128)(2,1)} %bitcast.12, bf16[128,3072]{1,0:T(8,128)(2,1)} %collective-permute-done.1.sib.refs_1_, bf16[3072,3072]{1,0:T(8,128)(2,1)} %w.23), custom_call_target="tpu_custom_call" | custom-call | flops 1 | bytes 1 | tf_op jit(solution)/shard_map/pallas_call | solution.py:209
  48.6 8.1 %collective-permute-done.own.refs_5_ = bf16[128,3072]{1,0:T(8,128)(2,1)} collective-permute-done((bf16[128,3072]{1,0:T(8,128)(2,1)}, bf16[128,3072]{1,0:T(8,128)(2,1)}, u32[]{:S(2)}, u32[]{:S(2)}) %collective-permute-start) | collective-permute-done | bytes 786464 | tf_op jit(solution)/shard_map/ppermute | solution.py:365
  57.2 2.1 collective-permute-done.2.sib.refs_6_
  59.3 8.1 %shard_map.89 = (bf16[256,3072]{1,0:T(8,128)(2,1)}, bf16[256,1536]{1,0:T(8,128)(2,1)}) custom-call(s32[2]{0:T(128)} %pad_add_fusion.info, bf16[128,3072]{1,0:T(8,128)(2,1)} %collective-permute-done.own.refs_5_, bf16[128,3072]{1,0:T(8,128)(2,1)} %collective-permute-done.2.sib.refs_6_, bf16[3072,3072]{1,0:T(8,128)(2,1)} %w.23), custom_call_target="tpu_custom_call" | custom-call | flops 1 | bytes 1 | tf_op jit(solution)/shard_map/pallas_call | solution.py:209
  67.9 3.0 %shard_map.90 = bf16[4,32,3072]{2,1,0:T(8,128)(2,1)} custom-call(s32[2]{0:T(128)} %pad_add_fusion.info, s32[8]{0:T(128)} %count.7, s32[8,8]{1,0:T(8,128)} %patches.3, bf16[8,32,3072]{2,1,0:T(8,128)(2,1)} %all-to-all-done.1.arrived), custom_call_target="tpu_custom_call" | custom-call | flops 1 | bytes 1 | tf_op jit(solution)/shard_map/pallas_call | solution.py:98
  70.9 7.8 %collective-permute-done.4.own.refs_10_ = bf16[128,3072]{1,0:T(8,128)(2,1)} collective-permute-done((bf16[128,3072]{1,0:T(8,128)(2,1)}, bf16[128,3072]{1,0:T(8,128)(2,1)}, u32[]{:S(2)}, u32[]{:S(2)}) %collective-permute-start.4) | collective-permute-done | bytes 786464 | tf_op jit(solution)/shard_map/ppermute | solution.py:365
  79.2 2.1 collective-permute-done.5.sib.refs_11_
  81.4 8.1 %shard_map.91 = (bf16[256,3072]{1,0:T(8,128)(2,1)}, bf16[256,1536]{1,0:T(8,128)(2,1)}) custom-call(s32[2]{0:T(128)} %pad_add_fusion.info, bf16[128,3072]{1,0:T(8,128)(2,1)} %collective-permute-done.4.own.refs_10_, bf16[128,3072]{1,0:T(8,128)(2,1)} %collective-permute-done.5.sib.refs_11_, bf16[3072,3072]{1,0:T(8,128)(2,1)} %w.23), custom_call_target="tpu_custom_call" | custom-call | flops 1 | bytes 1 | tf_op jit(solution)/shard_map/pallas_call | solution.py:209
  90.0 4.3 %collective-permute-done.7.refs_9_.refs_7_ = bf16[256,3072]{1,0:T(8,128)(2,1)} collective-permute-done((bf16[256,3072]{1,0:T(8,128)(2,1)}, bf16[256,3072]{1,0:T(8,128)(2,1)}, u32[]{:S(2)}, u32[]{:S(2)}) %collective-permute-start.7) | collective-permute-done | bytes 1572896 | tf_op jit(solution)/shard_map/ppermute | solution.py:371
  94.3 7.7 %shard_map.92.pre.refs_3_ = bf16[256,3072]{1,0:T(8,128)(2,1)} custom-call(s32[2]{0:T(128)} %pad_add_fusion.info, bf16[128,3072]{1,0:T(8,128)(2,1)} %bitcast.16, bf16[128,3072]{1,0:T(8,128)(2,1)} %collective-permute-done.3.sib.refs_1_, bf16[3072,3072]{1,0:T(8,128)(2,1)} %w.22, bf16[256,1536]{1,0:T(8,128)(2,1)} %get-tuple-element.98.slope), custom_call_target="tpu_custom_call" | custom-call | flops 1 | bytes 1 | tf_op jit(solution)/shard_map/pallas_call | solution.py:209
  103.1 1.6 collective-permute-start.12
  105.3 8.0 %shard_map.93 = (bf16[256,3072]{1,0:T(8,128)(2,1)}, bf16[256,1536]{1,0:T(8,128)(2,1)}) custom-call(s32[2]{0:T(128)} %pad_add_fusion.info, bf16[128,3072]{1,0:T(8,128)(2,1)} %collective-permute-done.8.own.refs_15_, bf16[128,3072]{1,0:T(8,128)(2,1)} %collective-permute-done.9.sib.refs_16_, bf16[3072,3072]{1,0:T(8,128)(2,1)} %w.23), custom_call_target="tpu_custom_call" | custom-call | flops 1 | bytes 1 | tf_op jit(solution)/shard_map/pallas_call | solution.py:209
  113.4 7.0 %shard_map.94 = (bf16[128,3072]{1,0:T(8,128)(2,1)}, bf16[128,3072]{1,0:T(8,128)(2,1)}) custom-call(s32[2]{0:T(128)} %pad_add_fusion.info, bf16[256,3072]{1,0:T(8,128)(2,1)} %shard_map.92.pre.refs_3_, bf16[3072,3072]{1,0:T(8,128)(2,1)} %w.23), custom_call_target="tpu_custom_call" | custom-call | flops 1 | bytes 1 | tf_op jit(solution)/shard_map/pallas_call | solution.py:237
  120.3 4.4 %collective-permute-done.12.own.refs_5_ = bf16[128,3072]{1,0:T(8,128)(2,1)} collective-permute-done((bf16[128,3072]{1,0:T(8,128)(2,1)}, bf16[128,3072]{1,0:T(8,128)(2,1)}, u32[]{:S(2)}, u32[]{:S(2)}) %collective-permute-start.12) | collective-permute-done | bytes 786464 | tf_op jit(solution)/shard_map/ppermute | solution.py:365
  125.7 1.6 collective-permute-done.14.sib.refs_6_
  128.4 7.7 %shard_map.95.pre.refs_8_ = bf16[256,3072]{1,0:T(8,128)(2,1)} custom-call(s32[2]{0:T(128)} %pad_add_fusion.info, bf16[128,3072]{1,0:T(8,128)(2,1)} %collective-permute-done.12.own.refs_5_, bf16[128,3072]{1,0:T(8,128)(2,1)} %collective-permute-done.14.sib.refs_6_, bf16[3072,3072]{1,0:T(8,128)(2,1)} %w.22, bf16[256,1536]{1,0:T(8,128)(2,1)} %get-tuple-element.110.slope), custom_call_target="tpu_custom_call" | custom-call | flops 1 | bytes 1 | tf_op jit(solution)/shard_map/pallas_call | solution.py:209
  136.6 7.0 %shard_map.96 = (bf16[128,3072]{1,0:T(8,128)(2,1)}, bf16[128,3072]{1,0:T(8,128)(2,1)}) custom-call(s32[2]{0:T(128)} %pad_add_fusion.info, bf16[256,3072]{1,0:T(8,128)(2,1)} %shard_map.95.pre.refs_8_, bf16[3072,3072]{1,0:T(8,128)(2,1)} %w.23), custom_call_target="tpu_custom_call" | custom-call | flops 1 | bytes 1 | tf_op jit(solution)/shard_map/pallas_call | solution.py:237
  143.6 3.1 %collective-permute-done.13.own.refs_10_ = bf16[128,3072]{1,0:T(8,128)(2,1)} collective-permute-done((bf16[128,3072]{1,0:T(8,128)(2,1)}, bf16[128,3072]{1,0:T(8,128)(2,1)}, u32[]{:S(2)}, u32[]{:S(2)}) %collective-permute-start.13) | collective-permute-done | bytes 786464 | tf_op jit(solution)/shard_map/ppermute | solution.py:365
  147.3 2.1 collective-permute-done.18.sib.refs_11_
  150.5 7.8 %shard_map.97.pre.refs_13_ = bf16[256,3072]{1,0:T(8,128)(2,1)} custom-call(s32[2]{0:T(128)} %pad_add_fusion.info, bf16[128,3072]{1,0:T(8,128)(2,1)} %collective-permute-done.13.own.refs_10_, bf16[128,3072]{1,0:T(8,128)(2,1)} %collective-permute-done.18.sib.refs_11_, bf16[3072,3072]{1,0:T(8,128)(2,1)} %w.22, bf16[256,1536]{1,0:T(8,128)(2,1)} %get-tuple-element.117.slope), custom_call_target="tpu_custom_call" | custom-call | flops 1 | bytes 1 | tf_op jit(solution)/shard_map/pallas_call | solution.py:209
  158.8 7.0 %shard_map.98 = (bf16[128,3072]{1,0:T(8,128)(2,1)}, bf16[128,3072]{1,0:T(8,128)(2,1)}) custom-call(s32[2]{0:T(128)} %pad_add_fusion.info, bf16[256,3072]{1,0:T(8,128)(2,1)} %shard_map.97.pre.refs_13_, bf16[3072,3072]{1,0:T(8,128)(2,1)} %w.23), custom_call_target="tpu_custom_call" | custom-call | flops 1 | bytes 1 | tf_op jit(solution)/shard_map/pallas_call | solution.py:237
  165.8 2.5 add_convert_fusion.7
  169.3 2.1 collective-permute-done.21.sib.refs_16_
  171.5 3.1 %shard_map.99 = bf16[256,1536]{1,0:T(8,128)(2,1)} custom-call(s32[2]{0:T(128)} %pad_add_fusion.info, bf16[128,3072]{1,0:T(8,128)(2,1)} %collective-permute-done.16.own.refs_15_, bf16[128,3072]{1,0:T(8,128)(2,1)} %collective-permute-done.21.sib.refs_16_), custom_call_target="tpu_custom_call" | custom-call | flops 1 | bytes 1 | tf_op jit(solution)/shard_map/pallas_call | solution.py:173
  176.2 7.4 %shard_map.100.pre.refs_18_ = bf16[256,1536]{1,0:T(8,128)(2,1)} custom-call(s32[2]{0:T(128)} %pad_add_fusion.info, bf16[128,3072]{1,0:T(8,128)(2,1)} %collective-permute-done.16.own.refs_15_, bf16[128,3072]{1,0:T(8,128)(2,1)} %collective-permute-done.21.sib.refs_16_, bf16[3072,3072]{1,0:T(8,128)(2,1)} %w.22, bf16[256,1536]{1,0:T(8,128)(2,1)} %get-tuple-element.127.slope), custom_call_target="tpu_custom_call" | custom-call | flops 1 | bytes 1 | tf_op jit(solution)/shard_map/pallas_call | solution.py:209
  184.7 7.0 %shard_map.101 = (bf16[128,3072]{1,0:T(8,128)(2,1)}, bf16[128,3072]{1,0:T(8,128)(2,1)}) custom-call(s32[2]{0:T(128)} %pad_add_fusion.info, bf16[256,1536]{1,0:T(8,128)(2,1)} %shard_map.100.pre.refs_18_, bf16[3072,3072]{1,0:T(8,128)(2,1)} %w.23), custom_call_target="tpu_custom_call" | custom-call | flops 1 | bytes 1 | tf_op jit(solution)/shard_map/pallas_call | solution.py:237
  191.7 10.7 %shard_map.102 = (bf16[384,1536]{1,0:T(8,128)(2,1)}, bf16[384,1536]{1,0:T(8,128)(2,1)}) custom-call(s32[3]{0:T(128)} %get-tuple-element.160.at, bf16[128,3072]{1,0:T(8,128)(2,1)} %bitcast.18, bf16[128,3072]{1,0:T(8,128)(2,1)} %collective-permute-done.3.sib.refs_1_, bf16[256,3072]{1,0:T(8,128)(2,1)} %collective-permute-done.15.refs_2_.refs_4_, ...), custom_call_target="tpu_custom_call" | custom-call | flops 1 | bytes 1 | tf_op jit(solution)/shard_map/pallas_call | solution.py:318
  202.4 2.9 %add_convert_fusion.6 = bf16[128,3072]{1,0:T(8,128)(2,1)} fusion(bf16[128,3072]{1,0:T(8,128)(2,1)} %collective-permute-done.26, bf16[128,3072]{1,0:T(8,128)(2,1)} %collective-permute-done.22, bf16[128,3072]{1,0:T(8,128)(2,1)} %get-tuple-element.136), kind=kLoop, calls=%fused_computation.8 | loop fusion | flops 2359296 | bytes 3145728 | tf_op jit(solution)/shard_map/convert_element_type | solution.py:340
  207.4 10.6 %shard_map.103 = (bf16[384,1536]{1,0:T(8,128)(2,1)}, bf16[384,1536]{1,0:T(8,128)(2,1)}) custom-call(s32[3]{0:T(128)} %get-tuple-element.160.at, bf16[128,3072]{1,0:T(8,128)(2,1)} %bitcast.13, bf16[128,3072]{1,0:T(8,128)(2,1)} %collective-permute-done.1.sib.refs_1_, bf16[256,3072]{1,0:T(8,128)(2,1)} %collective-permute-done.6.refs_4_.refs_2_, ...), custom_call_target="tpu_custom_call" | custom-call | flops 1 | bytes 1 | tf_op jit(solution)/shard_map/pallas_call | solution.py:318
  218.9 10.6 %shard_map.104 = (bf16[384,1536]{1,0:T(8,128)(2,1)}, bf16[384,1536]{1,0:T(8,128)(2,1)}) custom-call(s32[3]{0:T(128)} %get-tuple-element.159.at, bf16[128,3072]{1,0:T(8,128)(2,1)} %bitcast.19, bf16[128,3072]{1,0:T(8,128)(2,1)} %collective-permute-done.3.sib.refs_1_, bf16[256,3072]{1,0:T(8,128)(2,1)} %collective-permute-done.15.refs_2_.refs_4_, ...), custom_call_target="tpu_custom_call" | custom-call | flops 1 | bytes 1 | tf_op jit(solution)/shard_map/pallas_call | solution.py:318
  230.9 2.8 %add_convert_fusion.5 = bf16[128,3072]{1,0:T(8,128)(2,1)} fusion(bf16[128,3072]{1,0:T(8,128)(2,1)} %collective-permute-done.28, bf16[128,3072]{1,0:T(8,128)(2,1)} %collective-permute-done.24, bf16[128,3072]{1,0:T(8,128)(2,1)} %get-tuple-element.144), kind=kLoop, calls=%fused_computation.7 | loop fusion | flops 2359296 | bytes 3145728 | tf_op jit(solution)/shard_map/convert_element_type | solution.py:340
  234.5 10.6 %shard_map.105 = (bf16[384,1536]{1,0:T(8,128)(2,1)}, bf16[384,1536]{1,0:T(8,128)(2,1)}) custom-call(s32[3]{0:T(128)} %get-tuple-element.159.at, bf16[128,3072]{1,0:T(8,128)(2,1)} %bitcast.14, bf16[128,3072]{1,0:T(8,128)(2,1)} %collective-permute-done.1.sib.refs_1_, bf16[256,3072]{1,0:T(8,128)(2,1)} %collective-permute-done.6.refs_4_.refs_2_, ...), custom_call_target="tpu_custom_call" | custom-call | flops 1 | bytes 1 | tf_op jit(solution)/shard_map/pallas_call | solution.py:318
  245.2 1.9 add_convert_fusion.3
  247.1 1.9 add_convert_fusion.2
  249.0 1.7 maximum_select_fusion
  250.7 1.6 add_convert_fusion.1
  252.3 2.9 %collective-permute-done.33 = bf16[128,3072]{1,0:T(8,128)(2,1)} collective-permute-done((bf16[128,3072]{1,0:T(8,128)(2,1)}, bf16[128,3072]{1,0:T(8,128)(2,1)}, u32[]{:S(2)}, u32[]{:S(2)}) %collective-permute-start.33) | collective-permute-done | bytes 786464 | tf_op jit(solution)/shard_map/ppermute | solution.py:365
  255.2 2.6 add_convert_fusion.4
  257.8 1.3 collective-permute-done.35
  259.1 1.6 add_convert_fusion
  260.7 1.7 maximum_select_fusion.1
  (65 shorter events, 18.2 us)
Async XLA Ops:
  4.6 26.3 %all-to-all-start = ((bf16[8,32,3072]{2,1,0:T(8,128)(2,1)}), bf16[8,32,3072]{2,1,0:T(8,128)(2,1)}, u32[]{:S(2)}, u32[]{:S(2)}) async-start(bf16[8,32,3072]{2,1,0:T(8,128)(2,1)} %shard_map.85), calls=%async_computation | async-start | bytes 3145728 | tf_op jit(solution)/shard_map/all_to_all | solution.py:374
  34.0 6.5 %collective-permute-start.1 = (bf16[128,3072]{1,0:T(8,128)(2,1)}, bf16[128,3072]{1,0:T(8,128)(2,1)}, u32[]{:S(2)}, u32[]{:S(2)}) collective-permute-start(bf16[128,3072]{1,0:T(8,128)(2,1)} %bitcast.10), channel_id=1, source_target_pairs={{0,4},{4,0},{8,12},{12,8},{16,20},{20,16},{24,28},{28,24},{1,5},{5... | collective-permute-start | bytes 2359304 | tf_op jit(solution)/shard_map/ppermute | solution.py:368
  34.1 22.6 %collective-permute-start = (bf16[128,3072]{1,0:T(8,128)(2,1)}, bf16[128,3072]{1,0:T(8,128)(2,1)}, u32[]{:S(2)}, u32[]{:S(2)}) collective-permute-start(bf16[128,3072]{1,0:T(8,128)(2,1)} %bitcast.11), channel_id=1, source_target_pairs={{0,1},{1,2},{2,3},{3,0},{4,5},{5,6},{6,7},{7,4},{8,9},{9,10},{10,1... | collective-permute-start | bytes 2359304 | tf_op jit(solution)/shard_map/ppermute | solution.py:365
  36.2 31.7 %all-to-all-start.1 = ((bf16[8,32,3072]{2,1,0:T(8,128)(2,1)}), bf16[8,32,3072]{2,1,0:T(8,128)(2,1)}, u32[]{:S(2)}, u32[]{:S(2)}) async-start(bf16[8,32,3072]{2,1,0:T(8,128)(2,1)} %shard_map.86), calls=%async_computation.1 | async-start | bytes 3145728 | tf_op jit(solution)/shard_map/all_to_all | solution.py:374
  56.7 2.6 %collective-permute-start.2 = (bf16[128,3072]{1,0:T(8,128)(2,1)}, bf16[128,3072]{1,0:T(8,128)(2,1)}, u32[]{:S(2)}, u32[]{:S(2)}) collective-permute-start(bf16[128,3072]{1,0:T(8,128)(2,1)} %collective-permute-done.own.refs_5_), channel_id=1, source_target_pairs={{0,4},{4,0},{8,12},{12,8},{16,20},{20,16},{24,28},{28,24},{1,5},{5... | collective-permute-start | bytes 2359304 | tf_op jit(solution)/shard_map/ppermute | solution.py:368
  56.7 22.1 %collective-permute-start.4 = (bf16[128,3072]{1,0:T(8,128)(2,1)}, bf16[128,3072]{1,0:T(8,128)(2,1)}, u32[]{:S(2)}, u32[]{:S(2)}) collective-permute-start(bf16[128,3072]{1,0:T(8,128)(2,1)} %collective-permute-done.own.refs_5_), channel_id=1, source_target_pairs={{0,1},{1,2},{2,3},{3,0},{4,5},{5,6},{6,7},{7,4},{8,9},{9,10},{10,1... | collective-permute-start | bytes 2359304 | tf_op jit(solution)/shard_map/ppermute | solution.py:365
  56.7 22.6 %collective-permute-start.6 = (bf16[256,3072]{1,0:T(8,128)(2,1)}, bf16[256,3072]{1,0:T(8,128)(2,1)}, u32[]{:S(2)}, u32[]{:S(2)}) collective-permute-start(bf16[256,3072]{1,0:T(8,128)(2,1)} %get-tuple-element.86.refs_3_), channel_id=1, source_target_pairs={{0,8},{4,20},{8,0},{12,28},{16,24},{20,4},{24,16},{28,12},{1,9},{5... | collective-permute-start | bytes 4718600 | tf_op jit(solution)/shard_map/ppermute | solution.py:371
  67.4 26.9 %collective-permute-start.7 = (bf16[256,3072]{1,0:T(8,128)(2,1)}, bf16[256,3072]{1,0:T(8,128)(2,1)}, u32[]{:S(2)}, u32[]{:S(2)}) collective-permute-start(bf16[256,3072]{1,0:T(8,128)(2,1)} %get-tuple-element.90.refs_8_), channel_id=1, source_target_pairs={{0,8},{4,20},{8,0},{12,28},{16,24},{20,4},{24,16},{28,12},{1,9},{5... | collective-permute-start | bytes 4718600 | tf_op jit(solution)/shard_map/ppermute | solution.py:371
  78.7 2.6 %collective-permute-start.5 = (bf16[128,3072]{1,0:T(8,128)(2,1)}, bf16[128,3072]{1,0:T(8,128)(2,1)}, u32[]{:S(2)}, u32[]{:S(2)}) collective-permute-start(bf16[128,3072]{1,0:T(8,128)(2,1)} %collective-permute-done.4.own.refs_10_), channel_id=1, source_target_pairs={{0,4},{4,0},{8,12},{12,8},{16,20},{20,16},{24,28},{28,24},{1,5},{5... | collective-permute-start | bytes 2359304 | tf_op jit(solution)/shard_map/ppermute | solution.py:368
  78.7 11.2 %collective-permute-start.3 = (bf16[128,3072]{1,0:T(8,128)(2,1)}, bf16[128,3072]{1,0:T(8,128)(2,1)}, u32[]{:S(2)}, u32[]{:S(2)}) collective-permute-start(bf16[128,3072]{1,0:T(8,128)(2,1)} %bitcast.15), channel_id=1, source_target_pairs={{0,4},{4,0},{8,12},{12,8},{16,20},{20,16},{24,28},{28,24},{1,5},{5... | collective-permute-start | bytes 2359304 | tf_op jit(solution)/shard_map/ppermute | solution.py:368
  79.2 22.8 %collective-permute-start.8 = (bf16[128,3072]{1,0:T(8,128)(2,1)}, bf16[128,3072]{1,0:T(8,128)(2,1)}, u32[]{:S(2)}, u32[]{:S(2)}) collective-permute-start(bf16[128,3072]{1,0:T(8,128)(2,1)} %collective-permute-done.4.own.refs_10_), channel_id=1, source_target_pairs={{0,1},{1,2},{2,3},{3,0},{4,5},{5,6},{6,7},{7,4},{8,9},{9,10},{10,1... | collective-permute-start | bytes 2359304 | tf_op jit(solution)/shard_map/ppermute | solution.py:365
  89.5 23.9 %collective-permute-start.10 = (bf16[256,3072]{1,0:T(8,128)(2,1)}, bf16[256,3072]{1,0:T(8,128)(2,1)}, u32[]{:S(2)}, u32[]{:S(2)}) collective-permute-start(bf16[256,3072]{1,0:T(8,128)(2,1)} %get-tuple-element.95.refs_13_), channel_id=1, source_target_pairs={{0,8},{4,20},{8,0},{12,28},{16,24},{20,4},{24,16},{28,12},{1,9},{5... | collective-permute-start | bytes 4718600 | tf_op jit(solution)/shard_map/ppermute | solution.py:371
  102.0 3.3 %collective-permute-start.9 = (bf16[128,3072]{1,0:T(8,128)(2,1)}, bf16[128,3072]{1,0:T(8,128)(2,1)}, u32[]{:S(2)}, u32[]{:S(2)}) collective-permute-start(bf16[128,3072]{1,0:T(8,128)(2,1)} %collective-permute-done.8.own.refs_15_), channel_id=1, source_target_pairs={{0,4},{4,0},{8,12},{12,8},{16,20},{20,16},{24,28},{28,24},{1,5},{5... | collective-permute-start | bytes 2359304 | tf_op jit(solution)/shard_map/ppermute | solution.py:368
  103.1 21.6 %collective-permute-start.12 = (bf16[128,3072]{1,0:T(8,128)(2,1)}, bf16[128,3072]{1,0:T(8,128)(2,1)}, u32[]{:S(2)}, u32[]{:S(2)}) collective-permute-start(bf16[128,3072]{1,0:T(8,128)(2,1)} %bitcast.17), channel_id=1, source_target_pairs={{0,1},{1,2},{2,3},{3,0},{4,5},{5,6},{6,7},{7,4},{8,9},{9,10},{10,1... | collective-permute-start | bytes 2359304 | tf_op jit(solution)/shard_map/ppermute | solution.py:365
  104.6 32.0 %collective-permute-start.15 = (bf16[256,3072]{1,0:T(8,128)(2,1)}, bf16[256,3072]{1,0:T(8,128)(2,1)}, u32[]{:S(2)}, u32[]{:S(2)}) collective-permute-start(bf16[256,3072]{1,0:T(8,128)(2,1)} %shard_map.92.pre.refs_3_), channel_id=1, source_target_pairs={{0,8},{4,20},{8,0},{12,28},{16,24},{20,4},{24,16},{28,12},{1,9},{5... | collective-permute-start | bytes 4718600 | tf_op jit(solution)/shard_map/ppermute | solution.py:371
  124.7 2.6 %collective-permute-start.14 = (bf16[128,3072]{1,0:T(8,128)(2,1)}, bf16[128,3072]{1,0:T(8,128)(2,1)}, u32[]{:S(2)}, u32[]{:S(2)}) collective-permute-start(bf16[128,3072]{1,0:T(8,128)(2,1)} %collective-permute-done.12.own.refs_5_), channel_id=1, source_target_pairs={{0,4},{4,0},{8,12},{12,8},{16,20},{20,16},{24,28},{28,24},{1,5},{5... | collective-permute-start | bytes 2359304 | tf_op jit(solution)/shard_map/ppermute | solution.py:368
  124.7 3.7 %collective-permute-start.11 = (bf16[128,3072]{1,0:T(8,128)(2,1)}, bf16[128,3072]{1,0:T(8,128)(2,1)}, u32[]{:S(2)}, u32[]{:S(2)}) collective-permute-start(bf16[128,3072]{1,0:T(8,128)(2,1)} %get-tuple-element.105), channel_id=1, source_target_pairs={{0,4},{4,0},{8,12},{12,8},{16,20},{20,16},{24,28},{28,24},{1,5},{5... | collective-permute-start | bytes 2359304 | tf_op jit(solution)/shard_map/ppermute | solution.py:368
  125.2 21.6 %collective-permute-start.13 = (bf16[128,3072]{1,0:T(8,128)(2,1)}, bf16[128,3072]{1,0:T(8,128)(2,1)}, u32[]{:S(2)}, u32[]{:S(2)}) collective-permute-start(bf16[128,3072]{1,0:T(8,128)(2,1)} %collective-permute-done.12.own.refs_5_), channel_id=1, source_target_pairs={{0,1},{1,2},{2,3},{3,0},{4,5},{5,6},{6,7},{7,4},{8,9},{9,10},{10,1... | collective-permute-start | bytes 2359304 | tf_op jit(solution)/shard_map/ppermute | solution.py:365
  125.2 25.3 %collective-permute-start.19 = (bf16[256,3072]{1,0:T(8,128)(2,1)}, bf16[256,3072]{1,0:T(8,128)(2,1)}, u32[]{:S(2)}, u32[]{:S(2)}) collective-permute-start(bf16[256,3072]{1,0:T(8,128)(2,1)} %get-tuple-element.102.refs_18_), channel_id=1, source_target_pairs={{0,8},{4,20},{8,0},{12,28},{16,24},{20,4},{24,16},{28,12},{1,9},{5... | collective-permute-start | bytes 4718600 | tf_op jit(solution)/shard_map/ppermute | solution.py:371
  136.1 29.7 %collective-permute-start.20 = (bf16[256,3072]{1,0:T(8,128)(2,1)}, bf16[256,3072]{1,0:T(8,128)(2,1)}, u32[]{:S(2)}, u32[]{:S(2)}) collective-permute-start(bf16[256,3072]{1,0:T(8,128)(2,1)} %shard_map.95.pre.refs_8_), channel_id=1, source_target_pairs={{0,8},{4,20},{8,0},{12,28},{16,24},{20,4},{24,16},{28,12},{1,9},{5... | collective-permute-start | bytes 4718600 | tf_op jit(solution)/shard_map/ppermute | solution.py:371
  146.8 2.6 %collective-permute-start.18 = (bf16[128,3072]{1,0:T(8,128)(2,1)}, bf16[128,3072]{1,0:T(8,128)(2,1)}, u32[]{:S(2)}, u32[]{:S(2)}) collective-permute-start(bf16[128,3072]{1,0:T(8,128)(2,1)} %collective-permute-done.13.own.refs_10_), channel_id=1, source_target_pairs={{0,4},{4,0},{8,12},{12,8},{16,20},{20,16},{24,28},{28,24},{1,5},{5... | collective-permute-start | bytes 2359304 | tf_op jit(solution)/shard_map/ppermute | solution.py:368
  146.8 3.7 %collective-permute-start.17 = (bf16[128,3072]{1,0:T(8,128)(2,1)}, bf16[128,3072]{1,0:T(8,128)(2,1)}, u32[]{:S(2)}, u32[]{:S(2)}) collective-permute-start(bf16[128,3072]{1,0:T(8,128)(2,1)} %get-tuple-element.112), channel_id=1, source_target_pairs={{0,4},{4,0},{8,12},{12,8},{16,20},{20,16},{24,28},{28,24},{1,5},{5... | collective-permute-start | bytes 2359304 | tf_op jit(solution)/shard_map/ppermute | solution.py:368
  147.3 21.6 %collective-permute-start.16 = (bf16[128,3072]{1,0:T(8,128)(2,1)}, bf16[128,3072]{1,0:T(8,128)(2,1)}, u32[]{:S(2)}, u32[]{:S(2)}) collective-permute-start(bf16[128,3072]{1,0:T(8,128)(2,1)} %collective-permute-done.13.own.refs_10_), channel_id=1, source_target_pairs={{0,1},{1,2},{2,3},{3,0},{4,5},{5,6},{6,7},{7,4},{8,9},{9,10},{10,1... | collective-permute-start | bytes 2359304 | tf_op jit(solution)/shard_map/ppermute | solution.py:365
  158.3 26.4 %collective-permute-start.23 = (bf16[256,3072]{1,0:T(8,128)(2,1)}, bf16[256,3072]{1,0:T(8,128)(2,1)}, u32[]{:S(2)}, u32[]{:S(2)}) collective-permute-start(bf16[256,3072]{1,0:T(8,128)(2,1)} %shard_map.97.pre.refs_13_), channel_id=1, source_target_pairs={{0,8},{4,20},{8,0},{12,28},{16,24},{20,4},{24,16},{28,12},{1,9},{5... | collective-permute-start | bytes 4718600 | tf_op jit(solution)/shard_map/ppermute | solution.py:371
  168.8 2.6 %collective-permute-start.21 = (bf16[128,3072]{1,0:T(8,128)(2,1)}, bf16[128,3072]{1,0:T(8,128)(2,1)}, u32[]{:S(2)}, u32[]{:S(2)}) collective-permute-start(bf16[128,3072]{1,0:T(8,128)(2,1)} %collective-permute-done.16.own.refs_15_), channel_id=1, source_target_pairs={{0,4},{4,0},{8,12},{12,8},{16,20},{20,16},{24,28},{28,24},{1,5},{5... | collective-permute-start | bytes 2359304 | tf_op jit(solution)/shard_map/ppermute | solution.py:368
  168.8 7.4 %collective-permute-start.22 = (bf16[128,3072]{1,0:T(8,128)(2,1)}, bf16[128,3072]{1,0:T(8,128)(2,1)}, u32[]{:S(2)}, u32[]{:S(2)}) collective-permute-start(bf16[128,3072]{1,0:T(8,128)(2,1)} %get-tuple-element.119), channel_id=1, source_target_pairs={{0,4},{4,0},{8,12},{12,8},{16,20},{20,16},{24,28},{28,24},{1,5},{5... | collective-permute-start | bytes 2359304 | tf_op jit(solution)/shard_map/ppermute | solution.py:368
  169.3 22.3 %collective-permute-start.26 = (bf16[128,3072]{1,0:T(8,128)(2,1)}, bf16[128,3072]{1,0:T(8,128)(2,1)}, u32[]{:S(2)}, u32[]{:S(2)}) collective-permute-start(bf16[128,3072]{1,0:T(8,128)(2,1)} %add_convert_fusion.7), channel_id=1, source_target_pairs={{0,1},{1,2},{2,3},{3,0},{4,5},{5,6},{6,7},{7,4},{8,9},{9,10},{10,1... | collective-permute-start | bytes 2359304 | tf_op jit(solution)/shard_map/ppermute | solution.py:365
  174.5 17.1 %collective-permute-start.25 = (bf16[256,1536]{1,0:T(8,128)(2,1)}, bf16[256,1536]{1,0:T(8,128)(2,1)}, u32[]{:S(2)}, u32[]{:S(2)}) collective-permute-start(bf16[256,1536]{1,0:T(8,128)(2,1)} %shard_map.99), channel_id=1, source_target_pairs={{0,8},{4,20},{8,0},{12,28},{16,24},{20,4},{24,16},{28,12},{1,9},{5... | collective-permute-start | bytes 2359304 | tf_op jit(solution)/shard_map/ppermute | solution.py:371
  183.6 23.7 %collective-permute-start.27 = (bf16[256,1536]{1,0:T(8,128)(2,1)}, bf16[256,1536]{1,0:T(8,128)(2,1)}, u32[]{:S(2)}, u32[]{:S(2)}) collective-permute-start(bf16[256,1536]{1,0:T(8,128)(2,1)} %shard_map.100.pre.refs_18_), channel_id=1, source_target_pairs={{0,8},{4,20},{8,0},{12,28},{16,24},{20,4},{24,16},{28,12},{1,9},{5... | collective-permute-start | bytes 2359304 | tf_op jit(solution)/shard_map/ppermute | solution.py:371
  191.6 37.9 %collective-permute-start.24 = (bf16[128,3072]{1,0:T(8,128)(2,1)}, bf16[128,3072]{1,0:T(8,128)(2,1)}, u32[]{:S(2)}, u32[]{:S(2)}) collective-permute-start(bf16[128,3072]{1,0:T(8,128)(2,1)} %get-tuple-element.130), channel_id=1, source_target_pairs={{0,4},{4,0},{8,12},{12,8},{16,20},{20,16},{24,28},{28,24},{1,5},{5... | collective-permute-start | bytes 2359304 | tf_op jit(solution)/shard_map/ppermute | solution.py:368
  205.3 24.4 %collective-permute-start.28 = (bf16[128,3072]{1,0:T(8,128)(2,1)}, bf16[128,3072]{1,0:T(8,128)(2,1)}, u32[]{:S(2)}, u32[]{:S(2)}) collective-permute-start(bf16[128,3072]{1,0:T(8,128)(2,1)} %add_convert_fusion.6), channel_id=1, source_target_pairs={{0,1},{1,2},{2,3},{3,0},{4,5},{5,6},{6,7},{7,4},{8,9},{9,10},{10,1... | collective-permute-start | bytes 2359304 | tf_op jit(solution)/shard_map/ppermute | solution.py:365
  205.3 28.4 %collective-permute-start.30 = (bf16[384,1536]{1,0:T(8,128)(2,1)}, bf16[384,1536]{1,0:T(8,128)(2,1)}, u32[]{:S(2)}, u32[]{:S(2)}) collective-permute-start(bf16[384,1536]{1,0:T(8,128)(2,1)} %get-tuple-element.146), channel_id=1, source_target_pairs={{0,20},{4,8},{8,28},{12,0},{16,4},{20,24},{24,12},{28,16},{1,21},{... | collective-permute-start | bytes 3538952 | tf_op jit(solution)/shard_map/ppermute | solution.py:475
  206.2 28.2 %collective-permute-start.29 = (bf16[384,1536]{1,0:T(8,128)(2,1)}, bf16[384,1536]{1,0:T(8,128)(2,1)}, u32[]{:S(2)}, u32[]{:S(2)}) collective-permute-start(bf16[384,1536]{1,0:T(8,128)(2,1)} %get-tuple-element.135), channel_id=1, source_target_pairs={{0,16},{4,12},{8,24},{12,4},{16,0},{20,28},{24,8},{28,20},{1,17},{... | collective-permute-start | bytes 3538952 | tf_op jit(solution)/shard_map/ppermute | solution.py:475
  218.0 32.7 %collective-permute-start.32 = (bf16[384,1536]{1,0:T(8,128)(2,1)}, bf16[384,1536]{1,0:T(8,128)(2,1)}, u32[]{:S(2)}, u32[]{:S(2)}) collective-permute-start(bf16[384,1536]{1,0:T(8,128)(2,1)} %get-tuple-element.140), channel_id=1, source_target_pairs={{0,16},{4,12},{8,24},{12,4},{16,0},{20,28},{24,8},{28,20},{1,17},{... | collective-permute-start | bytes 3538952 | tf_op jit(solution)/shard_map/ppermute | solution.py:475
  229.6 17.5 %collective-permute-start.31 = (bf16[384,1536]{1,0:T(8,128)(2,1)}, bf16[384,1536]{1,0:T(8,128)(2,1)}, u32[]{:S(2)}, u32[]{:S(2)}) collective-permute-start(bf16[384,1536]{1,0:T(8,128)(2,1)} %get-tuple-element.151), channel_id=1, source_target_pairs={{0,4},{4,0},{8,12},{12,8},{16,20},{20,16},{24,28},{28,24},{1,5},{5... | collective-permute-start | bytes 3538952 | tf_op jit(solution)/shard_map/ppermute | solution.py:368
  229.6 29.5 %collective-permute-start.35 = (bf16[384,1536]{1,0:T(8,128)(2,1)}, bf16[384,1536]{1,0:T(8,128)(2,1)}, u32[]{:S(2)}, u32[]{:S(2)}) collective-permute-start(bf16[384,1536]{1,0:T(8,128)(2,1)} %get-tuple-element.158), channel_id=1, source_target_pairs={{0,20},{4,8},{8,28},{12,0},{16,4},{20,24},{24,12},{28,16},{1,21},{... | collective-permute-start | bytes 3538952 | tf_op jit(solution)/shard_map/ppermute | solution.py:475
  233.7 21.5 %collective-permute-start.33 = (bf16[128,3072]{1,0:T(8,128)(2,1)}, bf16[128,3072]{1,0:T(8,128)(2,1)}, u32[]{:S(2)}, u32[]{:S(2)}) collective-permute-start(bf16[128,3072]{1,0:T(8,128)(2,1)} %add_convert_fusion.5), channel_id=1, source_target_pairs={{0,1},{1,2},{2,3},{3,0},{4,5},{5,6},{6,7},{7,4},{8,9},{9,10},{10,1... | collective-permute-start | bytes 2359304 | tf_op jit(solution)/shard_map/ppermute | solution.py:365
  245.1 12.7 %collective-permute-start.34 = (bf16[384,1536]{1,0:T(8,128)(2,1)}, bf16[384,1536]{1,0:T(8,128)(2,1)S(1)}, u32[]{:S(2)}, u32[]{:S(2)}) collective-permute-start(bf16[384,1536]{1,0:T(8,128)(2,1)} %get-tuple-element.156), channel_id=1, source_target_pairs={{0,4},{4,0},{8,12},{12,8},{16,20},{20,16},{24,28},{28,24},{1,5},{5... | collective-permute-start | bytes 3538952 | tf_op jit(solution)/shard_map/ppermute | solution.py:368
  249.0 1.7 copy-start
  250.7 4.5 %copy-start.1 = (bf16[128,3072]{1,0:T(8,128)(2,1)S(1)}, bf16[128,3072]{1,0:T(8,128)(2,1)}, u32[]{:S(2)}) copy-start(bf16[128,3072]{1,0:T(8,128)(2,1)} %get-tuple-element.154) | copy-start | bytes 2359300
